TPU v7x, 1024 devices: a whole 4x4x32 slice. The times are simulated.
1024 devices in a mesh: group: 16 (over z_lo), local: 64 (over x, z_hi, y, core).
Axes of the slice: x: 4, y: 4, z: 32 (z_hi: 2, z_lo: 16; z = z_hi * 16 + z_lo), core: 2. Of those that a mesh axis runs over, the one named last changes fastest.
Arguments:
- inputs: bfloat16 [131072, 2048], P(('group', 'local')), may hold values from -24 to 24
- out_grad: bfloat16 [131072, 2048], P(('group', 'local')), may hold values from -24 to 24
- routes: int32 [131072, 2], P(('group', 'local')), may hold values from 0 to 127, as said below
- router_weight: bfloat16 [2048, 128], replicated, may hold values from -0.25 to 0.25
- w_in: bfloat16 [2048, 32768], P(None, 'local'), may hold values from -0.125 to 0.125
- w_out: bfloat16 [32768, 2048], P('local'), may hold values from -0.0625 to 0.0625
Outputs:
- in_grad: bfloat16 [131072, 2048], P(('group', 'local'))
- w_in_grad: bfloat16 [2048, 32768], P('group', 'local')
- w_out_grad: bfloat16 [32768, 2048], P('local', 'group')
Inputs may be any that keep to these rules, and one draw needn't show every extreme that they name: `routes`: the two experts of a token differ. Among the 128 tokens of one device at most 4 name any one expert below 4.
All inputs are finite; a program needn't handle non-finite values.
Results may differ from a plain program's by a relative error of at most 0.023.
Values may be sent and summed in bfloat16 or wider, within the bound.
No kernel may reach another device: no remote copies, remote signals or barrier semaphores. Data moves between devices by JAX's collectives and lax.ppermute only.
A program may use at most 32 MiB of HBM per device.

v0:
```python
import jax
import jax.numpy as jnp
from jax import lax
from jax.sharding import PartitionSpec as P

FF = 8192
TOPK = 2
CAP = 4


gelu_c = 0.7978845608
gelu_a = 0.044715


def gelu_pair(pre_act):
    inner = gelu_c * (pre_act + gelu_a * pre_act * pre_act * pre_act)
    tval = jnp.tanh(inner)
    value = 0.5 * pre_act * (1.0 + tval)
    slope = 0.5 * (1.0 + tval) + 0.5 * pre_act * (1.0 - tval * tval) * gelu_c * (
        1.0 + 3.0 * gelu_a * pre_act * pre_act
    )
    return (value, slope)


def expert_rows(x_rows, g_rows, w_first, w_second):
    pre_act = jnp.dot(x_rows, w_first, preferred_element_type=jnp.float32)
    value, slope = gelu_pair(pre_act)
    hidden = value.astype(jnp.bfloat16)
    back_hid = jnp.einsum("rd,fd->rf", g_rows, w_second, preferred_element_type=jnp.float32)
    hid_grad = (back_hid * slope).astype(jnp.bfloat16)
    partial_value = jnp.einsum(
        "rf,df->rd", hid_grad, w_first, preferred_element_type=jnp.float32
    ).astype(jnp.bfloat16)
    return (hidden, hid_grad, partial_value)


def shards(inputs, out_grad, routes, router_weight, w_in, w_out):
    tok_rows = inputs.shape[0]
    d_model = inputs.shape[1]
    n_experts = router_weight.shape[1]
    n_local = lax.axis_size("local")
    ff_dev = w_in.shape[1]
    split_count = FF // ff_dev
    window = n_local // split_count
    logits = jnp.dot(inputs, router_weight, preferred_element_type=jnp.float32)
    onehot = (routes[:, :, None] == jnp.arange(n_experts, dtype=jnp.int32)[None, None, :]).astype(
        jnp.float32
    )
    chosen = jnp.sum(onehot * logits[:, None, :], axis=2)
    gate_vals = 1.0 / (1.0 + jnp.exp(chosen[:, ::-1] - chosen))
    flat_routes = routes.reshape(-1)
    window_ids = jnp.arange(window, dtype=jnp.int32)
    mine = (flat_routes[None, :] == window_ids[:, None]).astype(jnp.int32)
    slot_pos = jnp.cumsum(mine, axis=1) - mine
    slot_ids = jnp.arange(CAP, dtype=jnp.int32)
    sel_route = (
        (slot_pos[:, None, :] == slot_ids[None, :, None]) & (mine[:, None, :] == 1)
    ).astype(jnp.float32)
    sel_token = sel_route.reshape(window, CAP, tok_rows, TOPK).sum(axis=3)
    slot_gate = jnp.einsum(
        "esr,r->es", sel_route, gate_vals.reshape(-1), precision=lax.Precision.HIGHEST
    )
    sel_flat = sel_token.reshape(window * CAP, tok_rows).astype(jnp.bfloat16)
    x_sel = jnp.dot(sel_flat, inputs, preferred_element_type=jnp.float32).astype(jnp.bfloat16)
    dy_sel = jnp.dot(sel_flat, out_grad, preferred_element_type=jnp.float32)
    g_sel = (slot_gate.reshape(-1)[:, None] * dy_sel).astype(jnp.bfloat16)
    send_x = jnp.repeat(x_sel.reshape(window, CAP, d_model), split_count, axis=0)
    send_g = jnp.repeat(g_sel.reshape(window, CAP, d_model), split_count, axis=0)
    got_x, got_g = (
        lax.all_to_all(send_x, "local", split_axis=0, concat_axis=0, tiled=True),
        lax.all_to_all(send_g, "local", split_axis=0, concat_axis=0, tiled=True),
    )
    x_rows = got_x.reshape(-1, d_model)
    g_rows = got_g.reshape(-1, d_model)
    hidden, hid_grad, partial_value = expert_rows(x_rows, g_rows, w_in, w_out)
    returned = lax.all_to_all(
        partial_value.reshape(n_local, CAP, d_model),
        "local",
        split_axis=0,
        concat_axis=0,
        tiled=True,
    )
    grad_first = jnp.einsum("rd,rf->df", x_rows, hid_grad, preferred_element_type=jnp.float32)
    grad_second = jnp.einsum("rf,rd->fd", hidden, g_rows, preferred_element_type=jnp.float32)
    slot_grad = returned.astype(jnp.float32).reshape(window, split_count, CAP, d_model).sum(axis=1)
    in_grad = jnp.einsum(
        "est,esd->td", sel_token, slot_grad, precision=lax.Precision.HIGHEST
    ).astype(jnp.bfloat16)
    summed_first, summed_second = (
        lax.psum_scatter(
            grad_first.astype(jnp.bfloat16), "group", scatter_dimension=0, tiled=True
        ).astype(jnp.float32),
        lax.psum_scatter(
            grad_second.astype(jnp.bfloat16), "group", scatter_dimension=1, tiled=True
        ).astype(jnp.float32),
    )
    return (in_grad, summed_first.astype(jnp.bfloat16), summed_second.astype(jnp.bfloat16))


def solution(mesh):
    return jax.shard_map(
        shards,
        mesh=mesh,
        in_specs=(
            P(("group", "local"), None),
            P(("group", "local"), None),
            P(("group", "local"), None),
            P(),
            P(None, "local"),
            P("local", None),
        ),
        out_specs=(P(("group", "local"), None), P("group", "local"), P("local", "group")),
        check_vma=False,
    )
```

profile of v0, /device:TPU:4, one launch (start us, length us, event | category | flops | bytes accessed | tf_op | source)
XLA Modules:
  0.0 720.6 jit_solution(812072311462310996)
XLA Ops:
  7.2 0.9 copy.41
  8.1 0.1 eq.96
  8.3 1.2 reduce-window.6
  9.7 0.7 convert_compare_fusion.1
  10.9 0.7 convert_subtract_fusion.1
  11.6 1.2 convolution_convert_fusion.3
  12.9 1.5 broadcast_in_dim.5
  14.4 34.6 %all-to-all-start.1 = ((bf16[64,4,2048]{2,1,0:T(4,128)(2,1)}), bf16[64,4,2048]{2,1,0:T(4,128)(2,1)S(1)}, u32[]{:S(2)}, u32[]{:S(2)}) async-start(bf16[64,4,2048]{2,1,0:T(4,128)(2,1)} %bitcast.40), calls=%async_computation.1 | async-start | bytes 2097152 | tf_op jit(solution)/shard_map/all_to_all | solution.py:70
  49.0 0.1 eq.108
  49.3 1.5 fusion.18
  50.8 0.2 select_reduce_fusion
  51.1 0.1 reshape.184
  51.4 1.2 fusion.1
  52.7 42.9 %all-to-all-done.1 = bf16[64,4,2048]{2,1,0:T(4,128)(2,1)S(1)} async-done(((bf16[64,4,2048]{2,1,0:T(4,128)(2,1)}), bf16[64,4,2048]{2,1,0:T(4,128)(2,1)S(1)}, u32[]{:S(2)}, u32[]{:S(2)}) %all-to-all-start.1) | async-done | bytes 1048608 | tf_op jit(solution)/shard_map/all_to_all | solution.py:70
  95.5 1.5 broadcast_in_dim.4
  97.1 8.1 %all-to-all-start = ((bf16[64,4,2048]{2,1,0:T(4,128)(2,1)}), bf16[64,4,2048]{2,1,0:T(4,128)(2,1)}, u32[]{:S(2)}, u32[]{:S(2)}) async-start(bf16[64,4,2048]{2,1,0:T(4,128)(2,1)} %bitcast.41), calls=%async_computation | async-start | bytes 2097152 | tf_op jit(solution)/shard_map/all_to_all | solution.py:71
  105.2 1.3 reshape.178
  106.5 1.5 fusion.19
  108.0 55.4 %all-to-all-done = bf16[64,4,2048]{2,1,0:T(4,128)(2,1)} async-done(((bf16[64,4,2048]{2,1,0:T(4,128)(2,1)}), bf16[64,4,2048]{2,1,0:T(4,128)(2,1)}, u32[]{:S(2)}, u32[]{:S(2)}) %all-to-all-start) | async-done | bytes 1048608 | tf_op jit(solution)/shard_map/all_to_all | solution.py:71
  163.4 2.1 reshape.175
  165.5 2.9 fusion.2
  168.5 1.7 convolution_convert_fusion.2
  170.2 2.3 reshape.179
  172.4 26.4 %all-to-all-start.2 = ((bf16[64,4,2048]{2,1,0:T(4,128)(2,1)}), bf16[64,4,2048]{2,1,0:T(4,128)(2,1)}, u32[]{:S(2)}, u32[]{:S(2)}) async-start(bf16[64,4,2048]{2,1,0:T(4,128)(2,1)} %reshape.179), calls=%async_computation.2 | async-start | bytes 2097152 | tf_op jit(solution)/shard_map/all_to_all | solution.py:76
  198.9 3.6 convolution_convert_fusion
  202.5 3.9 copy.51
  206.5 2.1 convolution_convert_fusion.1
  208.7 301.0 %reduce-scatter.7.cloned.1.call-done = bf16[128,512]{1,0:T(8,128)(2,1)} async-done(((bf16[2048,512]{1,0:T(8,128)(2,1)}), bf16[128,512]{1,0:T(8,128)(2,1)}) %reduce-scatter.7.cloned.1.call-update) | async-done | bytes 131088
  509.6 1.7 copy.52
  511.3 1.7 convert_reduce_fusion
  513.0 1.8 fusion
  514.8 198.9 %reduce-scatter.5.cloned.1.call-done = bf16[128,512]{1,0:T(8,128)(2,1)} async-done(((bf16[2048,512]{1,0:T(8,128)(2,1)}), bf16[128,512]{1,0:T(8,128)(2,1)}) %reduce-scatter.5.cloned.1.call-update) | async-done | bytes 131088 | tf_op jit(solution)/shard_map/reduce_scatter | solution.py:90
  (36 shorter events, 1.3 us)
Async XLA Ops:
  7.2 99.4 %copy-start = (bf16[2048,512]{1,0:T(8,128)(2,1)S(1)}, bf16[2048,512]{1,0:T(8,128)(2,1)}, u32[]{:S(2)}) copy-start(bf16[2048,512]{1,0:T(8,128)(2,1)} %param.10) | copy-start | bytes 6291460
  12.9 37.9 %copy-start.2 = (s32[128,2]{0,1:T(2,128)S(1)}, s32[128,2]{0,1:T(2,128)}, u32[]{:S(2)}) copy-start(s32[128,2]{0,1:T(2,128)} %param.8) | copy-start | bytes 3076
  14.4 81.1 %all-to-all-start.1 = ((bf16[64,4,2048]{2,1,0:T(4,128)(2,1)}), bf16[64,4,2048]{2,1,0:T(4,128)(2,1)S(1)}, u32[]{:S(2)}, u32[]{:S(2)}) async-start(bf16[64,4,2048]{2,1,0:T(4,128)(2,1)} %bitcast.40), calls=%async_computation.1 | async-start | bytes 2097152 | tf_op jit(solution)/shard_map/all_to_all | solution.py:70
  95.5 1.5 copy-start.1
  97.1 66.3 %all-to-all-start = ((bf16[64,4,2048]{2,1,0:T(4,128)(2,1)}), bf16[64,4,2048]{2,1,0:T(4,128)(2,1)}, u32[]{:S(2)}, u32[]{:S(2)}) async-start(bf16[64,4,2048]{2,1,0:T(4,128)(2,1)} %bitcast.41), calls=%async_computation | async-start | bytes 2097152 | tf_op jit(solution)/shard_map/all_to_all | solution.py:71
  172.4 338.8 %all-to-all-start.2 = ((bf16[64,4,2048]{2,1,0:T(4,128)(2,1)}), bf16[64,4,2048]{2,1,0:T(4,128)(2,1)}, u32[]{:S(2)}, u32[]{:S(2)}) async-start(bf16[64,4,2048]{2,1,0:T(4,128)(2,1)} %reshape.179), calls=%async_computation.2 | async-start | bytes 2097152 | tf_op jit(solution)/shard_map/all_to_all | solution.py:76
  198.9 310.7 %reduce-scatter.7.cloned.1.call-start = ((), (), s32[]{:S(2)}) async-start(), calls=%async_computation.6 | async-start | bytes 2228224
  206.5 507.2 %reduce-scatter.5.cloned.1.call-start = ((), (), s32[]{:S(2)}) async-start(), calls=%async_computation.5 | async-start | bytes 2228224 | tf_op jit(solution)/shard_map/reduce_scatter | solution.py:90
Sparse Core Ops, SparseCore 0:
  206.6 302.9 reduce-scatter.6
  513.6 200.0 reduce-scatter.4
where the time goes:
time: 721 us
  waiting for transfers between devices  598 us (83%)
  starting transfers between devices  69.2 us (10%)
  matrix products  17.7 us (2%)
  local copies, waits for them, and re-layouts  16.6 us (2%)
  between operations  14.2 us (2%)
    unnamed x3, waiting for transfers between devices  301 us
    reduce_scatter x1, waiting for transfers between devices, shards(): lax.psum_scatter(grad_first.astype(jnp.bfloat16), 'group', scatter_dimens...  199 us
    all_to_all x1, waiting for transfers between devices, shards(): lax.all_to_all(send_g, 'local', split_axis=0, concat_axis=0, tiled=True)  55.4 us
    all_to_all x1, waiting for transfers between devices, shards(): lax.all_to_all(send_x, 'local', split_axis=0, concat_axis=0, tiled=True)  42.9 us
    all_to_all x1, starting transfers between devices, shards(): lax.all_to_all(send_x, 'local', split_axis=0, concat_axis=0, tiled=True)  34.6 us
    all_to_all x1, starting transfers between devices, shards(): lax.all_to_all(partial_value.reshape(n_local, CAP, d_model), 'local', spl...  26.4 us
  transfers between devices with their start and end apart: 5, of which 4 were waited for; matrix products, arithmetic and copies ran while one was open for 3% of the time, Pallas kernels for 0%

commit v1 on v0

v1 whole, which is shorter than its diff:
```python
import jax
import jax.numpy as jnp
from jax import lax
from jax.sharding import Mesh, PartitionSpec as P

CAP = 4
SPLIT_AXES = (16, 4, 2, 4, 2)
AXES = ("group", "x", "zh", "y", "core")
LOCAL = ("x", "zh", "y", "core")

gelu_c = 0.7978845608
gelu_a = 0.044715


def gelu_pair(pre_act):
    inner = gelu_c * (pre_act + gelu_a * pre_act * pre_act * pre_act)
    tval = jnp.tanh(inner)
    value = 0.5 * pre_act * (1.0 + tval)
    slope = 0.5 * (1.0 + tval) + 0.5 * pre_act * (1.0 - tval * tval) * gelu_c * (
        1.0 + 3.0 * gelu_a * pre_act * pre_act
    )
    return (value, slope)


def dot_f32(a, b, dims):
    return lax.dot_general(a, b, (dims, ((), ())), preferred_element_type=jnp.float32)


def swap(value, axis):
    return lax.ppermute(value, axis, [(0, 1), (1, 0)])


def shift(value, by):
    return lax.ppermute(value, "y", [(i, (i + by) % 4) for i in range(4)])


def slot_rows(inputs, out_grad, routes, router_weight):
    tok_rows = inputs.shape[0]
    n_experts = router_weight.shape[1]
    first, second = routes[:, 0], routes[:, 1]
    expert = lax.broadcasted_iota(jnp.int32, (4, tok_rows), 0)
    mine = (first[None, :] == expert) | (second[None, :] == expert)
    other = jnp.where(mine, first[None, :] + second[None, :] - expert, 0)
    earlier = (
        lax.broadcasted_iota(jnp.int32, (tok_rows, tok_rows), 0)
        < lax.broadcasted_iota(jnp.int32, (tok_rows, tok_rows), 1)
    ).astype(jnp.bfloat16)
    slot_pos = dot_f32(mine.astype(jnp.bfloat16), earlier, ((1,), (0,))).astype(jnp.int32)
    slot_ids = lax.broadcasted_iota(jnp.int32, (4, 2 * CAP, tok_rows), 1) % CAP
    picked = mine[:, None, :] & (slot_pos[:, None, :] == slot_ids)
    sel = picked.reshape(-1, tok_rows)
    other_of = jnp.sum(jnp.where(picked, other[:, None, :], 0), axis=2).reshape(-1)
    sel_bf = sel.astype(jnp.bfloat16)
    x_sel = dot_f32(sel_bf, inputs, ((1,), (0,))).astype(jnp.bfloat16)
    dy_sel = dot_f32(sel_bf, out_grad, ((1,), (0,)))
    logits = dot_f32(x_sel, router_weight, ((1,), (0,)))
    n_rows = sel.shape[0]
    lane = lax.broadcasted_iota(jnp.int32, (n_rows, n_experts), 1)
    row = lax.broadcasted_iota(jnp.int32, (n_rows, n_experts), 0)
    own_logit = jnp.sum(jnp.where(lane == row // (2 * CAP), logits, 0.0), axis=1)
    other_logit = jnp.sum(jnp.where(lane == other_of[:, None], logits, 0.0), axis=1)
    gate = 1.0 / (1.0 + jnp.exp(other_logit - own_logit))
    g_sel = (gate[:, None] * dy_sel).astype(jnp.bfloat16)
    is_x = (lax.broadcasted_iota(jnp.int32, (n_rows, 1), 0) // CAP) % 2 == 0
    return jnp.where(is_x, x_sel, g_sel), sel_bf


def gather_plane(rows):
    pieces = [rows] + [shift(rows, by) for by in (1, 3, 2)]
    own = jnp.concatenate(pieces, axis=1)
    both = jnp.concatenate([own, swap(own, "core")], axis=1)
    return both[0], both[1]


def return_plane(partial):
    half = partial.shape[0] // 2
    core_sum = partial[:half].astype(jnp.float32) + swap(partial[half:], "core").astype(jnp.float32)
    core_sum = core_sum.astype(jnp.bfloat16).reshape(4, half // 4, -1)
    total = core_sum[0].astype(jnp.float32)
    for k, by in ((1, 3), (2, 1), (3, 2)):
        total = total + shift(core_sum[k], by).astype(jnp.float32)
    return total


def expert_part(x_rows, g_rows, w_in, w_out):
    pre_act = dot_f32(x_rows, w_in, ((1,), (0,)))
    value, slope = gelu_pair(pre_act)
    back_hid = dot_f32(g_rows, w_out, ((1,), (1,)))
    hid_grad = (back_hid * slope).astype(jnp.bfloat16)
    partial = dot_f32(hid_grad, w_in, ((1,), (1,))).astype(jnp.bfloat16)
    return value.astype(jnp.bfloat16), hid_grad, partial


def shards(inputs, out_grad, routes, router_weight, w_in, w_out):
    d_model = inputs.shape[1]
    ff_dev = w_in.shape[1]
    send, sel = slot_rows(inputs, out_grad, routes, router_weight)
    got = lax.all_to_all(send.reshape(4, 2 * CAP, d_model), "x", 0, 0, tiled=True)
    near = got.reshape(4, 2, CAP, d_model).transpose(1, 0, 2, 3).reshape(2, 4 * CAP, d_model)
    far = swap(near, "zh")
    x_near, g_near = gather_plane(near)
    hidden_near, hid_grad_near, partial_near = expert_part(x_near, g_near, w_in, w_out)
    x_far, g_far = gather_plane(far)
    hidden_far, hid_grad_far, partial_far = expert_part(x_far, g_far, w_in, w_out)
    x_all = jnp.concatenate([x_near, x_far], axis=0)
    g_all = jnp.concatenate([g_near, g_far], axis=0)
    hidden = jnp.concatenate([hidden_near, hidden_far], axis=0)
    hid_grad = jnp.concatenate([hid_grad_near, hid_grad_far], axis=0)
    grad_in = dot_f32(x_all, hid_grad, ((0,), (0,))).astype(jnp.bfloat16)
    grad_out = dot_f32(g_all, hidden, ((0,), (0,))).astype(jnp.bfloat16)
    both = lax.psum_scatter(
        jnp.concatenate([grad_in, grad_out], axis=1), "group", scatter_dimension=0, tiled=True
    )
    back_far = return_plane(partial_far).astype(jnp.bfloat16)
    slots = return_plane(partial_near) + swap(back_far, "zh").astype(jnp.float32)
    slots = lax.all_to_all(
        slots.astype(jnp.bfloat16).reshape(4, CAP, d_model), "x", 0, 0, tiled=True
    ).reshape(4 * CAP, d_model)
    n_tok = inputs.shape[0]
    sel_slots = sel.reshape(4, 2, CAP, n_tok)[:, 0].reshape(4 * CAP, n_tok)
    in_grad = dot_f32(sel_slots, slots, ((0,), (0,))).astype(jnp.bfloat16)
    return in_grad, both[:, :ff_dev], both[:, ff_dev:].T


def solution(mesh):
    fine = Mesh(mesh.devices.reshape(SPLIT_AXES), AXES)
    everyone = ("group",) + LOCAL
    return jax.shard_map(
        shards,
        mesh=fine,
        in_specs=(
            P(everyone, None),
            P(everyone, None),
            P(everyone, None),
            P(),
            P(None, LOCAL),
            P(LOCAL, None),
        ),
        out_specs=(P(everyone, None), P("group", LOCAL), P(LOCAL, "group")),
        check_vma=False,
    )
```

time: 721 us -> 352 us (0.49)
  the two profiles are of different devices: /device:TPU:4 before, /device:TPU:2 now
where the time goes in v1:
time: 352 us; the launch traced here: 351 us
  waiting for transfers between devices  187 us (53%)
  starting transfers between devices  94.4 us (27%)
  blocking collectives  20.1 us (6%)
  local copies, waits for them, and re-layouts  17.6 us (5%)
  between operations  14.6 us (4%)
  matrix products  11.2 us (3%)
  other arithmetic  5.47 us (2%)
    unnamed x2, waiting for transfers between devices  173 us
    ppermute x6, starting transfers between devices, swap(): return lax.ppermute(value, axis, [(0, 1), (1, 0)])  50.3 us
    ppermute x12, starting transfers between devices, shift(): return lax.ppermute(value, 'y', [(i, (i + by) % 4) for i in range(4)])  39.3 us
    all_to_all x1, blocking collectives, shards(): lax.all_to_all(send.reshape(4, 2 * CAP, d_model), 'x', 0, 0, tiled=True)  20.1 us
    dot_general x13, matrix products, dot_f32(): lax.dot_general(a, b, (dims, ((), ())), preferred_element_type=jnp.float32)  11.2 us
    unnamed x22, local copies, waits for them, and re-layouts  9.96 us
  transfers between devices with their start and end apart: 20, of which 6 were waited for; matrix products, arithmetic and copies ran while one was open for 3% of the time, Pallas kernels for 0%

profile of v1, /device:TPU:2, one launch (start us, length us, event | category | flops | bytes accessed | tf_op | source)
XLA Modules:
  0.0 350.6 jit_solution(11579458669455468335)
XLA Ops:
  10.9 1.4 select_reduce_fusion
  13.6 20.1 %all_to_all.10 = bf16[4,8,2048]{2,1,0:T(8,128)(2,1)S(1)} all-to-all(bf16[4,8,2048]{2,1,0:T(8,128)(2,1)S(1)} %fusion.2), channel_id=1, replica_groups=mesh['group'=16,'x'=4,'zh'=2,'y'=4,'core'=2] {'x'}, dimensions={0} | all-to-all | bytes 262144 | tf_op jit(solution)/shard_map/all_to_all | solution.py:98
  33.9 1.9 collective-permute-start
  35.9 5.1 %collective-permute-start.1 = (bf16[2,16,2048]{2,0,1:T(2,128)(2,1)S(1)}, bf16[2,16,2048]{2,0,1:T(2,128)(2,1)S(1)}, u32[]{:S(2)}, u32[]{:S(2)}) collective-permute-start(bf16[2,16,2048]{2,0,1:T(2,128)(2,1)S(1)} %bitcast.64), channel_id=1, source_target_pairs={{0,6},{2,0},{4,2},{6,4},{1,7},{3,1},{5,3},{7,5},{8,14},{10,8},{12,... | collective-permute-start | bytes 393224 | tf_op jit(solution)/shard_map/ppermute | solution.py:34
  41.0 1.9 collective-permute-start.2
  42.9 20.0 %collective-permute-start.8 = (bf16[2,16,2048]{2,0,1:T(2,128)(2,1)S(1)}, bf16[2,16,2048]{2,0,1:T(2,128)(2,1)S(1)}, u32[]{:S(2)}, u32[]{:S(2)}) collective-permute-start(bf16[2,16,2048]{2,0,1:T(2,128)(2,1)S(1)} %bitcast.66), channel_id=1, source_target_pairs={{0,8},{8,0},{1,9},{9,1},{2,10},{10,2},{3,11},{11,3},{4,12},{12,4},... | collective-permute-start | bytes 393224 | tf_op jit(solution)/shard_map/ppermute | solution.py:30
  63.8 1.9 collective-permute-start.3
  65.8 2.7 collective-permute-done.8
  68.6 2.8 collective-permute-start.9
  71.4 4.3 %collective-permute-start.10 = (bf16[2,16,2048]{2,0,1:T(2,128)(2,1)S(1)}, bf16[2,16,2048]{2,0,1:T(2,128)(2,1)S(1)}, u32[]{:S(2)}, u32[]{:S(2)}) collective-permute-start(bf16[2,16,2048]{2,0,1:T(2,128)(2,1)S(1)} %collective-permute-done.8), channel_id=1, source_target_pairs={{0,6},{2,0},{4,2},{6,4},{1,7},{3,1},{5,3},{7,5},{8,14},{10,8},{12,... | collective-permute-start | bytes 393224 | tf_op jit(solution)/shard_map/ppermute | solution.py:34
  75.7 4.3 %collective-permute-start.11 = (bf16[2,16,2048]{2,0,1:T(2,128)(2,1)S(1)}, bf16[2,16,2048]{2,0,1:T(2,128)(2,1)S(1)}, u32[]{:S(2)}, u32[]{:S(2)}) collective-permute-start(bf16[2,16,2048]{2,0,1:T(2,128)(2,1)S(1)} %collective-permute-done.8), channel_id=1, source_target_pairs={{0,4},{2,6},{4,0},{6,2},{1,5},{3,7},{5,1},{7,3},{8,12},{10,14},{12... | collective-permute-start | bytes 393224 | tf_op jit(solution)/shard_map/ppermute | solution.py:34
  80.3 3.8 %collective-permute-done.11 = bf16[2,16,2048]{2,0,1:T(2,128)(2,1)S(1)} collective-permute-done((bf16[2,16,2048]{2,0,1:T(2,128)(2,1)S(1)}, bf16[2,16,2048]{2,0,1:T(2,128)(2,1)S(1)}, u32[]{:S(2)}, u32[]{:S(2)}) %collective-permute-start.11) | collective-permute-done | bytes 131104 | tf_op jit(solution)/shard_map/ppermute | solution.py:34
  84.8 2.1 collective-permute-start.12
  87.7 1.5 fusion.49
  92.4 1.5 fusion.50
  97.5 2.6 pad_maximum_fusion
  100.1 6.4 %copy.37 = bf16[2048,1024]{1,0:T(8,128)(2,1)} copy(bf16[2048,1024]{0,1:T(8,128)(2,1)} %pad_maximum_fusion) | data formatting | bytes 8388608
  107.4 2.4 collective-permute-start.4
  110.7 1.9 collective-permute-start.13
  112.7 1.4 collective-permute-done.13
  114.2 2.8 collective-permute-start.14
  117.0 3.0 collective-permute-start.15
  120.0 4.3 %collective-permute-start.16 = (bf16[16,2048]{1,0:T(8,128)(2,1)S(1)}, bf16[16,2048]{1,0:T(8,128)(2,1)S(1)}, u32[]{:S(2)}, u32[]{:S(2)}) collective-permute-start(bf16[16,2048]{1,0:T(8,128)(2,1)S(1)} %get-tuple-element.38), channel_id=1, source_target_pairs={{0,4},{2,6},{4,0},{6,2},{1,5},{3,7},{5,1},{7,3},{8,12},{10,14},{12... | collective-permute-start | bytes 196616 | tf_op jit(solution)/shard_map/ppermute | solution.py:34
  124.4 2.5 collective-permute-start.5
  126.9 3.3 collective-permute-start.6
  130.2 3.1 collective-permute-start.7
  133.4 22.0 %collective-permute-start.17 = (bf16[16,2048]{1,0:T(8,128)(2,1)S(1)}, bf16[16,2048]{1,0:T(8,128)(2,1)S(1)}, u32[]{:S(2)}, u32[]{:S(2)}) collective-permute-start(bf16[16,2048]{1,0:T(8,128)(2,1)S(1)} %add_convert_fusion.3), channel_id=1, source_target_pairs={{0,8},{8,0},{1,9},{9,1},{2,10},{10,2},{3,11},{11,3},{4,12},{12,4},... | collective-permute-start | bytes 196616 | tf_op jit(solution)/shard_map/ppermute | solution.py:30
  155.4 2.7 collective-permute-done.17
  158.8 4.7 %all-to-all-start.1 = ((bf16[4,4,2048]{2,1,0:T(4,128)(2,1)}), bf16[4,4,2048]{2,1,0:T(4,128)(2,1)S(1)}, u32[]{:S(2)}, u32[]{:S(2)}) async-start(bf16[4,4,2048]{2,1,0:T(4,128)(2,1)} %reshape.216), calls=%async_computation.1 | async-start | bytes 131072 | tf_op jit(solution)/shard_map/all_to_all | solution.py:116
  163.5 4.1 %all-to-all-done.1 = bf16[4,4,2048]{2,1,0:T(4,128)(2,1)S(1)} async-done(((bf16[4,4,2048]{2,1,0:T(4,128)(2,1)}), bf16[4,4,2048]{2,1,0:T(4,128)(2,1)S(1)}, u32[]{:S(2)}, u32[]{:S(2)}) %all-to-all-start.1) | async-done | bytes 65568 | tf_op jit(solution)/shard_map/all_to_all | solution.py:116
  168.8 172.6 %reduce-scatter.4.cloned.1.call-done = bf16[128,1024]{1,0:T(8,128)(2,1)} async-done(((bf16[2048,1024]{1,0:T(8,128)(2,1)}), bf16[128,1024]{1,0:T(8,128)(2,1)}) %reduce-scatter.4.cloned.1.call-update) | async-done | bytes 262160
  341.4 1.6 fusion.51
  (90 shorter events, 19.3 us)
Async XLA Ops:
  7.2 82.6 %copy-start = (bf16[2048,512]{1,0:T(8,128)(2,1)S(1)}, bf16[2048,512]{1,0:T(8,128)(2,1)}, u32[]{:S(2)}) copy-start(bf16[2048,512]{1,0:T(8,128)(2,1)} %param.10) | copy-start | bytes 6291460
  7.2 334.2 %reduce-scatter.4.cloned.1.call-start = ((), (), s32[]{:S(2)}) async-start(), calls=%async_computation.3 | async-start | bytes 4456448
  33.9 29.1 %collective-permute-start = (bf16[2,16,2048]{2,0,1:T(2,128)(2,1)S(1)}, bf16[2,16,2048]{2,0,1:T(2,128)(2,1)S(1)}, u32[]{:S(2)}, u32[]{:S(2)}) collective-permute-start(bf16[2,16,2048]{2,0,1:T(2,128)(2,1)S(1)} %bitcast.63), channel_id=1, source_target_pairs={{0,2},{2,4},{4,6},{6,0},{1,3},{3,5},{5,7},{7,1},{8,10},{10,12},{12... | collective-permute-start | bytes 393224 | tf_op jit(solution)/shard_map/ppermute | solution.py:34
  35.9 27.2 %collective-permute-start.1 = (bf16[2,16,2048]{2,0,1:T(2,128)(2,1)S(1)}, bf16[2,16,2048]{2,0,1:T(2,128)(2,1)S(1)}, u32[]{:S(2)}, u32[]{:S(2)}) collective-permute-start(bf16[2,16,2048]{2,0,1:T(2,128)(2,1)S(1)} %bitcast.64), channel_id=1, source_target_pairs={{0,6},{2,0},{4,2},{6,4},{1,7},{3,1},{5,3},{7,5},{8,14},{10,8},{12,... | collective-permute-start | bytes 393224 | tf_op jit(solution)/shard_map/ppermute | solution.py:34
  41.0 22.1 %collective-permute-start.2 = (bf16[2,16,2048]{2,0,1:T(2,128)(2,1)S(1)}, bf16[2,16,2048]{2,0,1:T(2,128)(2,1)S(1)}, u32[]{:S(2)}, u32[]{:S(2)}) collective-permute-start(bf16[2,16,2048]{2,0,1:T(2,128)(2,1)S(1)} %bitcast.65), channel_id=1, source_target_pairs={{0,4},{2,6},{4,0},{6,2},{1,5},{3,7},{5,1},{7,3},{8,12},{10,14},{12... | collective-permute-start | bytes 393224 | tf_op jit(solution)/shard_map/ppermute | solution.py:34
  42.9 25.6 %collective-permute-start.8 = (bf16[2,16,2048]{2,0,1:T(2,128)(2,1)S(1)}, bf16[2,16,2048]{2,0,1:T(2,128)(2,1)S(1)}, u32[]{:S(2)}, u32[]{:S(2)}) collective-permute-start(bf16[2,16,2048]{2,0,1:T(2,128)(2,1)S(1)} %bitcast.66), channel_id=1, source_target_pairs={{0,8},{8,0},{1,9},{9,1},{2,10},{10,2},{3,11},{11,3},{4,12},{12,4},... | collective-permute-start | bytes 393224 | tf_op jit(solution)/shard_map/ppermute | solution.py:30
  63.8 23.4 %collective-permute-start.3 = (bf16[2,64,2048]{2,0,1:T(2,128)(2,1)S(1)}, bf16[2,64,2048]{2,0,1:T(2,128)(2,1)S(1)}, u32[]{:S(2)}, u32[]{:S(2)}) collective-permute-start(bf16[2,64,2048]{2,0,1:T(2,128)(2,1)S(1)} %pad_maximum_fusion.1), channel_id=1, source_target_pairs={{0,1},{1,0},{2,3},{3,2},{4,5},{5,4},{6,7},{7,6},{8,9},{9,8},{10,11... | collective-permute-start | bytes 1572872 | tf_op jit(solution)/shard_map/ppermute | solution.py:30
  68.6 11.7 %collective-permute-start.9 = (bf16[2,16,2048]{2,0,1:T(2,128)(2,1)S(1)}, bf16[2,16,2048]{2,0,1:T(2,128)(2,1)S(1)}, u32[]{:S(2)}, u32[]{:S(2)}) collective-permute-start(bf16[2,16,2048]{2,0,1:T(2,128)(2,1)S(1)} %collective-permute-done.8), channel_id=1, source_target_pairs={{0,2},{2,4},{4,6},{6,0},{1,3},{3,5},{5,7},{7,1},{8,10},{10,12},{12... | collective-permute-start | bytes 393224 | tf_op jit(solution)/shard_map/ppermute | solution.py:34
  71.4 8.9 %collective-permute-start.10 = (bf16[2,16,2048]{2,0,1:T(2,128)(2,1)S(1)}, bf16[2,16,2048]{2,0,1:T(2,128)(2,1)S(1)}, u32[]{:S(2)}, u32[]{:S(2)}) collective-permute-start(bf16[2,16,2048]{2,0,1:T(2,128)(2,1)S(1)} %collective-permute-done.8), channel_id=1, source_target_pairs={{0,6},{2,0},{4,2},{6,4},{1,7},{3,1},{5,3},{7,5},{8,14},{10,8},{12,... | collective-permute-start | bytes 393224 | tf_op jit(solution)/shard_map/ppermute | solution.py:34
  75.7 8.4 %collective-permute-start.11 = (bf16[2,16,2048]{2,0,1:T(2,128)(2,1)S(1)}, bf16[2,16,2048]{2,0,1:T(2,128)(2,1)S(1)}, u32[]{:S(2)}, u32[]{:S(2)}) collective-permute-start(bf16[2,16,2048]{2,0,1:T(2,128)(2,1)S(1)} %collective-permute-done.8), channel_id=1, source_target_pairs={{0,4},{2,6},{4,0},{6,2},{1,5},{3,7},{5,1},{7,3},{8,12},{10,14},{12... | collective-permute-start | bytes 393224 | tf_op jit(solution)/shard_map/ppermute | solution.py:34
  84.8 7.2 %collective-permute-start.12 = (bf16[2,64,2048]{2,0,1:T(2,128)(2,1)S(1)}, bf16[2,64,2048]{2,0,1:T(2,128)(2,1)S(1)}, u32[]{:S(2)}, u32[]{:S(2)}) collective-permute-start(bf16[2,64,2048]{2,0,1:T(2,128)(2,1)S(1)} %pad_maximum_fusion.2), channel_id=1, source_target_pairs={{0,1},{1,0},{2,3},{3,2},{4,5},{5,4},{6,7},{7,6},{8,9},{9,8},{10,11... | collective-permute-start | bytes 1572872 | tf_op jit(solution)/shard_map/ppermute | solution.py:30
  89.5 1.6 copy-start.3
  106.5 4.1 %copy-start.1 = (s32[2,4]{1,0:T(2,128)}, s32[2,4]{1,0:T(2,128)S(1)}, u32[]{:S(2)}) copy-start(s32[2,4]{1,0:T(2,128)S(1)} %broadcast_add_fusion) | copy-start | bytes 100
  106.5 4.1 %copy-start.2 = (s32[2,4]{1,0:T(2,128)}, s32[2,4]{1,0:T(2,128)S(1)}, u32[]{:S(2)}) copy-start(s32[2,4]{1,0:T(2,128)S(1)} %add_and_fusion) | copy-start | bytes 100
  107.4 5.2 %collective-permute-start.4 = (bf16[64,2048]{1,0:T(8,128)(2,1)S(1)}, bf16[64,2048]{1,0:T(8,128)(2,1)S(1)}, u32[]{:S(2)}, u32[]{:S(2)}) collective-permute-start(bf16[64,2048]{1,0:T(8,128)(2,1)S(1)} %slice.98), channel_id=1, source_target_pairs={{0,1},{1,0},{2,3},{3,2},{4,5},{5,4},{6,7},{7,6},{8,9},{9,8},{10,11... | collective-permute-start | bytes 786440 | tf_op jit(solution)/shard_map/ppermute | solution.py:30
  110.6 52.8 %slice-start = ((s32[2,4]{1,0:T(2,128)}), s32[1,4]{1,0:T(1,128)S(1)}, s32[]{:S(2)}) async-start(s32[2,4]{1,0:T(2,128)} %copy-done.1), calls=%async_computation.4 | async-start | bytes 1024 | tf_op jit(solution)/shard_map/slice | solution.py:120
  110.7 52.8 %slice-start.1 = ((s32[2,4]{1,0:T(2,128)}), s32[1,4]{1,0:T(1,128)S(1)}, s32[]{:S(2)}) async-start(s32[2,4]{1,0:T(2,128)} %copy-done.2), calls=%async_computation.5 | async-start | bytes 1024 | tf_op jit(solution)/shard_map/slice | solution.py:120
  110.7 3.4 collective-permute-start.13
  114.2 16.0 %collective-permute-start.14 = (bf16[16,2048]{1,0:T(8,128)(2,1)S(1)}, bf16[16,2048]{1,0:T(8,128)(2,1)S(1)}, u32[]{:S(2)}, u32[]{:S(2)}) collective-permute-start(bf16[16,2048]{1,0:T(8,128)(2,1)S(1)} %get-tuple-element.37), channel_id=1, source_target_pairs={{0,6},{2,0},{4,2},{6,4},{1,7},{3,1},{5,3},{7,5},{8,14},{10,8},{12,... | collective-permute-start | bytes 196616 | tf_op jit(solution)/shard_map/ppermute | solution.py:34
  117.0 16.3 %collective-permute-start.15 = (bf16[16,2048]{1,0:T(8,128)(2,1)S(1)}, bf16[16,2048]{1,0:T(8,128)(2,1)S(1)}, u32[]{:S(2)}, u32[]{:S(2)}) collective-permute-start(bf16[16,2048]{1,0:T(8,128)(2,1)S(1)} %get-tuple-element.39), channel_id=1, source_target_pairs={{0,2},{2,4},{4,6},{6,0},{1,3},{3,5},{5,7},{7,1},{8,10},{10,12},{12... | collective-permute-start | bytes 196616 | tf_op jit(solution)/shard_map/ppermute | solution.py:34
  120.0 13.3 %collective-permute-start.16 = (bf16[16,2048]{1,0:T(8,128)(2,1)S(1)}, bf16[16,2048]{1,0:T(8,128)(2,1)S(1)}, u32[]{:S(2)}, u32[]{:S(2)}) collective-permute-start(bf16[16,2048]{1,0:T(8,128)(2,1)S(1)} %get-tuple-element.38), channel_id=1, source_target_pairs={{0,4},{2,6},{4,0},{6,2},{1,5},{3,7},{5,1},{7,3},{8,12},{10,14},{12... | collective-permute-start | bytes 196616 | tf_op jit(solution)/shard_map/ppermute | solution.py:34
  124.4 31.0 %collective-permute-start.5 = (bf16[16,2048]{1,0:T(8,128)(2,1)S(1)}, bf16[16,2048]{1,0:T(8,128)(2,1)S(1)}, u32[]{:S(2)}, u32[]{:S(2)}) collective-permute-start(bf16[16,2048]{1,0:T(8,128)(2,1)S(1)} %get-tuple-element.34), channel_id=1, source_target_pairs={{0,6},{2,0},{4,2},{6,4},{1,7},{3,1},{5,3},{7,5},{8,14},{10,8},{12,... | collective-permute-start | bytes 196616 | tf_op jit(solution)/shard_map/ppermute | solution.py:34
  126.9 28.5 %collective-permute-start.6 = (bf16[16,2048]{1,0:T(8,128)(2,1)S(1)}, bf16[16,2048]{1,0:T(8,128)(2,1)S(1)}, u32[]{:S(2)}, u32[]{:S(2)}) collective-permute-start(bf16[16,2048]{1,0:T(8,128)(2,1)S(1)} %get-tuple-element.36), channel_id=1, source_target_pairs={{0,2},{2,4},{4,6},{6,0},{1,3},{3,5},{5,7},{7,1},{8,10},{10,12},{12... | collective-permute-start | bytes 196616 | tf_op jit(solution)/shard_map/ppermute | solution.py:34
  130.2 25.2 %collective-permute-start.7 = (bf16[16,2048]{1,0:T(8,128)(2,1)S(1)}, bf16[16,2048]{1,0:T(8,128)(2,1)S(1)}, u32[]{:S(2)}, u32[]{:S(2)}) collective-permute-start(bf16[16,2048]{1,0:T(8,128)(2,1)S(1)} %get-tuple-element.35), channel_id=1, source_target_pairs={{0,4},{2,6},{4,0},{6,2},{1,5},{3,7},{5,1},{7,3},{8,12},{10,14},{12... | collective-permute-start | bytes 196616 | tf_op jit(solution)/shard_map/ppermute | solution.py:34
  133.4 24.7 %collective-permute-start.17 = (bf16[16,2048]{1,0:T(8,128)(2,1)S(1)}, bf16[16,2048]{1,0:T(8,128)(2,1)S(1)}, u32[]{:S(2)}, u32[]{:S(2)}) collective-permute-start(bf16[16,2048]{1,0:T(8,128)(2,1)S(1)} %add_convert_fusion.3), channel_id=1, source_target_pairs={{0,8},{8,0},{1,9},{9,1},{2,10},{10,2},{3,11},{11,3},{4,12},{12,4},... | collective-permute-start | bytes 196616 | tf_op jit(solution)/shard_map/ppermute | solution.py:30
  158.8 8.9 %all-to-all-start.1 = ((bf16[4,4,2048]{2,1,0:T(4,128)(2,1)}), bf16[4,4,2048]{2,1,0:T(4,128)(2,1)S(1)}, u32[]{:S(2)}, u32[]{:S(2)}) async-start(bf16[4,4,2048]{2,1,0:T(4,128)(2,1)} %reshape.216), calls=%async_computation.1 | async-start | bytes 131072 | tf_op jit(solution)/shard_map/all_to_all | solution.py:116
Sparse Core Ops, SparseCore 0:
  106.6 234.7 reduce-scatter.3

commit v2 on v1

--- a/solution.py
+++ b/solution.py
@@ -65,61 +65,115 @@
     return jnp.where(is_x, x_sel, g_sel), sel_bf
 
 
-def gather_plane(rows):
-    pieces = [rows] + [shift(rows, by) for by in (1, 3, 2)]
-    own = jnp.concatenate(pieces, axis=1)
-    both = jnp.concatenate([own, swap(own, "core")], axis=1)
-    return both[0], both[1]
+def kinds_apart(rows):
+    n_rows = rows.shape[0]
+    to = lax.broadcasted_iota(jnp.int32, (n_rows, n_rows), 0)
+    at = lax.broadcasted_iota(jnp.int32, (n_rows, n_rows), 1)
+    half = n_rows // 2
+    source = (to % half) // CAP * (2 * CAP) + to // half * CAP + to % CAP
+    return dot_f32((at == source).astype(jnp.bfloat16), rows, ((1,), (0,))).astype(jnp.bfloat16)
 
 
-def return_plane(partial):
-    half = partial.shape[0] // 2
-    core_sum = partial[:half].astype(jnp.float32) + swap(partial[half:], "core").astype(jnp.float32)
-    core_sum = core_sum.astype(jnp.bfloat16).reshape(4, half // 4, -1)
-    total = core_sum[0].astype(jnp.float32)
-    for k, by in ((1, 3), (2, 1), (3, 2)):
-        total = total + shift(core_sum[k], by).astype(jnp.float32)
-    return total
+def gather_plane(rows):
+    pieces = [rows, shift(rows, 3), shift(rows, 2), shift(rows, 1)]
+    across = swap(jnp.concatenate(pieces, axis=0), "core")
+    half = rows.shape[0] // 2
+    pieces += [across[k * 2 * half : (k + 1) * 2 * half] for k in range(4)]
+    return (
+        jnp.concatenate([p[:half] for p in pieces], axis=0),
+        jnp.concatenate([p[half:] for p in pieces], axis=0),
+    )
 
 
 def expert_part(x_rows, g_rows, w_in, w_out):
     pre_act = dot_f32(x_rows, w_in, ((1,), (0,)))
     value, slope = gelu_pair(pre_act)
     back_hid = dot_f32(g_rows, w_out, ((1,), (1,)))
-    hid_grad = (back_hid * slope).astype(jnp.bfloat16)
-    partial = dot_f32(hid_grad, w_in, ((1,), (1,))).astype(jnp.bfloat16)
-    return value.astype(jnp.bfloat16), hid_grad, partial
+    return value.astype(jnp.bfloat16), (back_hid * slope).astype(jnp.bfloat16)
+
+
+def row_order(n_rows):
+    to = lax.broadcasted_iota(jnp.int32, (n_rows, n_rows), 0)
+    at = lax.broadcasted_iota(jnp.int32, (n_rows, n_rows), 1)
+    y = (to // 64 - lax.axis_index("y")) & 3
+    core = (to // 32 - lax.axis_index("core")) & 1
+    zh = (to // 16 - lax.axis_index("zh")) & 1
+    return (at == zh * 128 + core * 64 + y * 16 + (to & 15)).astype(jnp.bfloat16)
+
+
+def flip_cores(rows):
+    n_rows, width = rows.shape
+    parts = rows.reshape(2, 2, n_rows // 4, width)
+    return jnp.concatenate([parts[:, 1:], parts[:, :1]], axis=1).reshape(n_rows, width)
+
+
+def columns(rows, begin, width):
+    return lax.dynamic_slice(
+        rows, (0, begin), (rows.shape[0], width), allow_negative_indices=False
+    )
+
+
+def line_sums(streams, n_group):
+    width = streams[0][0].shape[1] // n_group
+    top = (n_group - 1) * width
+    here = lax.axis_index("group") * width
+    towards = width * (1 - 2 * lax.axis_index("core"))
+    carried = [None] * len(streams)
+    for step in range(n_group - 1):
+        ahead = n_group - 1 - step
+        begin = lax.clamp(0, here + ahead * towards, top)
+        pairs = [(2 * i, 2 * i + 2) for i in range(step + 1)]
+        pairs += [(2 * n_group - 1 - 2 * i, 2 * n_group - 3 - 2 * i) for i in range(step + 1)]
+        for k, (rows, units) in enumerate(streams):
+            cut = columns(rows, begin, width)
+            term = dot_f32(cut, units, ((0,), (0,)))
+            if carried[k] is not None:
+                term = term + carried[k].astype(jnp.float32)
+            carried[k] = lax.ppermute(term.astype(jnp.bfloat16), ("group", "core"), pairs)
+    return carried
 
 
 def shards(inputs, out_grad, routes, router_weight, w_in, w_out):
-    d_model = inputs.shape[1]
+    n_tok, d_model = inputs.shape
     ff_dev = w_in.shape[1]
+    n_group = lax.axis_size("group")
     send, sel = slot_rows(inputs, out_grad, routes, router_weight)
     got = lax.all_to_all(send.reshape(4, 2 * CAP, d_model), "x", 0, 0, tiled=True)
-    near = got.reshape(4, 2, CAP, d_model).transpose(1, 0, 2, 3).reshape(2, 4 * CAP, d_model)
-    far = swap(near, "zh")
+    near = kinds_apart(got.reshape(8 * CAP, d_model))
+    far, order = lax.optimization_barrier((swap(near, "zh"), row_order(64 * CAP)))
     x_near, g_near = gather_plane(near)
-    hidden_near, hid_grad_near, partial_near = expert_part(x_near, g_near, w_in, w_out)
+    hidden_near, hid_grad_near = expert_part(x_near, g_near, w_in, w_out)
     x_far, g_far = gather_plane(far)
-    hidden_far, hid_grad_far, partial_far = expert_part(x_far, g_far, w_in, w_out)
+    hidden_far, hid_grad_far = expert_part(x_far, g_far, w_in, w_out)
     x_all = jnp.concatenate([x_near, x_far], axis=0)
     g_all = jnp.concatenate([g_near, g_far], axis=0)
     hidden = jnp.concatenate([hidden_near, hidden_far], axis=0)
     hid_grad = jnp.concatenate([hid_grad_near, hid_grad_far], axis=0)
-    grad_in = dot_f32(x_all, hid_grad, ((0,), (0,))).astype(jnp.bfloat16)
-    grad_out = dot_f32(g_all, hidden, ((0,), (0,))).astype(jnp.bfloat16)
-    both = lax.psum_scatter(
-        jnp.concatenate([grad_in, grad_out], axis=1), "group", scatter_dimension=0, tiled=True
-    )
-    back_far = return_plane(partial_far).astype(jnp.bfloat16)
-    slots = return_plane(partial_near) + swap(back_far, "zh").astype(jnp.float32)
-    slots = lax.all_to_all(
-        slots.astype(jnp.bfloat16).reshape(4, CAP, d_model), "x", 0, 0, tiled=True
-    ).reshape(4 * CAP, d_model)
-    n_tok = inputs.shape[0]
+    other = flip_cores(swap(jnp.concatenate([hid_grad, hidden], axis=1), "core"))
+    hid_grad_both = jnp.concatenate([hid_grad, other[:, :ff_dev]], axis=1)
+    hidden_both = jnp.concatenate([hidden, other[:, ff_dev:]], axis=1)
+
+    ordered = dot_f32(order, hid_grad, ((1,), (0,))).astype(jnp.bfloat16)
+    partial = dot_f32(ordered, w_in, ((1,), (1,))).astype(jnp.bfloat16)
+    hid_grad_both, partial = lax.optimization_barrier((hid_grad_both, partial))
+    plane = lax.psum_scatter(partial, ("y", "core"), scatter_dimension=0, tiled=True)
+    slots = lax.psum_scatter(plane, "zh", scatter_dimension=0, tiled=True)
+    slots = lax.all_to_all(slots.reshape(4, CAP, d_model), "x", 0, 0, tiled=True)
+    slots = slots.reshape(4 * CAP, d_model)
     sel_slots = sel.reshape(4, 2, CAP, n_tok)[:, 0].reshape(4 * CAP, n_tok)
     in_grad = dot_f32(sel_slots, slots, ((0,), (0,))).astype(jnp.bfloat16)
-    return in_grad, both[:, :ff_dev], both[:, ff_dev:].T
+
+    sum_in, sum_out = line_sums([(x_all, hid_grad_both), (g_all, hidden_both)], n_group)
+    width = d_model // n_group
+    here = lax.axis_index("group") * width
+    own_in = dot_f32(columns(x_all, here, width), hid_grad, ((0,), (0,)))
+    own_out = dot_f32(hidden, columns(g_all, here, width), ((0,), (0,)))
+    across = swap(jnp.concatenate([sum_in[:, ff_dev:], sum_out[:, ff_dev:]], axis=1), "core")
+    across = across.astype(jnp.float32)
+    w_in_grad = own_in + sum_in[:, :ff_dev].astype(jnp.float32) + across[:, :ff_dev]
+    sum_out = sum_out[:, :ff_dev].astype(jnp.float32) + across[:, ff_dev:]
+    w_out_grad = own_out + sum_out.T
+    return in_grad, w_in_grad.astype(jnp.bfloat16), w_out_grad.astype(jnp.bfloat16)
 
 
 def solution(mesh):

time: 352 us -> 454 us (1.29)
  the two profiles are of different devices: /device:TPU:2 before, /device:TPU:8 now
where the time goes in v2:
time: 454 us; the launch traced here: 451 us
  starting transfers between devices  236 us (52%)
  waiting for transfers between devices  108 us (24%)
  matrix products  74 us (16%)
  local copies, waits for them, and re-layouts  16.4 us (4%)
  between operations  14.6 us (3%)
    ppermute x30, starting transfers between devices, line_sums(): lax.ppermute(term.astype(jnp.bfloat16), ('group', 'core'), pairs)  105 us
    ppermute x6, starting transfers between devices, shift(): return lax.ppermute(value, 'y', [(i, (i + by) % 4) for i in range(4)])  89.7 us
    dot_general x43, matrix products, dot_f32(): lax.dot_general(a, b, (dims, ((), ())), preferred_element_type=jnp.float32)  74 us
    reduce_scatter x1, waiting for transfers between devices, shards(): slots = lax.psum_scatter(plane, 'zh', scatter_dimension=0, tiled=True)  48.9 us
    ppermute x5, waiting for transfers between devices, swap(): return lax.ppermute(value, axis, [(0, 1), (1, 0)])  45.4 us
    ppermute x5, starting transfers between devices, swap(): return lax.ppermute(value, axis, [(0, 1), (1, 0)])  32.2 us
    unnamed x41, local copies, waits for them, and re-layouts  10.6 us
  transfers between devices with their start and end apart: 45, of which 6 were waited for; matrix products, arithmetic and copies ran while one was open for 17% of the time, Pallas kernels for 0%

profile of v2, /device:TPU:8, one launch (start us, length us, event | category | flops | bytes accessed | tf_op | source)
XLA Modules:
  0.0 451.2 jit_solution(6814026056252111179)
XLA Ops:
  14.2 4.3 all-to-all-start
  19.2 5.3 %all-to-all-done = bf16[4,8,2048]{2,1,0:T(8,128)(2,1)S(1)} async-done(((bf16[4,8,2048]{2,1,0:T(8,128)(2,1)}), bf16[4,8,2048]{2,1,0:T(8,128)(2,1)S(1)}, u32[]{:S(2)}, u32[]{:S(2)}) %all-to-all-start) | async-done | bytes 131104 | tf_op jit(solution)/shard_map/all_to_all | solution.py:141
  24.7 32.0 %collective-permute-start = (bf16[32,2048]{1,0:T(8,128)(2,1)S(1)}, bf16[32,2048]{1,0:T(8,128)(2,1)S(1)}, u32[]{:S(2)}, u32[]{:S(2)}) collective-permute-start(bf16[32,2048]{1,0:T(8,128)(2,1)S(1)} %convolution_convert_fusion.2), channel_id=1, source_target_pairs={{0,6},{2,0},{4,2},{6,4},{1,7},{3,1},{5,3},{7,5},{8,14},{10,8},{12,... | collective-permute-start | bytes 393224 | tf_op jit(solution)/shard_map/ppermute | solution.py:34
  56.8 4.0 collective-permute-start.1
  60.8 9.7 %collective-permute-start.2 = (bf16[32,2048]{1,0:T(8,128)(2,1)S(1)}, bf16[32,2048]{1,0:T(8,128)(2,1)S(1)}, u32[]{:S(2)}, u32[]{:S(2)}) collective-permute-start(bf16[32,2048]{1,0:T(8,128)(2,1)S(1)} %convolution_convert_fusion.2), channel_id=1, source_target_pairs={{0,2},{2,4},{4,6},{6,0},{1,3},{3,5},{5,7},{7,1},{8,10},{10,12},{12... | collective-permute-start | bytes 393224 | tf_op jit(solution)/shard_map/ppermute | solution.py:34
  70.5 24.1 %collective-permute-start.4 = (bf16[32,2048]{1,0:T(8,128)(2,1)S(1)}, bf16[32,2048]{1,0:T(8,128)(2,1)S(1)}, u32[]{:S(2)}, u32[]{:S(2)}) collective-permute-start(bf16[32,2048]{1,0:T(8,128)(2,1)S(1)} %convolution_convert_fusion.2), channel_id=1, source_target_pairs={{0,8},{8,0},{1,9},{9,1},{2,10},{10,2},{3,11},{11,3},{4,12},{12,4},... | collective-permute-start | bytes 393224 | tf_op jit(solution)/shard_map/ppermute | solution.py:30
  95.3 45.4 %collective-permute-done.4 = bf16[32,2048]{1,0:T(8,128)(2,1)S(1)} collective-permute-done((bf16[32,2048]{1,0:T(8,128)(2,1)S(1)}, bf16[32,2048]{1,0:T(8,128)(2,1)S(1)}, u32[]{:S(2)}, u32[]{:S(2)}) %collective-permute-start.4) | collective-permute-done | bytes 131104 | tf_op jit(solution)/shard_map/ppermute | solution.py:30
  140.7 9.8 %collective-permute-start.5 = (bf16[32,2048]{1,0:T(8,128)(2,1)S(1)}, bf16[32,2048]{1,0:T(8,128)(2,1)S(1)}, u32[]{:S(2)}, u32[]{:S(2)}) collective-permute-start(bf16[32,2048]{1,0:T(8,128)(2,1)S(1)} %collective-permute-done.4), channel_id=1, source_target_pairs={{0,6},{2,0},{4,2},{6,4},{1,7},{3,1},{5,3},{7,5},{8,14},{10,8},{12,... | collective-permute-start | bytes 393224 | tf_op jit(solution)/shard_map/ppermute | solution.py:34
  150.5 30.8 %collective-permute-start.6 = (bf16[32,2048]{1,0:T(8,128)(2,1)S(1)}, bf16[32,2048]{1,0:T(8,128)(2,1)S(1)}, u32[]{:S(2)}, u32[]{:S(2)}) collective-permute-start(bf16[32,2048]{1,0:T(8,128)(2,1)S(1)} %collective-permute-done.4), channel_id=1, source_target_pairs={{0,4},{2,6},{4,0},{6,2},{1,5},{3,7},{5,1},{7,3},{8,12},{10,14},{12... | collective-permute-start | bytes 393224 | tf_op jit(solution)/shard_map/ppermute | solution.py:34
  181.2 3.4 collective-permute-start.7
  188.6 6.0 %collective-permute-done.7 = bf16[32,2048]{1,0:T(8,128)(2,1)S(1)} collective-permute-done((bf16[32,2048]{1,0:T(8,128)(2,1)S(1)}, bf16[32,2048]{1,0:T(8,128)(2,1)S(1)}, u32[]{:S(2)}, u32[]{:S(2)}) %collective-permute-start.7) | collective-permute-done | bytes 131104 | tf_op jit(solution)/shard_map/ppermute | solution.py:34
  206.2 2.4 collective-permute-start.9
  222.8 5.1 %collective-permute-start.26 = (bf16[128,1024]{1,0:T(8,128)(2,1)}, bf16[128,1024]{1,0:T(8,128)(2,1)}, u32[]{:S(2)}, u32[]{:S(2)}) collective-permute-start(bf16[128,1024]{1,0:T(8,128)(2,1)} %fusion.30), channel_id=1, source_target_pairs={{0,64},{64,128},{961,897},{897,833},{2,66},{66,130},{963,899},{899... | collective-permute-start | bytes 786440 | tf_op jit(solution)/shard_map/ppermute | solution.py:132
  234.1 4.6 %collective-permute-start.27 = (bf16[128,1024]{1,0:T(8,128)(2,1)}, bf16[128,1024]{1,0:T(8,128)(2,1)}, u32[]{:S(2)}, u32[]{:S(2)}) collective-permute-start(bf16[128,1024]{1,0:T(8,128)(2,1)} %fusion.29), channel_id=1, source_target_pairs={{0,64},{64,128},{128,192},{961,897},{897,833},{833,769},{2,66},{66... | collective-permute-start | bytes 786440 | tf_op jit(solution)/shard_map/ppermute | solution.py:132
  244.9 4.5 collective-permute-start.28
  255.5 4.5 collective-permute-start.29
  266.2 4.5 collective-permute-start.30
  276.8 4.5 collective-permute-start.31
  287.4 4.5 collective-permute-start.32
  294.0 2.9 collective-permute-start.17
  298.9 3.6 collective-permute-start.33
  304.6 4.1 collective-permute-start.18
  310.8 2.3 collective-permute-start.34
  315.2 5.4 %collective-permute-start.19 = (bf16[128,1024]{1,0:T(8,128)(2,1)}, bf16[128,1024]{1,0:T(8,128)(2,1)}, u32[]{:S(2)}, u32[]{:S(2)}) collective-permute-start(bf16[128,1024]{1,0:T(8,128)(2,1)} %fusion.8), channel_id=1, source_target_pairs={{0,64},{64,128},{128,192},{192,256},{256,320},{320,384},{384,448},... | collective-permute-start | bytes 786440 | tf_op jit(solution)/shard_map/ppermute | solution.py:132
  326.8 5.7 %collective-permute-start.20 = (bf16[128,1024]{1,0:T(8,128)(2,1)}, bf16[128,1024]{1,0:T(8,128)(2,1)}, u32[]{:S(2)}, u32[]{:S(2)}) collective-permute-start(bf16[128,1024]{1,0:T(8,128)(2,1)} %fusion.7), channel_id=1, source_target_pairs={{0,64},{64,128},{128,192},{192,256},{256,320},{320,384},{384,448},... | collective-permute-start | bytes 786440 | tf_op jit(solution)/shard_map/ppermute | solution.py:132
  338.7 5.6 %collective-permute-start.21 = (bf16[128,1024]{1,0:T(8,128)(2,1)}, bf16[128,1024]{1,0:T(8,128)(2,1)}, u32[]{:S(2)}, u32[]{:S(2)}) collective-permute-start(bf16[128,1024]{1,0:T(8,128)(2,1)} %fusion.6), channel_id=1, source_target_pairs={{0,64},{64,128},{128,192},{192,256},{256,320},{320,384},{384,448},... | collective-permute-start | bytes 786440 | tf_op jit(solution)/shard_map/ppermute | solution.py:132
  350.6 5.4 %collective-permute-start.22 = (bf16[128,1024]{1,0:T(8,128)(2,1)}, bf16[128,1024]{1,0:T(8,128)(2,1)}, u32[]{:S(2)}, u32[]{:S(2)}) collective-permute-start(bf16[128,1024]{1,0:T(8,128)(2,1)} %fusion.5), channel_id=1, source_target_pairs={{0,64},{64,128},{128,192},{192,256},{256,320},{320,384},{384,448},... | collective-permute-start | bytes 786440 | tf_op jit(solution)/shard_map/ppermute | solution.py:132
  362.3 5.6 %collective-permute-start.23 = (bf16[128,1024]{1,0:T(8,128)(2,1)}, bf16[128,1024]{1,0:T(8,128)(2,1)}, u32[]{:S(2)}, u32[]{:S(2)}) collective-permute-start(bf16[128,1024]{1,0:T(8,128)(2,1)} %fusion.4), channel_id=1, source_target_pairs={{0,64},{64,128},{128,192},{192,256},{256,320},{320,384},{384,448},... | collective-permute-start | bytes 786440 | tf_op jit(solution)/shard_map/ppermute | solution.py:132
  370.0 2.1 collective-permute-start.39
  373.5 5.6 %collective-permute-start.24 = (bf16[128,1024]{1,0:T(8,128)(2,1)S(1)}, bf16[128,1024]{1,0:T(8,128)(2,1)}, u32[]{:S(2)}, u32[]{:S(2)}) collective-permute-start(bf16[128,1024]{1,0:T(8,128)(2,1)S(1)} %fusion.3), channel_id=1, source_target_pairs={{0,64},{64,128},{128,192},{192,256},{256,320},{320,384},{384,448},... | collective-permute-start | bytes 786440 | tf_op jit(solution)/shard_map/ppermute | solution.py:132
  379.1 48.9 %reduce-scatter.5.cloned.1.call-done = bf16[16,2048]{1,0:T(8,128)(2,1)} async-done(((bf16[32,2048]{1,0:T(8,128)(2,1)}), bf16[16,2048]{1,0:T(8,128)(2,1)}) %reduce-scatter.5.cloned.1.call-update) | async-done | bytes 65552 | tf_op jit(solution)/shard_map/reduce_scatter | solution.py:160
  429.5 4.3 all-to-all-start.1
  (193 shorter events, 125.8 us)
Async XLA Ops:
  14.2 10.3 %all-to-all-start = ((bf16[4,8,2048]{2,1,0:T(8,128)(2,1)}), bf16[4,8,2048]{2,1,0:T(8,128)(2,1)S(1)}, u32[]{:S(2)}, u32[]{:S(2)}) async-start(bf16[4,8,2048]{2,1,0:T(8,128)(2,1)} %fusion.2), calls=%async_computation | async-start | bytes 262144 | tf_op jit(solution)/shard_map/all_to_all | solution.py:141
  18.5 349.4 %reduce-scatter.3.cloned.1.call-start = ((), (), s32[]{:S(2)}) async-start(), calls=%async_computation.4 | async-start | bytes 1179648 | tf_op jit(solution)/shard_map/reduce_scatter | solution.py:159
  24.7 156.5 %collective-permute-start = (bf16[32,2048]{1,0:T(8,128)(2,1)S(1)}, bf16[32,2048]{1,0:T(8,128)(2,1)S(1)}, u32[]{:S(2)}, u32[]{:S(2)}) collective-permute-start(bf16[32,2048]{1,0:T(8,128)(2,1)S(1)} %convolution_convert_fusion.2), channel_id=1, source_target_pairs={{0,6},{2,0},{4,2},{6,4},{1,7},{3,1},{5,3},{7,5},{8,14},{10,8},{12,... | collective-permute-start | bytes 393224 | tf_op jit(solution)/shard_map/ppermute | solution.py:34
  56.8 127.9 %collective-permute-start.1 = (bf16[32,2048]{1,0:T(8,128)(2,1)S(1)}, bf16[32,2048]{1,0:T(8,128)(2,1)S(1)}, u32[]{:S(2)}, u32[]{:S(2)}) collective-permute-start(bf16[32,2048]{1,0:T(8,128)(2,1)S(1)} %convolution_convert_fusion.2), channel_id=1, source_target_pairs={{0,4},{2,6},{4,0},{6,2},{1,5},{3,7},{5,1},{7,3},{8,12},{10,14},{12... | collective-permute-start | bytes 393224 | tf_op jit(solution)/shard_map/ppermute | solution.py:34
  60.8 123.8 %collective-permute-start.2 = (bf16[32,2048]{1,0:T(8,128)(2,1)S(1)}, bf16[32,2048]{1,0:T(8,128)(2,1)S(1)}, u32[]{:S(2)}, u32[]{:S(2)}) collective-permute-start(bf16[32,2048]{1,0:T(8,128)(2,1)S(1)} %convolution_convert_fusion.2), channel_id=1, source_target_pairs={{0,2},{2,4},{4,6},{6,0},{1,3},{3,5},{5,7},{7,1},{8,10},{10,12},{12... | collective-permute-start | bytes 393224 | tf_op jit(solution)/shard_map/ppermute | solution.py:34
  70.5 70.1 %collective-permute-start.4 = (bf16[32,2048]{1,0:T(8,128)(2,1)S(1)}, bf16[32,2048]{1,0:T(8,128)(2,1)S(1)}, u32[]{:S(2)}, u32[]{:S(2)}) collective-permute-start(bf16[32,2048]{1,0:T(8,128)(2,1)S(1)} %convolution_convert_fusion.2), channel_id=1, source_target_pairs={{0,8},{8,0},{1,9},{9,1},{2,10},{10,2},{3,11},{11,3},{4,12},{12,4},... | collective-permute-start | bytes 393224 | tf_op jit(solution)/shard_map/ppermute | solution.py:30
  140.7 47.9 %collective-permute-start.5 = (bf16[32,2048]{1,0:T(8,128)(2,1)S(1)}, bf16[32,2048]{1,0:T(8,128)(2,1)S(1)}, u32[]{:S(2)}, u32[]{:S(2)}) collective-permute-start(bf16[32,2048]{1,0:T(8,128)(2,1)S(1)} %collective-permute-done.4), channel_id=1, source_target_pairs={{0,6},{2,0},{4,2},{6,4},{1,7},{3,1},{5,3},{7,5},{8,14},{10,8},{12,... | collective-permute-start | bytes 393224 | tf_op jit(solution)/shard_map/ppermute | solution.py:34
  150.5 38.1 %collective-permute-start.6 = (bf16[32,2048]{1,0:T(8,128)(2,1)S(1)}, bf16[32,2048]{1,0:T(8,128)(2,1)S(1)}, u32[]{:S(2)}, u32[]{:S(2)}) collective-permute-start(bf16[32,2048]{1,0:T(8,128)(2,1)S(1)} %collective-permute-done.4), channel_id=1, source_target_pairs={{0,4},{2,6},{4,0},{6,2},{1,5},{3,7},{5,1},{7,3},{8,12},{10,14},{12... | collective-permute-start | bytes 393224 | tf_op jit(solution)/shard_map/ppermute | solution.py:34
  181.2 13.3 %collective-permute-start.7 = (bf16[32,2048]{1,0:T(8,128)(2,1)S(1)}, bf16[32,2048]{1,0:T(8,128)(2,1)S(1)}, u32[]{:S(2)}, u32[]{:S(2)}) collective-permute-start(bf16[32,2048]{1,0:T(8,128)(2,1)S(1)} %collective-permute-done.4), channel_id=1, source_target_pairs={{0,2},{2,4},{4,6},{6,0},{1,3},{3,5},{5,7},{7,1},{8,10},{10,12},{12... | collective-permute-start | bytes 393224 | tf_op jit(solution)/shard_map/ppermute | solution.py:34
  184.7 11.9 %collective-permute-start.3 = (bf16[128,2048]{1,0:T(8,128)(2,1)S(1)}, bf16[128,2048]{1,0:T(8,128)(2,1)S(1)}, u32[]{:S(2)}, u32[]{:S(2)}) collective-permute-start(bf16[128,2048]{1,0:T(8,128)(2,1)S(1)} %pad_maximum_fusion), channel_id=1, source_target_pairs={{0,1},{1,0},{2,3},{3,2},{4,5},{5,4},{6,7},{7,6},{8,9},{9,8},{10,11... | collective-permute-start | bytes 1572872 | tf_op jit(solution)/shard_map/ppermute | solution.py:30
  218.3 9.5 %collective-permute-start.10 = (bf16[128,1024]{1,0:T(8,128)(2,1)S(1)}, bf16[128,1024]{1,0:T(8,128)(2,1)}, u32[]{:S(2)}, u32[]{:S(2)}) collective-permute-start(bf16[128,1024]{1,0:T(8,128)(2,1)S(1)} %convolution_convert_fusion.5), channel_id=1, source_target_pairs={{0,64},{961,897},{2,66},{963,899},{4,68},{965,901},{6,70},{967,903... | collective-permute-start | bytes 786440 | tf_op jit(solution)/shard_map/ppermute | solution.py:132
  222.8 9.1 %collective-permute-start.26 = (bf16[128,1024]{1,0:T(8,128)(2,1)}, bf16[128,1024]{1,0:T(8,128)(2,1)}, u32[]{:S(2)}, u32[]{:S(2)}) collective-permute-start(bf16[128,1024]{1,0:T(8,128)(2,1)} %fusion.30), channel_id=1, source_target_pairs={{0,64},{64,128},{961,897},{897,833},{2,66},{66,130},{963,899},{899... | collective-permute-start | bytes 786440 | tf_op jit(solution)/shard_map/ppermute | solution.py:132
  229.9 8.8 %collective-permute-start.11 = (bf16[128,1024]{1,0:T(8,128)(2,1)}, bf16[128,1024]{1,0:T(8,128)(2,1)}, u32[]{:S(2)}, u32[]{:S(2)}) collective-permute-start(bf16[128,1024]{1,0:T(8,128)(2,1)} %fusion.16), channel_id=1, source_target_pairs={{0,64},{64,128},{961,897},{897,833},{2,66},{66,130},{963,899},{899... | collective-permute-start | bytes 786440 | tf_op jit(solution)/shard_map/ppermute | solution.py:132
  234.1 8.7 %collective-permute-start.27 = (bf16[128,1024]{1,0:T(8,128)(2,1)}, bf16[128,1024]{1,0:T(8,128)(2,1)}, u32[]{:S(2)}, u32[]{:S(2)}) collective-permute-start(bf16[128,1024]{1,0:T(8,128)(2,1)} %fusion.29), channel_id=1, source_target_pairs={{0,64},{64,128},{128,192},{961,897},{897,833},{833,769},{2,66},{66... | collective-permute-start | bytes 786440 | tf_op jit(solution)/shard_map/ppermute | solution.py:132
  240.8 8.6 %collective-permute-start.12 = (bf16[128,1024]{1,0:T(8,128)(2,1)}, bf16[128,1024]{1,0:T(8,128)(2,1)}, u32[]{:S(2)}, u32[]{:S(2)}) collective-permute-start(bf16[128,1024]{1,0:T(8,128)(2,1)} %fusion.15), channel_id=1, source_target_pairs={{0,64},{64,128},{128,192},{961,897},{897,833},{833,769},{2,66},{66... | collective-permute-start | bytes 786440 | tf_op jit(solution)/shard_map/ppermute | solution.py:132
  276.8 8.6 %collective-permute-start.31 = (bf16[128,1024]{1,0:T(8,128)(2,1)}, bf16[128,1024]{1,0:T(8,128)(2,1)}, u32[]{:S(2)}, u32[]{:S(2)}) collective-permute-start(bf16[128,1024]{1,0:T(8,128)(2,1)} %fusion.25), channel_id=1, source_target_pairs={{0,64},{64,128},{128,192},{192,256},{256,320},{320,384},{384,448},... | collective-permute-start | bytes 786440 | tf_op jit(solution)/shard_map/ppermute | solution.py:132
  287.4 9.4 %collective-permute-start.32 = (bf16[128,1024]{1,0:T(8,128)(2,1)}, bf16[128,1024]{1,0:T(8,128)(2,1)}, u32[]{:S(2)}, u32[]{:S(2)}) collective-permute-start(bf16[128,1024]{1,0:T(8,128)(2,1)} %fusion.24), channel_id=1, source_target_pairs={{0,64},{64,128},{128,192},{192,256},{256,320},{320,384},{384,448},... | collective-permute-start | bytes 786440 | tf_op jit(solution)/shard_map/ppermute | solution.py:132
  298.9 9.9 %collective-permute-start.33 = (bf16[128,1024]{1,0:T(8,128)(2,1)}, bf16[128,1024]{1,0:T(8,128)(2,1)}, u32[]{:S(2)}, u32[]{:S(2)}) collective-permute-start(bf16[128,1024]{1,0:T(8,128)(2,1)} %fusion.23), channel_id=1, source_target_pairs={{0,64},{64,128},{128,192},{192,256},{256,320},{320,384},{384,448},... | collective-permute-start | bytes 786440 | tf_op jit(solution)/shard_map/ppermute | solution.py:132
  308.7 119.3 %reduce-scatter.5.cloned.1.call-start = ((), (), s32[]{:S(2)}) async-start(), calls=%async_computation.5 | async-start | bytes 196608 | tf_op jit(solution)/shard_map/reduce_scatter | solution.py:160
  310.8 9.8 %collective-permute-start.34 = (bf16[128,1024]{1,0:T(8,128)(2,1)}, bf16[128,1024]{1,0:T(8,128)(2,1)}, u32[]{:S(2)}, u32[]{:S(2)}) collective-permute-start(bf16[128,1024]{1,0:T(8,128)(2,1)} %fusion.22), channel_id=1, source_target_pairs={{0,64},{64,128},{128,192},{192,256},{256,320},{320,384},{384,448},... | collective-permute-start | bytes 786440 | tf_op jit(solution)/shard_map/ppermute | solution.py:132
  315.2 9.5 %collective-permute-start.19 = (bf16[128,1024]{1,0:T(8,128)(2,1)}, bf16[128,1024]{1,0:T(8,128)(2,1)}, u32[]{:S(2)}, u32[]{:S(2)}) collective-permute-start(bf16[128,1024]{1,0:T(8,128)(2,1)} %fusion.8), channel_id=1, source_target_pairs={{0,64},{64,128},{128,192},{192,256},{256,320},{320,384},{384,448},... | collective-permute-start | bytes 786440 | tf_op jit(solution)/shard_map/ppermute | solution.py:132
  322.6 9.9 %collective-permute-start.35 = (bf16[128,1024]{1,0:T(8,128)(2,1)}, bf16[128,1024]{1,0:T(8,128)(2,1)}, u32[]{:S(2)}, u32[]{:S(2)}) collective-permute-start(bf16[128,1024]{1,0:T(8,128)(2,1)} %fusion.21), channel_id=1, source_target_pairs={{0,64},{64,128},{128,192},{192,256},{256,320},{320,384},{384,448},... | collective-permute-start | bytes 786440 | tf_op jit(solution)/shard_map/ppermute | solution.py:132
  326.8 9.9 %collective-permute-start.20 = (bf16[128,1024]{1,0:T(8,128)(2,1)}, bf16[128,1024]{1,0:T(8,128)(2,1)}, u32[]{:S(2)}, u32[]{:S(2)}) collective-permute-start(bf16[128,1024]{1,0:T(8,128)(2,1)} %fusion.7), channel_id=1, source_target_pairs={{0,64},{64,128},{128,192},{192,256},{256,320},{320,384},{384,448},... | collective-permute-start | bytes 786440 | tf_op jit(solution)/shard_map/ppermute | solution.py:132
  334.6 9.8 %collective-permute-start.36 = (bf16[128,1024]{1,0:T(8,128)(2,1)}, bf16[128,1024]{1,0:T(8,128)(2,1)}, u32[]{:S(2)}, u32[]{:S(2)}) collective-permute-start(bf16[128,1024]{1,0:T(8,128)(2,1)} %fusion.20), channel_id=1, source_target_pairs={{0,64},{64,128},{128,192},{192,256},{256,320},{320,384},{384,448},... | collective-permute-start | bytes 786440 | tf_op jit(solution)/shard_map/ppermute | solution.py:132
  338.7 9.8 %collective-permute-start.21 = (bf16[128,1024]{1,0:T(8,128)(2,1)}, bf16[128,1024]{1,0:T(8,128)(2,1)}, u32[]{:S(2)}, u32[]{:S(2)}) collective-permute-start(bf16[128,1024]{1,0:T(8,128)(2,1)} %fusion.6), channel_id=1, source_target_pairs={{0,64},{64,128},{128,192},{192,256},{256,320},{320,384},{384,448},... | collective-permute-start | bytes 786440 | tf_op jit(solution)/shard_map/ppermute | solution.py:132
  346.4 9.6 %collective-permute-start.37 = (bf16[128,1024]{1,0:T(8,128)(2,1)}, bf16[128,1024]{1,0:T(8,128)(2,1)}, u32[]{:S(2)}, u32[]{:S(2)}) collective-permute-start(bf16[128,1024]{1,0:T(8,128)(2,1)} %fusion.19), channel_id=1, source_target_pairs={{0,64},{64,128},{128,192},{192,256},{256,320},{320,384},{384,448},... | collective-permute-start | bytes 786440 | tf_op jit(solution)/shard_map/ppermute | solution.py:132
  350.6 9.6 %collective-permute-start.22 = (bf16[128,1024]{1,0:T(8,128)(2,1)}, bf16[128,1024]{1,0:T(8,128)(2,1)}, u32[]{:S(2)}, u32[]{:S(2)}) collective-permute-start(bf16[128,1024]{1,0:T(8,128)(2,1)} %fusion.5), channel_id=1, source_target_pairs={{0,64},{64,128},{128,192},{192,256},{256,320},{320,384},{384,448},... | collective-permute-start | bytes 786440 | tf_op jit(solution)/shard_map/ppermute | solution.py:132
  358.1 9.8 %collective-permute-start.38 = (bf16[128,1024]{1,0:T(8,128)(2,1)}, bf16[128,1024]{1,0:T(8,128)(2,1)}, u32[]{:S(2)}, u32[]{:S(2)}) collective-permute-start(bf16[128,1024]{1,0:T(8,128)(2,1)} %fusion.18), channel_id=1, source_target_pairs={{0,64},{64,128},{128,192},{192,256},{256,320},{320,384},{384,448},... | collective-permute-start | bytes 786440 | tf_op jit(solution)/shard_map/ppermute | solution.py:132
  362.3 9.8 %collective-permute-start.23 = (bf16[128,1024]{1,0:T(8,128)(2,1)}, bf16[128,1024]{1,0:T(8,128)(2,1)}, u32[]{:S(2)}, u32[]{:S(2)}) collective-permute-start(bf16[128,1024]{1,0:T(8,128)(2,1)} %fusion.4), channel_id=1, source_target_pairs={{0,64},{64,128},{128,192},{192,256},{256,320},{320,384},{384,448},... | collective-permute-start | bytes 786440 | tf_op jit(solution)/shard_map/ppermute | solution.py:132
  370.0 63.8 %collective-permute-start.39 = (bf16[128,1024]{1,0:T(8,128)(2,1)}, bf16[128,1024]{1,0:T(8,128)(2,1)}, u32[]{:S(2)}, u32[]{:S(2)}) collective-permute-start(bf16[128,1024]{1,0:T(8,128)(2,1)} %fusion.17), channel_id=1, source_target_pairs={{0,64},{64,128},{128,192},{192,256},{256,320},{320,384},{384,448},... | collective-permute-start | bytes 786440 | tf_op jit(solution)/shard_map/ppermute | solution.py:132
  373.5 61.2 %collective-permute-start.24 = (bf16[128,1024]{1,0:T(8,128)(2,1)S(1)}, bf16[128,1024]{1,0:T(8,128)(2,1)}, u32[]{:S(2)}, u32[]{:S(2)}) collective-permute-start(bf16[128,1024]{1,0:T(8,128)(2,1)S(1)} %fusion.3), channel_id=1, source_target_pairs={{0,64},{64,128},{128,192},{192,256},{256,320},{320,384},{384,448},... | collective-permute-start | bytes 786440 | tf_op jit(solution)/shard_map/ppermute | solution.py:132
  429.5 9.9 %all-to-all-start.1 = ((bf16[4,4,2048]{2,1,0:T(4,128)(2,1)}), bf16[4,4,2048]{2,1,0:T(4,128)(2,1)S(1)}, u32[]{:S(2)}, u32[]{:S(2)}) async-start(bf16[4,4,2048]{2,1,0:T(4,128)(2,1)} %reshape.202), calls=%async_computation.3 | async-start | bytes 131072 | tf_op jit(solution)/shard_map/all_to_all | solution.py:161
  (23 other events, 339.7 us)
Sparse Core Ops, SparseCore 0:
  308.8 46.7 reduce-scatter.2
  368.0 59.9 reduce-scatter.4

commit v3 on v1

--- a/solution.py
+++ b/solution.py
@@ -66,60 +66,111 @@
 
 
 def gather_plane(rows):
-    pieces = [rows] + [shift(rows, by) for by in (1, 3, 2)]
-    own = jnp.concatenate(pieces, axis=1)
-    both = jnp.concatenate([own, swap(own, "core")], axis=1)
-    return both[0], both[1]
+    pieces = [rows, shift(rows, 3), shift(rows, 2), shift(rows, 1)]
+    own = jnp.concatenate(pieces, axis=0)
+    return jnp.concatenate([own, swap(own, "core")], axis=0)
 
 
-def return_plane(partial):
-    half = partial.shape[0] // 2
-    core_sum = partial[:half].astype(jnp.float32) + swap(partial[half:], "core").astype(jnp.float32)
-    core_sum = core_sum.astype(jnp.bfloat16).reshape(4, half // 4, -1)
-    total = core_sum[0].astype(jnp.float32)
-    for k, by in ((1, 3), (2, 1), (3, 2)):
-        total = total + shift(core_sum[k], by).astype(jnp.float32)
-    return total
+def row_order(n_rows, kind):
+    to = lax.broadcasted_iota(jnp.int32, (n_rows, 2 * n_rows), 0)
+    at = lax.broadcasted_iota(jnp.int32, (n_rows, 2 * n_rows), 1)
+    core = (to // 128 - lax.axis_index("core")) & 1
+    source = core * 256 + ((to & 127) // CAP) * (2 * CAP) + kind * CAP + (to & (CAP - 1))
+    return (at == source).astype(jnp.bfloat16)
 
 
 def expert_part(x_rows, g_rows, w_in, w_out):
     pre_act = dot_f32(x_rows, w_in, ((1,), (0,)))
     value, slope = gelu_pair(pre_act)
     back_hid = dot_f32(g_rows, w_out, ((1,), (1,)))
-    hid_grad = (back_hid * slope).astype(jnp.bfloat16)
-    partial = dot_f32(hid_grad, w_in, ((1,), (1,))).astype(jnp.bfloat16)
-    return value.astype(jnp.bfloat16), hid_grad, partial
+    return value.astype(jnp.bfloat16), (back_hid * slope).astype(jnp.bfloat16)
+
+
+def block_of(rows, begin, height):
+    return lax.dynamic_slice(
+        rows, (begin, 0), (height, rows.shape[1]), allow_negative_indices=False
+    )
+
+
+def line_sums(streams, n_group, beside, ties):
+    height = streams[0].shape[0] // n_group
+    top = (n_group - 1) * height
+    here, core = lax.axis_index("group"), lax.axis_index("core")
+    rank = jnp.where(core == 0, here, n_group - 1 - here)
+    towards = height * (1 - 2 * core)
+    pairs = [(2 * i, 2 * i + 2) for i in range(n_group - 1)]
+    pairs += [(2 * i + 3, 2 * i + 1) for i in range(n_group - 1)]
+    carried = [None] * len(streams)
+    for step in range(n_group - 1):
+        begin = lax.clamp(0, here * height + (n_group - 1 - step) * towards, top)
+        for k, rows in enumerate(streams):
+            term = block_of(rows, begin, height)
+            if step:
+                arrived = jnp.where(rank <= step, carried[k].astype(jnp.float32), 0.0)
+                term = (term.astype(jnp.float32) + arrived).astype(jnp.bfloat16)
+            carried[k] = lax.ppermute(term, ("group", "core"), pairs)
+        if step in ties:
+            beside, carried[0] = lax.optimization_barrier((beside, carried[0]))
+            beside = ties[step](beside)
+    return carried, beside
 
 
 def shards(inputs, out_grad, routes, router_weight, w_in, w_out):
-    d_model = inputs.shape[1]
+    n_tok, d_model = inputs.shape
     ff_dev = w_in.shape[1]
+    n_group = lax.axis_size("group")
     send, sel = slot_rows(inputs, out_grad, routes, router_weight)
     got = lax.all_to_all(send.reshape(4, 2 * CAP, d_model), "x", 0, 0, tiled=True)
-    near = got.reshape(4, 2, CAP, d_model).transpose(1, 0, 2, 3).reshape(2, 4 * CAP, d_model)
-    far = swap(near, "zh")
-    x_near, g_near = gather_plane(near)
-    hidden_near, hid_grad_near, partial_near = expert_part(x_near, g_near, w_in, w_out)
-    x_far, g_far = gather_plane(far)
-    hidden_far, hid_grad_far, partial_far = expert_part(x_far, g_far, w_in, w_out)
-    x_all = jnp.concatenate([x_near, x_far], axis=0)
-    g_all = jnp.concatenate([g_near, g_far], axis=0)
-    hidden = jnp.concatenate([hidden_near, hidden_far], axis=0)
-    hid_grad = jnp.concatenate([hid_grad_near, hid_grad_far], axis=0)
-    grad_in = dot_f32(x_all, hid_grad, ((0,), (0,))).astype(jnp.bfloat16)
-    grad_out = dot_f32(g_all, hidden, ((0,), (0,))).astype(jnp.bfloat16)
-    both = lax.psum_scatter(
-        jnp.concatenate([grad_in, grad_out], axis=1), "group", scatter_dimension=0, tiled=True
+    got = got.reshape(8 * CAP, d_model)
+    far, order_x, order_g = lax.optimization_barrier(
+        (swap(got, "zh"), row_order(64 * CAP, 0), row_order(64 * CAP, 1))
     )
-    back_far = return_plane(partial_far).astype(jnp.bfloat16)
-    slots = return_plane(partial_near) + swap(back_far, "zh").astype(jnp.float32)
-    slots = lax.all_to_all(
-        slots.astype(jnp.bfloat16).reshape(4, CAP, d_model), "x", 0, 0, tiled=True
-    ).reshape(4 * CAP, d_model)
-    n_tok = inputs.shape[0]
+    rows = gather_plane(jnp.concatenate([got, far], axis=0))
+    x_all = dot_f32(order_x, rows, ((1,), (0,))).astype(jnp.bfloat16)
+    g_all = dot_f32(order_g, rows, ((1,), (0,))).astype(jnp.bfloat16)
+    hidden, hid_grad = expert_part(x_all, g_all, w_in, w_out)
+    other = swap(jnp.concatenate([hid_grad, hidden], axis=1), "core")
+    partial = dot_f32(hid_grad, w_in, ((1,), (1,))).astype(jnp.bfloat16)
+    hid_grad_both = jnp.concatenate([hid_grad, other[:, :ff_dev]], axis=1)
+    hidden_both = jnp.concatenate([hidden, other[:, ff_dev:]], axis=1)
+    hid_grad_both, partial = lax.optimization_barrier((hid_grad_both, partial))
+    grad_in = dot_f32(x_all, hid_grad_both, ((0,), (0,))).astype(jnp.bfloat16)
+    grad_out = dot_f32(g_all, hidden_both, ((0,), (0,))).astype(jnp.bfloat16)
+
+    def along_y(rows):
+        parts = rows.reshape(4, -1, d_model)
+        total = parts[0].astype(jnp.float32)
+        for by in (1, 3, 2):
+            total = total + shift(parts[by], by).astype(jnp.float32)
+        return total.astype(jnp.bfloat16)
+
+    def across_zh(rows):
+        half = rows.shape[0] // 2
+        total = rows[:half].astype(jnp.float32) + swap(rows[half:], "zh").astype(jnp.float32)
+        return total.astype(jnp.bfloat16)
+
+    def along_x(rows):
+        parts = rows.reshape(4, CAP, d_model)
+        return lax.all_to_all(parts, "x", 0, 0, tiled=True).reshape(4 * CAP, d_model)
+
+    core, half = lax.axis_index("core"), partial.shape[0] // 2
+    given = swap(block_of(partial, (1 - core) * half, half), "core").astype(jnp.float32)
+    given = (block_of(partial, core * half, half).astype(jnp.float32) + given).astype(jnp.bfloat16)
+    (sum_in, sum_out), slots = line_sums(
+        [grad_in, grad_out], n_group, given, {0: along_y, 3: across_zh, 9: along_x}
+    )
     sel_slots = sel.reshape(4, 2, CAP, n_tok)[:, 0].reshape(4 * CAP, n_tok)
     in_grad = dot_f32(sel_slots, slots, ((0,), (0,))).astype(jnp.bfloat16)
-    return in_grad, both[:, :ff_dev], both[:, ff_dev:].T
+
+    width = d_model // n_group
+    here = lax.axis_index("group") * width
+    own_in = block_of(grad_in, here, width)[:, :ff_dev].astype(jnp.float32)
+    own_out = block_of(grad_out, here, width)[:, :ff_dev].astype(jnp.float32)
+    across = swap(jnp.concatenate([sum_in[:, ff_dev:], sum_out[:, ff_dev:]], axis=1), "core")
+    across = across.astype(jnp.float32)
+    w_in_grad = own_in + sum_in[:, :ff_dev].astype(jnp.float32) + across[:, :ff_dev]
+    w_out_grad = own_out + sum_out[:, :ff_dev].astype(jnp.float32) + across[:, ff_dev:]
+    return in_grad, w_in_grad.astype(jnp.bfloat16), w_out_grad.astype(jnp.bfloat16).T
 
 
 def solution(mesh):

time: 352 us -> 299 us (0.85)
  the two profiles are of different devices: /device:TPU:2 before, /device:TPU:64 now
where the time goes in v3:
time: 299 us; the launch traced here: 296 us
  starting transfers between devices  200 us (67%)
  waiting for transfers between devices  44.9 us (15%)
  other arithmetic  32.9 us (11%)
  matrix products  12.4 us (4%)
  local copies, waits for them, and re-layouts  4.27 us (1%)
    ppermute x30, starting transfers between devices, line_sums(): carried[k] = lax.ppermute(term, ('group', 'core'), pairs)  117 us
    ppermute x6, starting transfers between devices, swap(): return lax.ppermute(value, axis, [(0, 1), (1, 0)])  54.2 us
    convert_element_type x28, other arithmetic, line_sums(): term = (term.astype(jnp.float32) + arrived).astype(jnp.bfloat16)  28.5 us
    ppermute x6, starting transfers between devices, shift(): return lax.ppermute(value, 'y', [(i, (i + by) % 4) for i in range(4)])  21.2 us
    ppermute x30, waiting for transfers between devices, line_sums(): carried[k] = lax.ppermute(term, ('group', 'core'), pairs)  18.9 us
    dot_general x12, matrix products, dot_f32(): lax.dot_general(a, b, (dims, ((), ())), preferred_element_type=jnp.float32)  12.4 us
    ppermute x6, waiting for transfers between devices, shift(): return lax.ppermute(value, 'y', [(i, (i + by) % 4) for i in range(4)])  8.75 us
    ppermute x6, waiting for transfers between devices, swap(): return lax.ppermute(value, axis, [(0, 1), (1, 0)])  7.76 us
  transfers between devices with their start and end apart: 44, of which 14 were waited for; matrix products, arithmetic and copies ran while one was open for 12% of the time, Pallas kernels for 0%

profile of v3, /device:TPU:64, one launch (start us, length us, event | category | flops | bytes accessed | tf_op | source)
XLA Modules:
  0.0 296.2 jit_solution(4193916211679116649)
XLA Ops:
  7.7 4.3 %all-to-all-start = ((bf16[4,8,2048]{2,1,0:T(8,128)(2,1)}), bf16[4,8,2048]{2,1,0:T(8,128)(2,1)S(1)}, u32[]{:S(2)}, u32[]{:S(2)}) async-start(bf16[4,8,2048]{2,1,0:T(8,128)(2,1)} %fusion.2), calls=%async_computation | async-start | bytes 262144 | tf_op jit(solution)/shard_map/all_to_all | solution.py:123
  12.0 5.9 %all-to-all-done = bf16[4,8,2048]{2,1,0:T(8,128)(2,1)S(1)} async-done(((bf16[4,8,2048]{2,1,0:T(8,128)(2,1)}), bf16[4,8,2048]{2,1,0:T(8,128)(2,1)S(1)}, u32[]{:S(2)}, u32[]{:S(2)}) %all-to-all-start) | async-done | bytes 131104 | tf_op jit(solution)/shard_map/all_to_all | solution.py:123
  17.9 27.2 %collective-permute-start = (bf16[32,2048]{1,0:T(8,128)(2,1)S(1)}, bf16[32,2048]{1,0:T(8,128)(2,1)S(1)}, u32[]{:S(2)}, u32[]{:S(2)}) collective-permute-start(bf16[32,2048]{1,0:T(8,128)(2,1)S(1)} %bitcast.47), channel_id=1, source_target_pairs={{0,8},{8,0},{1,9},{9,1},{2,10},{10,2},{3,11},{11,3},{4,12},{12,4},... | collective-permute-start | bytes 393224 | tf_op jit(solution)/shard_map/ppermute | solution.py:30
  45.4 3.8 %collective-permute-done = bf16[32,2048]{1,0:T(8,128)(2,1)S(1)} collective-permute-done((bf16[32,2048]{1,0:T(8,128)(2,1)S(1)}, bf16[32,2048]{1,0:T(8,128)(2,1)S(1)}, u32[]{:S(2)}, u32[]{:S(2)}) %collective-permute-start) | collective-permute-done | bytes 131104 | tf_op jit(solution)/shard_map/ppermute | solution.py:30
  49.3 6.2 %collective-permute-start.1 = (bf16[64,2048]{1,0:T(8,128)(2,1)S(1)}, bf16[64,2048]{1,0:T(8,128)(2,1)S(1)}, u32[]{:S(2)}, u32[]{:S(2)}) collective-permute-start(bf16[64,2048]{1,0:T(8,128)(2,1)S(1)} %pad_maximum_fusion.2), channel_id=1, source_target_pairs={{0,6},{2,0},{4,2},{6,4},{1,7},{3,1},{5,3},{7,5},{8,14},{10,8},{12,... | collective-permute-start | bytes 786440 | tf_op jit(solution)/shard_map/ppermute | solution.py:34
  61.0 3.6 %collective-permute-done.1 = bf16[64,2048]{1,0:T(8,128)(2,1)S(1)} collective-permute-done((bf16[64,2048]{1,0:T(8,128)(2,1)S(1)}, bf16[64,2048]{1,0:T(8,128)(2,1)S(1)}, u32[]{:S(2)}, u32[]{:S(2)}) %collective-permute-start.1) | collective-permute-done | bytes 262176 | tf_op jit(solution)/shard_map/ppermute | solution.py:34
  87.5 10.9 %collective-permute-start.26 = (bf16[128,1024]{1,0:T(8,128)(2,1)S(1)}, bf16[128,1024]{1,0:T(8,128)(2,1)S(1)}, u32[]{:S(2)}, u32[]{:S(2)}) collective-permute-start(bf16[128,1024]{1,0:T(8,128)(2,1)S(1)} %constant_dynamic-slice_fusion), channel_id=1, source_target_pairs={{0,64},{64,128},{128,192},{192,256},{256,320},{320,384},{384,448},... | collective-permute-start | bytes 786440 | tf_op jit(solution)/shard_map/ppermute | solution.py:111
  101.7 10.2 %collective-permute-done.26 = bf16[128,1024]{1,0:T(8,128)(2,1)S(1)} collective-permute-done((bf16[128,1024]{1,0:T(8,128)(2,1)S(1)}, bf16[128,1024]{1,0:T(8,128)(2,1)S(1)}, u32[]{:S(2)}, u32[]{:S(2)}) %collective-permute-start.26) | collective-permute-done | bytes 262176 | tf_op jit(solution)/shard_map/ppermute | solution.py:111
  132.1 4.3 %collective-permute-start.9 = (bf16[32,2048]{1,0:T(8,128)(2,1)S(1)}, bf16[32,2048]{1,0:T(8,128)(2,1)S(1)}, u32[]{:S(2)}, u32[]{:S(2)}) collective-permute-start(bf16[32,2048]{1,0:T(8,128)(2,1)S(1)} %get-tuple-element.41), channel_id=1, source_target_pairs={{0,6},{2,0},{4,2},{6,4},{1,7},{3,1},{5,3},{7,5},{8,14},{10,8},{12,... | collective-permute-start | bytes 393224 | tf_op jit(solution)/shard_map/ppermute | solution.py:34
  137.5 3.1 %collective-permute-start.29 = (bf16[128,1024]{1,0:T(8,128)(2,1)S(1)}, bf16[128,1024]{1,0:T(8,128)(2,1)S(1)}, u32[]{:S(2)}, u32[]{:S(2)}) collective-permute-start(bf16[128,1024]{1,0:T(8,128)(2,1)S(1)} %add_convert_fusion.12), channel_id=1, source_target_pairs={{0,64},{64,128},{128,192},{192,256},{256,320},{320,384},{384,448},... | collective-permute-start | bytes 786440 | tf_op jit(solution)/shard_map/ppermute | solution.py:111
  141.7 4.9 %collective-permute-start.13 = (bf16[128,1024]{1,0:T(8,128)(2,1)S(1)}, bf16[128,1024]{1,0:T(8,128)(2,1)S(1)}, u32[]{:S(2)}, u32[]{:S(2)}) collective-permute-start(bf16[128,1024]{1,0:T(8,128)(2,1)S(1)} %add_convert_fusion.26), channel_id=1, source_target_pairs={{0,64},{64,128},{128,192},{192,256},{256,320},{320,384},{384,448},... | collective-permute-start | bytes 786440 | tf_op jit(solution)/shard_map/ppermute | solution.py:111
  147.8 3.5 %collective-permute-start.30 = (bf16[128,1024]{1,0:T(8,128)(2,1)S(1)}, bf16[128,1024]{1,0:T(8,128)(2,1)S(1)}, u32[]{:S(2)}, u32[]{:S(2)}) collective-permute-start(bf16[128,1024]{1,0:T(8,128)(2,1)S(1)} %add_convert_fusion.11), channel_id=1, source_target_pairs={{0,64},{64,128},{128,192},{192,256},{256,320},{320,384},{384,448},... | collective-permute-start | bytes 786440 | tf_op jit(solution)/shard_map/ppermute | solution.py:111
  152.4 5.7 %collective-permute-start.15 = (bf16[128,1024]{1,0:T(8,128)(2,1)S(1)}, bf16[128,1024]{1,0:T(8,128)(2,1)S(1)}, u32[]{:S(2)}, u32[]{:S(2)}) collective-permute-start(bf16[128,1024]{1,0:T(8,128)(2,1)S(1)} %add_convert_fusion.25), channel_id=1, source_target_pairs={{0,64},{64,128},{128,192},{192,256},{256,320},{320,384},{384,448},... | collective-permute-start | bytes 786440 | tf_op jit(solution)/shard_map/ppermute | solution.py:111
  159.2 3.5 %collective-permute-start.31 = (bf16[128,1024]{1,0:T(8,128)(2,1)S(1)}, bf16[128,1024]{1,0:T(8,128)(2,1)S(1)}, u32[]{:S(2)}, u32[]{:S(2)}) collective-permute-start(bf16[128,1024]{1,0:T(8,128)(2,1)S(1)} %add_convert_fusion.10), channel_id=1, source_target_pairs={{0,64},{64,128},{128,192},{192,256},{256,320},{320,384},{384,448},... | collective-permute-start | bytes 786440 | tf_op jit(solution)/shard_map/ppermute | solution.py:111
  163.8 4.8 %collective-permute-start.16 = (bf16[128,1024]{1,0:T(8,128)(2,1)S(1)}, bf16[128,1024]{1,0:T(8,128)(2,1)S(1)}, u32[]{:S(2)}, u32[]{:S(2)}) collective-permute-start(bf16[128,1024]{1,0:T(8,128)(2,1)S(1)} %add_convert_fusion.24), channel_id=1, source_target_pairs={{0,64},{64,128},{128,192},{192,256},{256,320},{320,384},{384,448},... | collective-permute-start | bytes 786440 | tf_op jit(solution)/shard_map/ppermute | solution.py:111
  169.8 3.5 %collective-permute-start.32 = (bf16[128,1024]{1,0:T(8,128)(2,1)S(1)}, bf16[128,1024]{1,0:T(8,128)(2,1)S(1)}, u32[]{:S(2)}, u32[]{:S(2)}) collective-permute-start(bf16[128,1024]{1,0:T(8,128)(2,1)S(1)} %add_convert_fusion.9), channel_id=1, source_target_pairs={{0,64},{64,128},{128,192},{192,256},{256,320},{320,384},{384,448},... | collective-permute-start | bytes 786440 | tf_op jit(solution)/shard_map/ppermute | solution.py:111
  174.4 5.3 %collective-permute-start.17 = (bf16[128,1024]{1,0:T(8,128)(2,1)S(1)}, bf16[128,1024]{1,0:T(8,128)(2,1)S(1)}, u32[]{:S(2)}, u32[]{:S(2)}) collective-permute-start(bf16[128,1024]{1,0:T(8,128)(2,1)S(1)} %add_convert_fusion.23), channel_id=1, source_target_pairs={{0,64},{64,128},{128,192},{192,256},{256,320},{320,384},{384,448},... | collective-permute-start | bytes 786440 | tf_op jit(solution)/shard_map/ppermute | solution.py:111
  180.8 3.0 %collective-permute-start.33 = (bf16[128,1024]{1,0:T(8,128)(2,1)S(1)}, bf16[128,1024]{1,0:T(8,128)(2,1)S(1)}, u32[]{:S(2)}, u32[]{:S(2)}) collective-permute-start(bf16[128,1024]{1,0:T(8,128)(2,1)S(1)} %add_convert_fusion.8), channel_id=1, source_target_pairs={{0,64},{64,128},{128,192},{192,256},{256,320},{320,384},{384,448},... | collective-permute-start | bytes 786440 | tf_op jit(solution)/shard_map/ppermute | solution.py:111
  184.9 5.5 %collective-permute-start.18 = (bf16[128,1024]{1,0:T(8,128)(2,1)S(1)}, bf16[128,1024]{1,0:T(8,128)(2,1)S(1)}, u32[]{:S(2)}, u32[]{:S(2)}) collective-permute-start(bf16[128,1024]{1,0:T(8,128)(2,1)S(1)} %add_convert_fusion.22), channel_id=1, source_target_pairs={{0,64},{64,128},{128,192},{192,256},{256,320},{320,384},{384,448},... | collective-permute-start | bytes 786440 | tf_op jit(solution)/shard_map/ppermute | solution.py:111
  191.5 3.0 %collective-permute-start.34 = (bf16[128,1024]{1,0:T(8,128)(2,1)S(1)}, bf16[128,1024]{1,0:T(8,128)(2,1)S(1)}, u32[]{:S(2)}, u32[]{:S(2)}) collective-permute-start(bf16[128,1024]{1,0:T(8,128)(2,1)S(1)} %add_convert_fusion.7), channel_id=1, source_target_pairs={{0,64},{64,128},{128,192},{192,256},{256,320},{320,384},{384,448},... | collective-permute-start | bytes 786440 | tf_op jit(solution)/shard_map/ppermute | solution.py:111
  195.7 5.3 %collective-permute-start.19 = (bf16[128,1024]{1,0:T(8,128)(2,1)S(1)}, bf16[128,1024]{1,0:T(8,128)(2,1)S(1)}, u32[]{:S(2)}, u32[]{:S(2)}) collective-permute-start(bf16[128,1024]{1,0:T(8,128)(2,1)S(1)} %add_convert_fusion.21), channel_id=1, source_target_pairs={{0,64},{64,128},{128,192},{192,256},{256,320},{320,384},{384,448},... | collective-permute-start | bytes 786440 | tf_op jit(solution)/shard_map/ppermute | solution.py:111
  201.0 19.2 %collective-permute-start.14 = (bf16[16,2048]{1,0:T(8,128)(2,1)S(1)}, bf16[16,2048]{1,0:T(8,128)(2,1)S(1)}, u32[]{:S(2)}, u32[]{:S(2)}) collective-permute-start(bf16[16,2048]{1,0:T(8,128)(2,1)S(1)} %slice.70), channel_id=1, source_target_pairs={{0,8},{8,0},{1,9},{9,1},{2,10},{10,2},{3,11},{11,3},{4,12},{12,4},... | collective-permute-start | bytes 196616 | tf_op jit(solution)/shard_map/ppermute | solution.py:30
  227.3 4.0 %collective-permute-done.35 = bf16[128,1024]{1,0:T(8,128)(2,1)S(1)} collective-permute-done((bf16[128,1024]{1,0:T(8,128)(2,1)S(1)}, bf16[128,1024]{1,0:T(8,128)(2,1)S(1)}, u32[]{:S(2)}, u32[]{:S(2)}) %collective-permute-start.35) | collective-permute-done | bytes 262176 | tf_op jit(solution)/shard_map/ppermute | solution.py:111
  232.3 3.3 %collective-permute-start.36 = (bf16[128,1024]{1,0:T(8,128)(2,1)S(1)}, bf16[128,1024]{1,0:T(8,128)(2,1)S(1)}, u32[]{:S(2)}, u32[]{:S(2)}) collective-permute-start(bf16[128,1024]{1,0:T(8,128)(2,1)S(1)} %add_convert_fusion.5), channel_id=1, source_target_pairs={{0,64},{64,128},{128,192},{192,256},{256,320},{320,384},{384,448},... | collective-permute-start | bytes 786440 | tf_op jit(solution)/shard_map/ppermute | solution.py:111
  236.8 3.7 %collective-permute-start.21 = (bf16[128,1024]{1,0:T(8,128)(2,1)S(1)}, bf16[128,1024]{1,0:T(8,128)(2,1)S(1)}, u32[]{:S(2)}, u32[]{:S(2)}) collective-permute-start(bf16[128,1024]{1,0:T(8,128)(2,1)S(1)} %add_convert_fusion.19), channel_id=1, source_target_pairs={{0,64},{64,128},{128,192},{192,256},{256,320},{320,384},{384,448},... | collective-permute-start | bytes 786440 | tf_op jit(solution)/shard_map/ppermute | solution.py:111
  241.7 3.3 %collective-permute-start.37 = (bf16[128,1024]{1,0:T(8,128)(2,1)S(1)}, bf16[128,1024]{1,0:T(8,128)(2,1)S(1)}, u32[]{:S(2)}, u32[]{:S(2)}) collective-permute-start(bf16[128,1024]{1,0:T(8,128)(2,1)S(1)} %add_convert_fusion.4), channel_id=1, source_target_pairs={{0,64},{64,128},{128,192},{192,256},{256,320},{320,384},{384,448},... | collective-permute-start | bytes 786440 | tf_op jit(solution)/shard_map/ppermute | solution.py:111
  246.1 5.0 %collective-permute-start.22 = (bf16[128,1024]{1,0:T(8,128)(2,1)S(1)}, bf16[128,1024]{1,0:T(8,128)(2,1)S(1)}, u32[]{:S(2)}, u32[]{:S(2)}) collective-permute-start(bf16[128,1024]{1,0:T(8,128)(2,1)S(1)} %add_convert_fusion.18), channel_id=1, source_target_pairs={{0,64},{64,128},{128,192},{192,256},{256,320},{320,384},{384,448},... | collective-permute-start | bytes 786440 | tf_op jit(solution)/shard_map/ppermute | solution.py:111
  256.0 5.6 %collective-permute-start.23 = (bf16[128,1024]{1,0:T(8,128)(2,1)S(1)}, bf16[128,1024]{1,0:T(8,128)(2,1)}, u32[]{:S(2)}, u32[]{:S(2)}) collective-permute-start(bf16[128,1024]{1,0:T(8,128)(2,1)S(1)} %add_convert_fusion.17), channel_id=1, source_target_pairs={{0,64},{64,128},{128,192},{192,256},{256,320},{320,384},{384,448},... | collective-permute-start | bytes 786440 | tf_op jit(solution)/shard_map/ppermute | solution.py:111
  266.7 5.6 %collective-permute-start.24 = (bf16[128,1024]{1,0:T(8,128)(2,1)S(1)}, bf16[128,1024]{1,0:T(8,128)(2,1)}, u32[]{:S(2)}, u32[]{:S(2)}) collective-permute-start(bf16[128,1024]{1,0:T(8,128)(2,1)S(1)} %add_convert_fusion.16), channel_id=1, source_target_pairs={{0,64},{64,128},{128,192},{192,256},{256,320},{320,384},{384,448},... | collective-permute-start | bytes 786440 | tf_op jit(solution)/shard_map/ppermute | solution.py:111
  277.3 5.5 %collective-permute-start.25 = (bf16[128,1024]{1,0:T(8,128)(2,1)S(1)}, bf16[128,1024]{1,0:T(8,128)(2,1)S(1)}, u32[]{:S(2)}, u32[]{:S(2)}) collective-permute-start(bf16[128,1024]{1,0:T(8,128)(2,1)S(1)} %add_convert_fusion.15), channel_id=1, source_target_pairs={{0,64},{64,128},{128,192},{192,256},{256,320},{320,384},{384,448},... | collective-permute-start | bytes 786440 | tf_op jit(solution)/shard_map/ppermute | solution.py:111
  283.5 3.3 %all-to-all-start.1 = ((bf16[4,4,2048]{2,1,0:T(4,128)(2,1)}), bf16[4,4,2048]{2,1,0:T(4,128)(2,1)S(1)}, u32[]{:S(2)}, u32[]{:S(2)}) async-start(bf16[4,4,2048]{2,1,0:T(4,128)(2,1)} %reshape.203), calls=%async_computation.1 | async-start | bytes 131072 | tf_op jit(solution)/shard_map/all_to_all | solution.py:154
  288.9 3.5 %all-to-all-done.1 = bf16[4,4,2048]{2,1,0:T(4,128)(2,1)S(1)} async-done(((bf16[4,4,2048]{2,1,0:T(4,128)(2,1)}), bf16[4,4,2048]{2,1,0:T(4,128)(2,1)S(1)}, u32[]{:S(2)}, u32[]{:S(2)}) %all-to-all-start.1) | async-done | bytes 65568 | tf_op jit(solution)/shard_map/all_to_all | solution.py:154
  (165 shorter events, 104.7 us)
Async XLA Ops:
  7.7 10.3 %all-to-all-start = ((bf16[4,8,2048]{2,1,0:T(8,128)(2,1)}), bf16[4,8,2048]{2,1,0:T(8,128)(2,1)S(1)}, u32[]{:S(2)}, u32[]{:S(2)}) async-start(bf16[4,8,2048]{2,1,0:T(8,128)(2,1)} %fusion.2), calls=%async_computation | async-start | bytes 262144 | tf_op jit(solution)/shard_map/all_to_all | solution.py:123
  17.9 31.3 %collective-permute-start = (bf16[32,2048]{1,0:T(8,128)(2,1)S(1)}, bf16[32,2048]{1,0:T(8,128)(2,1)S(1)}, u32[]{:S(2)}, u32[]{:S(2)}) collective-permute-start(bf16[32,2048]{1,0:T(8,128)(2,1)S(1)} %bitcast.47), channel_id=1, source_target_pairs={{0,8},{8,0},{1,9},{9,1},{2,10},{10,2},{3,11},{11,3},{4,12},{12,4},... | collective-permute-start | bytes 393224 | tf_op jit(solution)/shard_map/ppermute | solution.py:30
  49.3 15.3 %collective-permute-start.1 = (bf16[64,2048]{1,0:T(8,128)(2,1)S(1)}, bf16[64,2048]{1,0:T(8,128)(2,1)S(1)}, u32[]{:S(2)}, u32[]{:S(2)}) collective-permute-start(bf16[64,2048]{1,0:T(8,128)(2,1)S(1)} %pad_maximum_fusion.2), channel_id=1, source_target_pairs={{0,6},{2,0},{4,2},{6,4},{1,7},{3,1},{5,3},{7,5},{8,14},{10,8},{12,... | collective-permute-start | bytes 786440 | tf_op jit(solution)/shard_map/ppermute | solution.py:34
  55.5 11.6 %collective-permute-start.2 = (bf16[64,2048]{1,0:T(8,128)(2,1)S(1)}, bf16[64,2048]{1,0:T(8,128)(2,1)S(1)}, u32[]{:S(2)}, u32[]{:S(2)}) collective-permute-start(bf16[64,2048]{1,0:T(8,128)(2,1)S(1)} %pad_maximum_fusion.2), channel_id=1, source_target_pairs={{0,4},{2,6},{4,0},{6,2},{1,5},{3,7},{5,1},{7,3},{8,12},{10,14},{12... | collective-permute-start | bytes 786440 | tf_op jit(solution)/shard_map/ppermute | solution.py:34
  58.1 11.8 %collective-permute-start.3 = (bf16[64,2048]{1,0:T(8,128)(2,1)S(1)}, bf16[64,2048]{1,0:T(8,128)(2,1)S(1)}, u32[]{:S(2)}, u32[]{:S(2)}) collective-permute-start(bf16[64,2048]{1,0:T(8,128)(2,1)S(1)} %pad_maximum_fusion.2), channel_id=1, source_target_pairs={{0,2},{2,4},{4,6},{6,0},{1,3},{3,5},{5,7},{7,1},{8,10},{10,12},{12... | collective-permute-start | bytes 786440 | tf_op jit(solution)/shard_map/ppermute | solution.py:34
  84.0 29.9 %collective-permute-start.6 = (bf16[128,2048]{1,0:T(8,128)(2,1)S(1)}, bf16[128,2048]{1,0:T(8,128)(2,1)S(1)}, u32[]{:S(2)}, u32[]{:S(2)}) collective-permute-start(bf16[128,2048]{1,0:T(8,128)(2,1)S(1)} %constant_dynamic-slice_fusion.2), channel_id=1, source_target_pairs={{0,1},{1,0},{2,3},{3,2},{4,5},{5,4},{6,7},{7,6},{8,9},{9,8},{10,11... | collective-permute-start | bytes 1572872 | tf_op jit(solution)/shard_map/ppermute | solution.py:30
  87.5 24.4 %collective-permute-start.26 = (bf16[128,1024]{1,0:T(8,128)(2,1)S(1)}, bf16[128,1024]{1,0:T(8,128)(2,1)S(1)}, u32[]{:S(2)}, u32[]{:S(2)}) collective-permute-start(bf16[128,1024]{1,0:T(8,128)(2,1)S(1)} %constant_dynamic-slice_fusion), channel_id=1, source_target_pairs={{0,64},{64,128},{128,192},{192,256},{256,320},{320,384},{384,448},... | collective-permute-start | bytes 786440 | tf_op jit(solution)/shard_map/ppermute | solution.py:111
  99.8 15.4 %collective-permute-start.7 = (bf16[128,1024]{1,0:T(8,128)(2,1)S(1)}, bf16[128,1024]{1,0:T(8,128)(2,1)S(1)}, u32[]{:S(2)}, u32[]{:S(2)}) collective-permute-start(bf16[128,1024]{1,0:T(8,128)(2,1)S(1)} %constant_dynamic-slice_fusion.1), channel_id=1, source_target_pairs={{0,64},{64,128},{128,192},{192,256},{256,320},{320,384},{384,448},... | collective-permute-start | bytes 786440 | tf_op jit(solution)/shard_map/ppermute | solution.py:111
  121.3 15.1 %collective-permute-start.28 = (bf16[128,1024]{1,0:T(8,128)(2,1)S(1)}, bf16[128,1024]{1,0:T(8,128)(2,1)S(1)}, u32[]{:S(2)}, u32[]{:S(2)}) collective-permute-start(bf16[128,1024]{1,0:T(8,128)(2,1)S(1)} %add_convert_fusion.13), channel_id=1, source_target_pairs={{0,64},{64,128},{128,192},{192,256},{256,320},{320,384},{384,448},... | collective-permute-start | bytes 786440 | tf_op jit(solution)/shard_map/ppermute | solution.py:111
  124.8 15.8 %collective-permute-start.12 = (bf16[128,1024]{1,0:T(8,128)(2,1)S(1)}, bf16[128,1024]{1,0:T(8,128)(2,1)S(1)}, u32[]{:S(2)}, u32[]{:S(2)}) collective-permute-start(bf16[128,1024]{1,0:T(8,128)(2,1)S(1)} %add_convert_fusion.27), channel_id=1, source_target_pairs={{0,64},{64,128},{128,192},{192,256},{256,320},{320,384},{384,448},... | collective-permute-start | bytes 786440 | tf_op jit(solution)/shard_map/ppermute | solution.py:111
  126.8 19.8 %collective-permute-start.10 = (bf16[32,2048]{1,0:T(8,128)(2,1)S(1)}, bf16[32,2048]{1,0:T(8,128)(2,1)S(1)}, u32[]{:S(2)}, u32[]{:S(2)}) collective-permute-start(bf16[32,2048]{1,0:T(8,128)(2,1)S(1)} %get-tuple-element.40), channel_id=1, source_target_pairs={{0,4},{2,6},{4,0},{6,2},{1,5},{3,7},{5,1},{7,3},{8,12},{10,14},{12... | collective-permute-start | bytes 393224 | tf_op jit(solution)/shard_map/ppermute | solution.py:34
  129.4 17.2 %collective-permute-start.8 = (bf16[32,2048]{1,0:T(8,128)(2,1)S(1)}, bf16[32,2048]{1,0:T(8,128)(2,1)S(1)}, u32[]{:S(2)}, u32[]{:S(2)}) collective-permute-start(bf16[32,2048]{1,0:T(8,128)(2,1)S(1)} %get-tuple-element.39), channel_id=1, source_target_pairs={{0,2},{2,4},{4,6},{6,0},{1,3},{3,5},{5,7},{7,1},{8,10},{10,12},{12... | collective-permute-start | bytes 393224 | tf_op jit(solution)/shard_map/ppermute | solution.py:34
  132.1 14.5 %collective-permute-start.9 = (bf16[32,2048]{1,0:T(8,128)(2,1)S(1)}, bf16[32,2048]{1,0:T(8,128)(2,1)S(1)}, u32[]{:S(2)}, u32[]{:S(2)}) collective-permute-start(bf16[32,2048]{1,0:T(8,128)(2,1)S(1)} %get-tuple-element.41), channel_id=1, source_target_pairs={{0,6},{2,0},{4,2},{6,4},{1,7},{3,1},{5,3},{7,5},{8,14},{10,8},{12,... | collective-permute-start | bytes 393224 | tf_op jit(solution)/shard_map/ppermute | solution.py:34
  141.7 9.6 %collective-permute-start.13 = (bf16[128,1024]{1,0:T(8,128)(2,1)S(1)}, bf16[128,1024]{1,0:T(8,128)(2,1)S(1)}, u32[]{:S(2)}, u32[]{:S(2)}) collective-permute-start(bf16[128,1024]{1,0:T(8,128)(2,1)S(1)} %add_convert_fusion.26), channel_id=1, source_target_pairs={{0,64},{64,128},{128,192},{192,256},{256,320},{320,384},{384,448},... | collective-permute-start | bytes 786440 | tf_op jit(solution)/shard_map/ppermute | solution.py:111
  147.8 10.3 %collective-permute-start.30 = (bf16[128,1024]{1,0:T(8,128)(2,1)S(1)}, bf16[128,1024]{1,0:T(8,128)(2,1)S(1)}, u32[]{:S(2)}, u32[]{:S(2)}) collective-permute-start(bf16[128,1024]{1,0:T(8,128)(2,1)S(1)} %add_convert_fusion.11), channel_id=1, source_target_pairs={{0,64},{64,128},{128,192},{192,256},{256,320},{320,384},{384,448},... | collective-permute-start | bytes 786440 | tf_op jit(solution)/shard_map/ppermute | solution.py:111
  152.4 10.3 %collective-permute-start.15 = (bf16[128,1024]{1,0:T(8,128)(2,1)S(1)}, bf16[128,1024]{1,0:T(8,128)(2,1)S(1)}, u32[]{:S(2)}, u32[]{:S(2)}) collective-permute-start(bf16[128,1024]{1,0:T(8,128)(2,1)S(1)} %add_convert_fusion.25), channel_id=1, source_target_pairs={{0,64},{64,128},{128,192},{192,256},{256,320},{320,384},{384,448},... | collective-permute-start | bytes 786440 | tf_op jit(solution)/shard_map/ppermute | solution.py:111
  159.2 9.5 %collective-permute-start.31 = (bf16[128,1024]{1,0:T(8,128)(2,1)S(1)}, bf16[128,1024]{1,0:T(8,128)(2,1)S(1)}, u32[]{:S(2)}, u32[]{:S(2)}) collective-permute-start(bf16[128,1024]{1,0:T(8,128)(2,1)S(1)} %add_convert_fusion.10), channel_id=1, source_target_pairs={{0,64},{64,128},{128,192},{192,256},{256,320},{320,384},{384,448},... | collective-permute-start | bytes 786440 | tf_op jit(solution)/shard_map/ppermute | solution.py:111
  169.8 9.9 %collective-permute-start.32 = (bf16[128,1024]{1,0:T(8,128)(2,1)S(1)}, bf16[128,1024]{1,0:T(8,128)(2,1)S(1)}, u32[]{:S(2)}, u32[]{:S(2)}) collective-permute-start(bf16[128,1024]{1,0:T(8,128)(2,1)S(1)} %add_convert_fusion.9), channel_id=1, source_target_pairs={{0,64},{64,128},{128,192},{192,256},{256,320},{320,384},{384,448},... | collective-permute-start | bytes 786440 | tf_op jit(solution)/shard_map/ppermute | solution.py:111
  174.4 9.5 %collective-permute-start.17 = (bf16[128,1024]{1,0:T(8,128)(2,1)S(1)}, bf16[128,1024]{1,0:T(8,128)(2,1)S(1)}, u32[]{:S(2)}, u32[]{:S(2)}) collective-permute-start(bf16[128,1024]{1,0:T(8,128)(2,1)S(1)} %add_convert_fusion.23), channel_id=1, source_target_pairs={{0,64},{64,128},{128,192},{192,256},{256,320},{320,384},{384,448},... | collective-permute-start | bytes 786440 | tf_op jit(solution)/shard_map/ppermute | solution.py:111
  180.8 9.6 %collective-permute-start.33 = (bf16[128,1024]{1,0:T(8,128)(2,1)S(1)}, bf16[128,1024]{1,0:T(8,128)(2,1)S(1)}, u32[]{:S(2)}, u32[]{:S(2)}) collective-permute-start(bf16[128,1024]{1,0:T(8,128)(2,1)S(1)} %add_convert_fusion.8), channel_id=1, source_target_pairs={{0,64},{64,128},{128,192},{192,256},{256,320},{320,384},{384,448},... | collective-permute-start | bytes 786440 | tf_op jit(solution)/shard_map/ppermute | solution.py:111
  184.9 9.6 %collective-permute-start.18 = (bf16[128,1024]{1,0:T(8,128)(2,1)S(1)}, bf16[128,1024]{1,0:T(8,128)(2,1)S(1)}, u32[]{:S(2)}, u32[]{:S(2)}) collective-permute-start(bf16[128,1024]{1,0:T(8,128)(2,1)S(1)} %add_convert_fusion.22), channel_id=1, source_target_pairs={{0,64},{64,128},{128,192},{192,256},{256,320},{320,384},{384,448},... | collective-permute-start | bytes 786440 | tf_op jit(solution)/shard_map/ppermute | solution.py:111
  191.5 28.6 %collective-permute-start.34 = (bf16[128,1024]{1,0:T(8,128)(2,1)S(1)}, bf16[128,1024]{1,0:T(8,128)(2,1)S(1)}, u32[]{:S(2)}, u32[]{:S(2)}) collective-permute-start(bf16[128,1024]{1,0:T(8,128)(2,1)S(1)} %add_convert_fusion.7), channel_id=1, source_target_pairs={{0,64},{64,128},{128,192},{192,256},{256,320},{320,384},{384,448},... | collective-permute-start | bytes 786440 | tf_op jit(solution)/shard_map/ppermute | solution.py:111
  195.7 28.6 %collective-permute-start.19 = (bf16[128,1024]{1,0:T(8,128)(2,1)S(1)}, bf16[128,1024]{1,0:T(8,128)(2,1)S(1)}, u32[]{:S(2)}, u32[]{:S(2)}) collective-permute-start(bf16[128,1024]{1,0:T(8,128)(2,1)S(1)} %add_convert_fusion.21), channel_id=1, source_target_pairs={{0,64},{64,128},{128,192},{192,256},{256,320},{320,384},{384,448},... | collective-permute-start | bytes 786440 | tf_op jit(solution)/shard_map/ppermute | solution.py:111
  201.0 26.2 %collective-permute-start.14 = (bf16[16,2048]{1,0:T(8,128)(2,1)S(1)}, bf16[16,2048]{1,0:T(8,128)(2,1)S(1)}, u32[]{:S(2)}, u32[]{:S(2)}) collective-permute-start(bf16[16,2048]{1,0:T(8,128)(2,1)S(1)} %slice.70), channel_id=1, source_target_pairs={{0,8},{8,0},{1,9},{9,1},{2,10},{10,2},{3,11},{11,3},{4,12},{12,4},... | collective-permute-start | bytes 196616 | tf_op jit(solution)/shard_map/ppermute | solution.py:30
  221.3 10.0 %collective-permute-start.35 = (bf16[128,1024]{1,0:T(8,128)(2,1)S(1)}, bf16[128,1024]{1,0:T(8,128)(2,1)S(1)}, u32[]{:S(2)}, u32[]{:S(2)}) collective-permute-start(bf16[128,1024]{1,0:T(8,128)(2,1)S(1)} %add_convert_fusion.6), channel_id=1, source_target_pairs={{0,64},{64,128},{128,192},{192,256},{256,320},{320,384},{384,448},... | collective-permute-start | bytes 786440 | tf_op jit(solution)/shard_map/ppermute | solution.py:111
  225.3 10.4 %collective-permute-start.20 = (bf16[128,1024]{1,0:T(8,128)(2,1)S(1)}, bf16[128,1024]{1,0:T(8,128)(2,1)S(1)}, u32[]{:S(2)}, u32[]{:S(2)}) collective-permute-start(bf16[128,1024]{1,0:T(8,128)(2,1)S(1)} %add_convert_fusion.20), channel_id=1, source_target_pairs={{0,64},{64,128},{128,192},{192,256},{256,320},{320,384},{384,448},... | collective-permute-start | bytes 786440 | tf_op jit(solution)/shard_map/ppermute | solution.py:111
  252.2 9.5 %collective-permute-start.38 = (bf16[128,1024]{1,0:T(8,128)(2,1)S(1)}, bf16[128,1024]{1,0:T(8,128)(2,1)S(1)}, u32[]{:S(2)}, u32[]{:S(2)}) collective-permute-start(bf16[128,1024]{1,0:T(8,128)(2,1)S(1)} %add_convert_fusion.3), channel_id=1, source_target_pairs={{0,64},{64,128},{128,192},{192,256},{256,320},{320,384},{384,448},... | collective-permute-start | bytes 786440 | tf_op jit(solution)/shard_map/ppermute | solution.py:111
  256.0 9.5 %collective-permute-start.23 = (bf16[128,1024]{1,0:T(8,128)(2,1)S(1)}, bf16[128,1024]{1,0:T(8,128)(2,1)}, u32[]{:S(2)}, u32[]{:S(2)}) collective-permute-start(bf16[128,1024]{1,0:T(8,128)(2,1)S(1)} %add_convert_fusion.17), channel_id=1, source_target_pairs={{0,64},{64,128},{128,192},{192,256},{256,320},{320,384},{384,448},... | collective-permute-start | bytes 786440 | tf_op jit(solution)/shard_map/ppermute | solution.py:111
  262.8 9.5 %collective-permute-start.39 = (bf16[128,1024]{1,0:T(8,128)(2,1)S(1)}, bf16[128,1024]{1,0:T(8,128)(2,1)S(1)}, u32[]{:S(2)}, u32[]{:S(2)}) collective-permute-start(bf16[128,1024]{1,0:T(8,128)(2,1)S(1)} %add_convert_fusion.2), channel_id=1, source_target_pairs={{0,64},{64,128},{128,192},{192,256},{256,320},{320,384},{384,448},... | collective-permute-start | bytes 786440 | tf_op jit(solution)/shard_map/ppermute | solution.py:111
  266.7 9.5 %collective-permute-start.24 = (bf16[128,1024]{1,0:T(8,128)(2,1)S(1)}, bf16[128,1024]{1,0:T(8,128)(2,1)}, u32[]{:S(2)}, u32[]{:S(2)}) collective-permute-start(bf16[128,1024]{1,0:T(8,128)(2,1)S(1)} %add_convert_fusion.16), channel_id=1, source_target_pairs={{0,64},{64,128},{128,192},{192,256},{256,320},{320,384},{384,448},... | collective-permute-start | bytes 786440 | tf_op jit(solution)/shard_map/ppermute | solution.py:111
  273.4 13.5 %collective-permute-start.40 = (bf16[128,1024]{1,0:T(8,128)(2,1)S(1)}, bf16[128,1024]{1,0:T(8,128)(2,1)S(1)}, u32[]{:S(2)}, u32[]{:S(2)}) collective-permute-start(bf16[128,1024]{1,0:T(8,128)(2,1)S(1)} %add_convert_fusion.1), channel_id=1, source_target_pairs={{0,64},{64,128},{128,192},{192,256},{256,320},{320,384},{384,448},... | collective-permute-start | bytes 786440 | tf_op jit(solution)/shard_map/ppermute | solution.py:111
  277.3 9.6 %collective-permute-start.25 = (bf16[128,1024]{1,0:T(8,128)(2,1)S(1)}, bf16[128,1024]{1,0:T(8,128)(2,1)S(1)}, u32[]{:S(2)}, u32[]{:S(2)}) collective-permute-start(bf16[128,1024]{1,0:T(8,128)(2,1)S(1)} %add_convert_fusion.15), channel_id=1, source_target_pairs={{0,64},{64,128},{128,192},{192,256},{256,320},{320,384},{384,448},... | collective-permute-start | bytes 786440 | tf_op jit(solution)/shard_map/ppermute | solution.py:111
  (20 other events, 224.7 us)

commit v4 on v3

--- a/solution.py
+++ b/solution.py
@@ -100,15 +100,15 @@
     towards = height * (1 - 2 * core)
     pairs = [(2 * i, 2 * i + 2) for i in range(n_group - 1)]
     pairs += [(2 * i + 3, 2 * i + 1) for i in range(n_group - 1)]
-    carried = [None] * len(streams)
+    carried, last = [None] * len(streams), streams[0]
     for step in range(n_group - 1):
         begin = lax.clamp(0, here * height + (n_group - 1 - step) * towards, top)
         for k, rows in enumerate(streams):
             term = block_of(rows, begin, height)
             if step:
-                arrived = jnp.where(rank <= step, carried[k].astype(jnp.float32), 0.0)
-                term = (term.astype(jnp.float32) + arrived).astype(jnp.bfloat16)
-            carried[k] = lax.ppermute(term, ("group", "core"), pairs)
+                carried[k], last = lax.optimization_barrier((carried[k], last))
+                term = term + jnp.where(rank <= step, carried[k], jnp.zeros_like(carried[k]))
+            carried[k], last = lax.ppermute(term, ("group", "core"), pairs), term
         if step in ties:
             beside, carried[0] = lax.optimization_barrier((beside, carried[0]))
             beside = ties[step](beside)
@@ -131,23 +131,32 @@
     hidden, hid_grad = expert_part(x_all, g_all, w_in, w_out)
     other = swap(jnp.concatenate([hid_grad, hidden], axis=1), "core")
     partial = dot_f32(hid_grad, w_in, ((1,), (1,))).astype(jnp.bfloat16)
-    hid_grad_both = jnp.concatenate([hid_grad, other[:, :ff_dev]], axis=1)
-    hidden_both = jnp.concatenate([hidden, other[:, ff_dev:]], axis=1)
-    hid_grad_both, partial = lax.optimization_barrier((hid_grad_both, partial))
-    grad_in = dot_f32(x_all, hid_grad_both, ((0,), (0,))).astype(jnp.bfloat16)
-    grad_out = dot_f32(g_all, hidden_both, ((0,), (0,))).astype(jnp.bfloat16)
+
+    def product(rows, units):
+        return dot_f32(rows, units, ((0,), (0,))).astype(jnp.bfloat16)
+
+    cut = ff_dev // 2
+    own_in = product(x_all, hid_grad)
+    own_out = product(g_all, hidden)
+    other_in = product(x_all, other[:, :ff_dev])
+    other_out = product(g_all, other[:, ff_dev:])
+    streams = [
+        own_in,
+        jnp.concatenate([own_out, other_in[:, :cut]], axis=1),
+        jnp.concatenate([other_in[:, cut:], other_out], axis=1),
+    ]
 
     def along_y(rows):
         parts = rows.reshape(4, -1, d_model)
         total = parts[0].astype(jnp.float32)
         for by in (1, 3, 2):
             total = total + shift(parts[by], by).astype(jnp.float32)
-        return total.astype(jnp.bfloat16)
+        total = total.astype(jnp.bfloat16)
+        turned = jnp.concatenate([total[4 * CAP :], total[: 4 * CAP]], axis=0)
+        return jnp.where(lax.axis_index("zh") == 0, total, turned)
 
     def across_zh(rows):
-        half = rows.shape[0] // 2
-        total = rows[:half].astype(jnp.float32) + swap(rows[half:], "zh").astype(jnp.float32)
-        return total.astype(jnp.bfloat16)
+        return lax.psum_scatter(rows, "zh", scatter_dimension=0, tiled=True)
 
     def along_x(rows):
         parts = rows.reshape(4, CAP, d_model)
@@ -156,21 +165,25 @@
     core, half = lax.axis_index("core"), partial.shape[0] // 2
     given = swap(block_of(partial, (1 - core) * half, half), "core").astype(jnp.float32)
     given = (block_of(partial, core * half, half).astype(jnp.float32) + given).astype(jnp.bfloat16)
-    (sum_in, sum_out), slots = line_sums(
-        [grad_in, grad_out], n_group, given, {0: along_y, 3: across_zh, 9: along_x}
-    )
     sel_slots = sel.reshape(4, 2, CAP, n_tok)[:, 0].reshape(4 * CAP, n_tok)
-    in_grad = dot_f32(sel_slots, slots, ((0,), (0,))).astype(jnp.bfloat16)
-
+
+    def to_tokens(rows):
+        return dot_f32(sel_slots, rows, ((0,), (0,))).astype(jnp.bfloat16)
+
+    sums, in_grad = line_sums(
+        streams, n_group, given, {0: along_y, 3: across_zh, 11: along_x, 14: to_tokens}
+    )
     width = d_model // n_group
     here = lax.axis_index("group") * width
-    own_in = block_of(grad_in, here, width)[:, :ff_dev].astype(jnp.float32)
-    own_out = block_of(grad_out, here, width)[:, :ff_dev].astype(jnp.float32)
-    across = swap(jnp.concatenate([sum_in[:, ff_dev:], sum_out[:, ff_dev:]], axis=1), "core")
-    across = across.astype(jnp.float32)
-    w_in_grad = own_in + sum_in[:, :ff_dev].astype(jnp.float32) + across[:, :ff_dev]
-    w_out_grad = own_out + sum_out[:, :ff_dev].astype(jnp.float32) + across[:, ff_dev:]
-    return in_grad, w_in_grad.astype(jnp.bfloat16), w_out_grad.astype(jnp.bfloat16).T
+    across = swap(jnp.concatenate([sums[1][:, ff_dev:], sums[2]], axis=1), "core")
+
+    def total(own, carried, given):
+        parts = (block_of(own, here, width), carried, given)
+        return sum(part.astype(jnp.float32) for part in parts).astype(jnp.bfloat16)
+
+    w_in_grad = total(own_in, sums[0], across[:, :ff_dev])
+    w_out_grad = total(own_out, sums[1][:, :ff_dev], across[:, ff_dev:])
+    return in_grad, w_in_grad, w_out_grad.T
 
 
 def solution(mesh):

time: 299 us -> 322 us (1.077)
  the two profiles are of different devices: /device:TPU:64 before, /device:TPU:34 now
where the time goes in v4:
time: 322 us; the launch traced here: 320 us
  starting transfers between devices  205 us (64%)
  waiting for transfers between devices  53 us (16%)
  other arithmetic  20.3 us (6%)
  matrix products  15.9 us (5%)
  between operations  15.6 us (5%)
  local copies, waits for them, and re-layouts  9.56 us (3%)
    ppermute x45, starting transfers between devices, line_sums(): carried[k], last = (lax.ppermute(term, ('group', 'core'), pairs), term)  141 us
    ppermute x5, starting transfers between devices, swap(): return lax.ppermute(value, axis, [(0, 1), (1, 0)])  36.2 us
    ppermute x5, waiting for transfers between devices, swap(): return lax.ppermute(value, axis, [(0, 1), (1, 0)])  22.9 us
    ppermute x6, starting transfers between devices, shift(): return lax.ppermute(value, 'y', [(i, (i + by) % 4) for i in range(4)])  18.7 us
    ppermute x45, waiting for transfers between devices, line_sums(): carried[k], last = (lax.ppermute(term, ('group', 'core'), pairs), term)  17.7 us
    dot_general x14, matrix products, dot_f32(): lax.dot_general(a, b, (dims, ((), ())), preferred_element_type=jnp.float32)  15.9 us
    add x42, other arithmetic, line_sums(): term + jnp.where(rank <= step, carried[k], jnp.zeros_like(carried[k]))  15.2 us
    ppermute x6, waiting for transfers between devices, shift(): return lax.ppermute(value, 'y', [(i, (i + by) % 4) for i in range(4)])  7.86 us
  transfers between devices with their start and end apart: 59, of which 13 were waited for; matrix products, arithmetic and copies ran while one was open for 8% of the time, Pallas kernels for 0%

profile of v4, /device:TPU:34, one launch (start us, length us, event | category | flops | bytes accessed | tf_op | source)
XLA Modules:
  0.0 319.8 jit_solution(7186377059899706190)
XLA Ops:
  14.2 4.8 %all-to-all-start = ((bf16[4,8,2048]{2,1,0:T(8,128)(2,1)}), bf16[4,8,2048]{2,1,0:T(8,128)(2,1)S(1)}, u32[]{:S(2)}, u32[]{:S(2)}) async-start(bf16[4,8,2048]{2,1,0:T(8,128)(2,1)} %fusion.2), calls=%async_computation | async-start | bytes 262144 | tf_op jit(solution)/shard_map/all_to_all | solution.py:123
  19.1 4.5 %all-to-all-done = bf16[4,8,2048]{2,1,0:T(8,128)(2,1)S(1)} async-done(((bf16[4,8,2048]{2,1,0:T(8,128)(2,1)}), bf16[4,8,2048]{2,1,0:T(8,128)(2,1)S(1)}, u32[]{:S(2)}, u32[]{:S(2)}) %all-to-all-start) | async-done | bytes 131104 | tf_op jit(solution)/shard_map/all_to_all | solution.py:123
  23.5 28.1 %collective-permute-start = (bf16[32,2048]{1,0:T(8,128)(2,1)S(1)}, bf16[32,2048]{1,0:T(8,128)(2,1)S(1)}, u32[]{:S(2)}, u32[]{:S(2)}) collective-permute-start(bf16[32,2048]{1,0:T(8,128)(2,1)S(1)} %bitcast.50), channel_id=1, source_target_pairs={{0,8},{8,0},{1,9},{9,1},{2,10},{10,2},{3,11},{11,3},{4,12},{12,4},... | collective-permute-start | bytes 393224 | tf_op jit(solution)/shard_map/ppermute | solution.py:30
  52.6 20.2 %collective-permute-done = bf16[32,2048]{1,0:T(8,128)(2,1)S(1)} collective-permute-done((bf16[32,2048]{1,0:T(8,128)(2,1)S(1)}, bf16[32,2048]{1,0:T(8,128)(2,1)S(1)}, u32[]{:S(2)}, u32[]{:S(2)}) %collective-permute-start) | collective-permute-done | bytes 131104 | tf_op jit(solution)/shard_map/ppermute | solution.py:30
  72.8 4.9 %collective-permute-start.1 = (bf16[64,2048]{1,0:T(8,128)(2,1)S(1)}, bf16[64,2048]{1,0:T(8,128)(2,1)S(1)}, u32[]{:S(2)}, u32[]{:S(2)}) collective-permute-start(bf16[64,2048]{1,0:T(8,128)(2,1)S(1)} %pad_maximum_fusion.1), channel_id=1, source_target_pairs={{0,6},{2,0},{4,2},{6,4},{1,7},{3,1},{5,3},{7,5},{8,14},{10,8},{12,... | collective-permute-start | bytes 786440 | tf_op jit(solution)/shard_map/ppermute | solution.py:34
  81.0 2.9 collective-permute-start.3
  84.6 3.2 collective-permute-done.1
  121.1 3.1 collective-permute-start.8
  134.8 5.5 %collective-permute-done.13 = bf16[128,768]{1,0:T(8,128)(2,1)S(1)} collective-permute-done((bf16[128,768]{1,0:T(8,128)(2,1)S(1)}, bf16[128,768]{1,0:T(8,128)(2,1)S(1)}, u32[]{:S(2)}, u32[]{:S(2)}) %collective-permute-start.13) | collective-permute-done | bytes 196640 | tf_op jit(solution)/shard_map/ppermute | solution.py:111
  144.5 4.4 %collective-permute-start.14 = (bf16[128,512]{1,0:T(8,128)(2,1)S(1)}, bf16[128,512]{1,0:T(8,128)(2,1)S(1)}, u32[]{:S(2)}, u32[]{:S(2)}) collective-permute-start(bf16[128,512]{1,0:T(8,128)(2,1)S(1)} %select_add_fusion.40), channel_id=1, source_target_pairs={{0,64},{64,128},{128,192},{192,256},{256,320},{320,384},{384,448},... | collective-permute-start | bytes 393224 | tf_op jit(solution)/shard_map/ppermute | solution.py:111
  149.0 5.1 %collective-permute-start.19 = (bf16[128,768]{1,0:T(8,128)(2,1)S(1)}, bf16[128,768]{1,0:T(8,128)(2,1)S(1)}, u32[]{:S(2)}, u32[]{:S(2)}) collective-permute-start(bf16[128,768]{1,0:T(8,128)(2,1)S(1)} %select_add_fusion.25), channel_id=1, source_target_pairs={{0,64},{64,128},{128,192},{192,256},{256,320},{320,384},{384,448},... | collective-permute-start | bytes 589832 | tf_op jit(solution)/shard_map/ppermute | solution.py:111
  155.7 4.4 %collective-permute-start.17 = (bf16[128,512]{1,0:T(8,128)(2,1)}, bf16[128,512]{1,0:T(8,128)(2,1)}, u32[]{:S(2)}, u32[]{:S(2)}) collective-permute-start(bf16[128,512]{1,0:T(8,128)(2,1)} %select_add_fusion.39), channel_id=1, source_target_pairs={{0,64},{64,128},{128,192},{192,256},{256,320},{320,384},{384,448},... | collective-permute-start | bytes 393224 | tf_op jit(solution)/shard_map/ppermute | solution.py:111
  160.8 3.3 %collective-permute-start.18 = (bf16[128,768]{1,0:T(8,128)(2,1)}, bf16[128,768]{1,0:T(8,128)(2,1)}, u32[]{:S(2)}, u32[]{:S(2)}) collective-permute-start(bf16[128,768]{1,0:T(8,128)(2,1)} %select_add_fusion.24), channel_id=1, source_target_pairs={{0,64},{64,128},{128,192},{192,256},{256,320},{320,384},{384,448},... | collective-permute-start | bytes 589832 | tf_op jit(solution)/shard_map/ppermute | solution.py:111
  165.3 5.4 %collective-permute-start.22 = (bf16[128,768]{1,0:T(8,128)(2,1)S(1)}, bf16[128,768]{1,0:T(8,128)(2,1)S(1)}, u32[]{:S(2)}, u32[]{:S(2)}) collective-permute-start(bf16[128,768]{1,0:T(8,128)(2,1)S(1)} %select_add_fusion.23), channel_id=1, source_target_pairs={{0,64},{64,128},{128,192},{192,256},{256,320},{320,384},{384,448},... | collective-permute-start | bytes 589832 | tf_op jit(solution)/shard_map/ppermute | solution.py:111
  171.8 4.8 %collective-permute-start.21 = (bf16[128,768]{1,0:T(8,128)(2,1)S(1)}, bf16[128,768]{1,0:T(8,128)(2,1)S(1)}, u32[]{:S(2)}, u32[]{:S(2)}) collective-permute-start(bf16[128,768]{1,0:T(8,128)(2,1)S(1)} %select_add_fusion.22), channel_id=1, source_target_pairs={{0,64},{64,128},{128,192},{192,256},{256,320},{320,384},{384,448},... | collective-permute-start | bytes 589832 | tf_op jit(solution)/shard_map/ppermute | solution.py:111
  177.6 4.4 %collective-permute-start.20 = (bf16[128,512]{1,0:T(8,128)(2,1)S(1)}, bf16[128,512]{1,0:T(8,128)(2,1)S(1)}, u32[]{:S(2)}, u32[]{:S(2)}) collective-permute-start(bf16[128,512]{1,0:T(8,128)(2,1)S(1)} %select_add_fusion.38), channel_id=1, source_target_pairs={{0,64},{64,128},{128,192},{192,256},{256,320},{320,384},{384,448},... | collective-permute-start | bytes 393224 | tf_op jit(solution)/shard_map/ppermute | solution.py:111
  184.4 4.6 %collective-permute-start.24 = (bf16[128,768]{1,0:T(8,128)(2,1)S(1)}, bf16[128,768]{1,0:T(8,128)(2,1)S(1)}, u32[]{:S(2)}, u32[]{:S(2)}) collective-permute-start(bf16[128,768]{1,0:T(8,128)(2,1)S(1)} %select_add_fusion.20), channel_id=1, source_target_pairs={{0,64},{64,128},{128,192},{192,256},{256,320},{320,384},{384,448},... | collective-permute-start | bytes 589832 | tf_op jit(solution)/shard_map/ppermute | solution.py:111
  191.2 5.0 %collective-permute-start.28 = (bf16[128,768]{1,0:T(8,128)(2,1)S(1)}, bf16[128,768]{1,0:T(8,128)(2,1)S(1)}, u32[]{:S(2)}, u32[]{:S(2)}) collective-permute-start(bf16[128,768]{1,0:T(8,128)(2,1)S(1)} %select_add_fusion.19), channel_id=1, source_target_pairs={{0,64},{64,128},{128,192},{192,256},{256,320},{320,384},{384,448},... | collective-permute-start | bytes 589832 | tf_op jit(solution)/shard_map/ppermute | solution.py:111
  203.8 3.0 collective-permute-start.31
  211.8 4.6 %collective-permute-start.29 = (bf16[128,512]{1,0:T(8,128)(2,1)S(1)}, bf16[128,512]{1,0:T(8,128)(2,1)S(1)}, u32[]{:S(2)}, u32[]{:S(2)}) collective-permute-start(bf16[128,512]{1,0:T(8,128)(2,1)S(1)} %select_add_fusion.35), channel_id=1, source_target_pairs={{0,64},{64,128},{128,192},{192,256},{256,320},{320,384},{384,448},... | collective-permute-start | bytes 393224 | tf_op jit(solution)/shard_map/ppermute | solution.py:111
  216.6 4.4 %collective-permute-start.34 = (bf16[128,768]{1,0:T(8,128)(2,1)S(1)}, bf16[128,768]{1,0:T(8,128)(2,1)S(1)}, u32[]{:S(2)}, u32[]{:S(2)}) collective-permute-start(bf16[128,768]{1,0:T(8,128)(2,1)S(1)} %select_add_fusion.15), channel_id=1, source_target_pairs={{0,64},{64,128},{128,192},{192,256},{256,320},{320,384},{384,448},... | collective-permute-start | bytes 589832 | tf_op jit(solution)/shard_map/ppermute | solution.py:111
  221.1 4.1 %collective-permute-start.33 = (bf16[128,768]{1,0:T(8,128)(2,1)S(1)}, bf16[128,768]{1,0:T(8,128)(2,1)S(1)}, u32[]{:S(2)}, u32[]{:S(2)}) collective-permute-start(bf16[128,768]{1,0:T(8,128)(2,1)S(1)} %select_add_fusion.14), channel_id=1, source_target_pairs={{0,64},{64,128},{128,192},{192,256},{256,320},{320,384},{384,448},... | collective-permute-start | bytes 589832 | tf_op jit(solution)/shard_map/ppermute | solution.py:111
  227.4 3.8 %collective-permute-start.37 = (bf16[128,768]{1,0:T(8,128)(2,1)S(1)}, bf16[128,768]{1,0:T(8,128)(2,1)S(1)}, u32[]{:S(2)}, u32[]{:S(2)}) collective-permute-start(bf16[128,768]{1,0:T(8,128)(2,1)S(1)} %select_add_fusion.13), channel_id=1, source_target_pairs={{0,64},{64,128},{128,192},{192,256},{256,320},{320,384},{384,448},... | collective-permute-start | bytes 589832 | tf_op jit(solution)/shard_map/ppermute | solution.py:111
  233.4 3.3 %collective-permute-start.35 = (bf16[128,512]{1,0:T(8,128)(2,1)S(1)}, bf16[128,512]{1,0:T(8,128)(2,1)S(1)}, u32[]{:S(2)}, u32[]{:S(2)}) collective-permute-start(bf16[128,512]{1,0:T(8,128)(2,1)S(1)} %select_add_fusion.33), channel_id=1, source_target_pairs={{0,64},{64,128},{128,192},{192,256},{256,320},{320,384},{384,448},... | collective-permute-start | bytes 393224 | tf_op jit(solution)/shard_map/ppermute | solution.py:111
  236.8 3.3 %collective-permute-start.40 = (bf16[128,768]{1,0:T(8,128)(2,1)S(1)}, bf16[128,768]{1,0:T(8,128)(2,1)S(1)}, u32[]{:S(2)}, u32[]{:S(2)}) collective-permute-start(bf16[128,768]{1,0:T(8,128)(2,1)S(1)} %select_add_fusion.11), channel_id=1, source_target_pairs={{0,64},{64,128},{128,192},{192,256},{256,320},{320,384},{384,448},... | collective-permute-start | bytes 589832 | tf_op jit(solution)/shard_map/ppermute | solution.py:111
  240.2 4.6 %collective-permute-start.39 = (bf16[128,768]{1,0:T(8,128)(2,1)S(1)}, bf16[128,768]{1,0:T(8,128)(2,1)S(1)}, u32[]{:S(2)}, u32[]{:S(2)}) collective-permute-start(bf16[128,768]{1,0:T(8,128)(2,1)S(1)} %select_add_fusion.10), channel_id=1, source_target_pairs={{0,64},{64,128},{128,192},{192,256},{256,320},{320,384},{384,448},... | collective-permute-start | bytes 589832 | tf_op jit(solution)/shard_map/ppermute | solution.py:111
  260.7 3.1 collective-permute-start.46
  268.5 5.6 %collective-permute-start.44 = (bf16[128,512]{1,0:T(8,128)(2,1)S(1)}, bf16[128,512]{1,0:T(8,128)(2,1)S(1)}, u32[]{:S(2)}, u32[]{:S(2)}) collective-permute-start(bf16[128,512]{1,0:T(8,128)(2,1)S(1)} %select_add_fusion.30), channel_id=1, source_target_pairs={{0,64},{64,128},{128,192},{192,256},{256,320},{320,384},{384,448},... | collective-permute-start | bytes 393224 | tf_op jit(solution)/shard_map/ppermute | solution.py:111
  282.0 3.9 %collective-permute-start.51 = (bf16[128,768]{1,0:T(8,128)(2,1)S(1)}, bf16[128,768]{1,0:T(8,128)(2,1)S(1)}, u32[]{:S(2)}, u32[]{:S(2)}) collective-permute-start(bf16[128,768]{1,0:T(8,128)(2,1)S(1)} %select_add_fusion.3), channel_id=1, source_target_pairs={{0,64},{64,128},{128,192},{192,256},{256,320},{320,384},{384,448},... | collective-permute-start | bytes 589832 | tf_op jit(solution)/shard_map/ppermute | solution.py:111
  289.8 3.9 %collective-permute-start.52 = (bf16[128,768]{1,0:T(8,128)(2,1)S(1)}, bf16[128,768]{1,0:T(8,128)(2,1)S(1)}, u32[]{:S(2)}, u32[]{:S(2)}) collective-permute-start(bf16[128,768]{1,0:T(8,128)(2,1)S(1)} %select_add_fusion.1), channel_id=1, source_target_pairs={{0,64},{64,128},{128,192},{192,256},{256,320},{320,384},{384,448},... | collective-permute-start | bytes 589832 | tf_op jit(solution)/shard_map/ppermute | solution.py:111
  298.0 4.3 %all-to-all-start.1 = ((bf16[4,4,2048]{2,1,0:T(4,128)(2,1)}), bf16[4,4,2048]{2,1,0:T(4,128)(2,1)S(1)}, u32[]{:S(2)}, u32[]{:S(2)}) async-start(bf16[4,4,2048]{2,1,0:T(4,128)(2,1)} %reshape.203), calls=%async_computation.2 | async-start | bytes 131072 | tf_op jit(solution)/shard_map/all_to_all | solution.py:163
  302.3 3.3 %collective-permute-start.50 = (bf16[128,512]{1,0:T(8,128)(2,1)}, bf16[128,512]{1,0:T(8,128)(2,1)S(1)}, u32[]{:S(2)}, u32[]{:S(2)}) collective-permute-start(bf16[128,512]{1,0:T(8,128)(2,1)} %select_add_fusion.28), channel_id=1, source_target_pairs={{0,64},{64,128},{128,192},{192,256},{256,320},{320,384},{384,448},... | collective-permute-start | bytes 393224 | tf_op jit(solution)/shard_map/ppermute | solution.py:111
  (225 shorter events, 130.5 us)
Async XLA Ops:
  19.0 238.1 %reduce-scatter.2.cloned.1.call-start = ((), (), s32[]{:S(2)}) async-start(), calls=%async_computation.3 | async-start | bytes 196608 | tf_op jit(solution)/shard_map/reduce_scatter | solution.py:159
  23.5 49.3 %collective-permute-start = (bf16[32,2048]{1,0:T(8,128)(2,1)S(1)}, bf16[32,2048]{1,0:T(8,128)(2,1)S(1)}, u32[]{:S(2)}, u32[]{:S(2)}) collective-permute-start(bf16[32,2048]{1,0:T(8,128)(2,1)S(1)} %bitcast.50), channel_id=1, source_target_pairs={{0,8},{8,0},{1,9},{9,1},{2,10},{10,2},{3,11},{11,3},{4,12},{12,4},... | collective-permute-start | bytes 393224 | tf_op jit(solution)/shard_map/ppermute | solution.py:30
  72.8 15.0 %collective-permute-start.1 = (bf16[64,2048]{1,0:T(8,128)(2,1)S(1)}, bf16[64,2048]{1,0:T(8,128)(2,1)S(1)}, u32[]{:S(2)}, u32[]{:S(2)}) collective-permute-start(bf16[64,2048]{1,0:T(8,128)(2,1)S(1)} %pad_maximum_fusion.1), channel_id=1, source_target_pairs={{0,6},{2,0},{4,2},{6,4},{1,7},{3,1},{5,3},{7,5},{8,14},{10,8},{12,... | collective-permute-start | bytes 786440 | tf_op jit(solution)/shard_map/ppermute | solution.py:34
  78.5 12.6 %collective-permute-start.2 = (bf16[64,2048]{1,0:T(8,128)(2,1)S(1)}, bf16[64,2048]{1,0:T(8,128)(2,1)S(1)}, u32[]{:S(2)}, u32[]{:S(2)}) collective-permute-start(bf16[64,2048]{1,0:T(8,128)(2,1)S(1)} %pad_maximum_fusion.1), channel_id=1, source_target_pairs={{0,4},{2,6},{4,0},{6,2},{1,5},{3,7},{5,1},{7,3},{8,12},{10,14},{12... | collective-permute-start | bytes 786440 | tf_op jit(solution)/shard_map/ppermute | solution.py:34
  81.0 13.2 %collective-permute-start.3 = (bf16[64,2048]{1,0:T(8,128)(2,1)S(1)}, bf16[64,2048]{1,0:T(8,128)(2,1)S(1)}, u32[]{:S(2)}, u32[]{:S(2)}) collective-permute-start(bf16[64,2048]{1,0:T(8,128)(2,1)S(1)} %pad_maximum_fusion.1), channel_id=1, source_target_pairs={{0,2},{2,4},{4,6},{6,0},{1,3},{3,5},{5,7},{7,1},{8,10},{10,12},{12... | collective-permute-start | bytes 786440 | tf_op jit(solution)/shard_map/ppermute | solution.py:34
  113.7 13.3 %collective-permute-start.10 = (bf16[256,1024]{1,0:T(8,128)(2,1)S(1)}, bf16[256,1024]{1,0:T(8,128)(2,1)S(1)}, u32[]{:S(2)}, u32[]{:S(2)}) collective-permute-start(bf16[256,1024]{1,0:T(8,128)(2,1)S(1)} %pad_maximum_fusion), channel_id=1, source_target_pairs={{0,1},{1,0},{2,3},{3,2},{4,5},{5,4},{6,7},{7,6},{8,9},{9,8},{10,11... | collective-permute-start | bytes 1572872 | tf_op jit(solution)/shard_map/ppermute | solution.py:30
  118.6 14.2 %collective-permute-start.9 = (bf16[32,2048]{1,0:T(8,128)(2,1)S(1)}, bf16[32,2048]{1,0:T(8,128)(2,1)S(1)}, u32[]{:S(2)}, u32[]{:S(2)}) collective-permute-start(bf16[32,2048]{1,0:T(8,128)(2,1)S(1)} %get-tuple-element.122), channel_id=1, source_target_pairs={{0,4},{2,6},{4,0},{6,2},{1,5},{3,7},{5,1},{7,3},{8,12},{10,14},{12... | collective-permute-start | bytes 393224 | tf_op jit(solution)/shard_map/ppermute | solution.py:34
  121.1 13.6 %collective-permute-start.8 = (bf16[32,2048]{1,0:T(8,128)(2,1)S(1)}, bf16[32,2048]{1,0:T(8,128)(2,1)S(1)}, u32[]{:S(2)}, u32[]{:S(2)}) collective-permute-start(bf16[32,2048]{1,0:T(8,128)(2,1)S(1)} %get-tuple-element.123), channel_id=1, source_target_pairs={{0,6},{2,0},{4,2},{6,4},{1,7},{3,1},{5,3},{7,5},{8,14},{10,8},{12,... | collective-permute-start | bytes 393224 | tf_op jit(solution)/shard_map/ppermute | solution.py:34
  124.2 10.5 %collective-permute-start.7 = (bf16[32,2048]{1,0:T(8,128)(2,1)S(1)}, bf16[32,2048]{1,0:T(8,128)(2,1)S(1)}, u32[]{:S(2)}, u32[]{:S(2)}) collective-permute-start(bf16[32,2048]{1,0:T(8,128)(2,1)S(1)} %get-tuple-element.121), channel_id=1, source_target_pairs={{0,2},{2,4},{4,6},{6,0},{1,3},{3,5},{5,7},{7,1},{8,10},{10,12},{12... | collective-permute-start | bytes 393224 | tf_op jit(solution)/shard_map/ppermute | solution.py:34
  128.7 13.7 %collective-permute-start.12 = (bf16[128,768]{1,0:T(8,128)(2,1)S(1)}, bf16[128,768]{1,0:T(8,128)(2,1)S(1)}, u32[]{:S(2)}, u32[]{:S(2)}) collective-permute-start(bf16[128,768]{1,0:T(8,128)(2,1)S(1)} %fusion.29), channel_id=1, source_target_pairs={{0,64},{64,128},{128,192},{192,256},{256,320},{320,384},{384,448},... | collective-permute-start | bytes 589832 | tf_op jit(solution)/shard_map/ppermute | solution.py:111
  130.8 13.6 %collective-permute-start.11 = (bf16[128,512]{1,0:T(8,128)(2,1)S(1)}, bf16[128,512]{1,0:T(8,128)(2,1)S(1)}, u32[]{:S(2)}, u32[]{:S(2)}) collective-permute-start(bf16[128,512]{1,0:T(8,128)(2,1)S(1)} %select_add_fusion.41), channel_id=1, source_target_pairs={{0,64},{64,128},{128,192},{192,256},{256,320},{320,384},{384,448},... | collective-permute-start | bytes 393224 | tf_op jit(solution)/shard_map/ppermute | solution.py:111
  142.5 11.7 %collective-permute-start.15 = (bf16[128,768]{1,0:T(8,128)(2,1)S(1)}, bf16[128,768]{1,0:T(8,128)(2,1)S(1)}, u32[]{:S(2)}, u32[]{:S(2)}) collective-permute-start(bf16[128,768]{1,0:T(8,128)(2,1)S(1)} %select_add_fusion.26), channel_id=1, source_target_pairs={{0,64},{64,128},{128,192},{192,256},{256,320},{320,384},{384,448},... | collective-permute-start | bytes 589832 | tf_op jit(solution)/shard_map/ppermute | solution.py:111
  144.5 10.5 %collective-permute-start.14 = (bf16[128,512]{1,0:T(8,128)(2,1)S(1)}, bf16[128,512]{1,0:T(8,128)(2,1)S(1)}, u32[]{:S(2)}, u32[]{:S(2)}) collective-permute-start(bf16[128,512]{1,0:T(8,128)(2,1)S(1)} %select_add_fusion.40), channel_id=1, source_target_pairs={{0,64},{64,128},{128,192},{192,256},{256,320},{320,384},{384,448},... | collective-permute-start | bytes 393224 | tf_op jit(solution)/shard_map/ppermute | solution.py:111
  149.0 15.1 %collective-permute-start.19 = (bf16[128,768]{1,0:T(8,128)(2,1)S(1)}, bf16[128,768]{1,0:T(8,128)(2,1)S(1)}, u32[]{:S(2)}, u32[]{:S(2)}) collective-permute-start(bf16[128,768]{1,0:T(8,128)(2,1)S(1)} %select_add_fusion.25), channel_id=1, source_target_pairs={{0,64},{64,128},{128,192},{192,256},{256,320},{320,384},{384,448},... | collective-permute-start | bytes 589832 | tf_op jit(solution)/shard_map/ppermute | solution.py:111
  165.3 16.7 %collective-permute-start.22 = (bf16[128,768]{1,0:T(8,128)(2,1)S(1)}, bf16[128,768]{1,0:T(8,128)(2,1)S(1)}, u32[]{:S(2)}, u32[]{:S(2)}) collective-permute-start(bf16[128,768]{1,0:T(8,128)(2,1)S(1)} %select_add_fusion.23), channel_id=1, source_target_pairs={{0,64},{64,128},{128,192},{192,256},{256,320},{320,384},{384,448},... | collective-permute-start | bytes 589832 | tf_op jit(solution)/shard_map/ppermute | solution.py:111
  171.8 12.5 %collective-permute-start.21 = (bf16[128,768]{1,0:T(8,128)(2,1)S(1)}, bf16[128,768]{1,0:T(8,128)(2,1)S(1)}, u32[]{:S(2)}, u32[]{:S(2)}) collective-permute-start(bf16[128,768]{1,0:T(8,128)(2,1)S(1)} %select_add_fusion.22), channel_id=1, source_target_pairs={{0,64},{64,128},{128,192},{192,256},{256,320},{320,384},{384,448},... | collective-permute-start | bytes 589832 | tf_op jit(solution)/shard_map/ppermute | solution.py:111
  177.6 11.5 %collective-permute-start.20 = (bf16[128,512]{1,0:T(8,128)(2,1)S(1)}, bf16[128,512]{1,0:T(8,128)(2,1)S(1)}, u32[]{:S(2)}, u32[]{:S(2)}) collective-permute-start(bf16[128,512]{1,0:T(8,128)(2,1)S(1)} %select_add_fusion.38), channel_id=1, source_target_pairs={{0,64},{64,128},{128,192},{192,256},{256,320},{320,384},{384,448},... | collective-permute-start | bytes 393224 | tf_op jit(solution)/shard_map/ppermute | solution.py:111
  184.4 11.8 %collective-permute-start.24 = (bf16[128,768]{1,0:T(8,128)(2,1)S(1)}, bf16[128,768]{1,0:T(8,128)(2,1)S(1)}, u32[]{:S(2)}, u32[]{:S(2)}) collective-permute-start(bf16[128,768]{1,0:T(8,128)(2,1)S(1)} %select_add_fusion.20), channel_id=1, source_target_pairs={{0,64},{64,128},{128,192},{192,256},{256,320},{320,384},{384,448},... | collective-permute-start | bytes 589832 | tf_op jit(solution)/shard_map/ppermute | solution.py:111
  191.2 12.5 %collective-permute-start.28 = (bf16[128,768]{1,0:T(8,128)(2,1)S(1)}, bf16[128,768]{1,0:T(8,128)(2,1)S(1)}, u32[]{:S(2)}, u32[]{:S(2)}) collective-permute-start(bf16[128,768]{1,0:T(8,128)(2,1)S(1)} %select_add_fusion.19), channel_id=1, source_target_pairs={{0,64},{64,128},{128,192},{192,256},{256,320},{320,384},{384,448},... | collective-permute-start | bytes 589832 | tf_op jit(solution)/shard_map/ppermute | solution.py:111
  196.3 12.7 %collective-permute-start.27 = (bf16[128,768]{1,0:T(8,128)(2,1)S(1)}, bf16[128,768]{1,0:T(8,128)(2,1)S(1)}, u32[]{:S(2)}, u32[]{:S(2)}) collective-permute-start(bf16[128,768]{1,0:T(8,128)(2,1)S(1)} %select_add_fusion.18), channel_id=1, source_target_pairs={{0,64},{64,128},{128,192},{192,256},{256,320},{320,384},{384,448},... | collective-permute-start | bytes 589832 | tf_op jit(solution)/shard_map/ppermute | solution.py:111
  199.2 12.6 %collective-permute-start.26 = (bf16[128,512]{1,0:T(8,128)(2,1)S(1)}, bf16[128,512]{1,0:T(8,128)(2,1)S(1)}, u32[]{:S(2)}, u32[]{:S(2)}) collective-permute-start(bf16[128,512]{1,0:T(8,128)(2,1)S(1)} %select_add_fusion.36), channel_id=1, source_target_pairs={{0,64},{64,128},{128,192},{192,256},{256,320},{320,384},{384,448},... | collective-permute-start | bytes 393224 | tf_op jit(solution)/shard_map/ppermute | solution.py:111
  203.8 12.7 %collective-permute-start.31 = (bf16[128,768]{1,0:T(8,128)(2,1)S(1)}, bf16[128,768]{1,0:T(8,128)(2,1)S(1)}, u32[]{:S(2)}, u32[]{:S(2)}) collective-permute-start(bf16[128,768]{1,0:T(8,128)(2,1)S(1)} %select_add_fusion.17), channel_id=1, source_target_pairs={{0,64},{64,128},{128,192},{192,256},{256,320},{320,384},{384,448},... | collective-permute-start | bytes 589832 | tf_op jit(solution)/shard_map/ppermute | solution.py:111
  209.2 11.8 %collective-permute-start.30 = (bf16[128,768]{1,0:T(8,128)(2,1)S(1)}, bf16[128,768]{1,0:T(8,128)(2,1)S(1)}, u32[]{:S(2)}, u32[]{:S(2)}) collective-permute-start(bf16[128,768]{1,0:T(8,128)(2,1)S(1)} %select_add_fusion.16), channel_id=1, source_target_pairs={{0,64},{64,128},{128,192},{192,256},{256,320},{320,384},{384,448},... | collective-permute-start | bytes 589832 | tf_op jit(solution)/shard_map/ppermute | solution.py:111
  211.8 13.3 %collective-permute-start.29 = (bf16[128,512]{1,0:T(8,128)(2,1)S(1)}, bf16[128,512]{1,0:T(8,128)(2,1)S(1)}, u32[]{:S(2)}, u32[]{:S(2)}) collective-permute-start(bf16[128,512]{1,0:T(8,128)(2,1)S(1)} %select_add_fusion.35), channel_id=1, source_target_pairs={{0,64},{64,128},{128,192},{192,256},{256,320},{320,384},{384,448},... | collective-permute-start | bytes 393224 | tf_op jit(solution)/shard_map/ppermute | solution.py:111
  216.6 10.7 %collective-permute-start.34 = (bf16[128,768]{1,0:T(8,128)(2,1)S(1)}, bf16[128,768]{1,0:T(8,128)(2,1)S(1)}, u32[]{:S(2)}, u32[]{:S(2)}) collective-permute-start(bf16[128,768]{1,0:T(8,128)(2,1)S(1)} %select_add_fusion.15), channel_id=1, source_target_pairs={{0,64},{64,128},{128,192},{192,256},{256,320},{320,384},{384,448},... | collective-permute-start | bytes 589832 | tf_op jit(solution)/shard_map/ppermute | solution.py:111
  221.1 10.2 %collective-permute-start.33 = (bf16[128,768]{1,0:T(8,128)(2,1)S(1)}, bf16[128,768]{1,0:T(8,128)(2,1)S(1)}, u32[]{:S(2)}, u32[]{:S(2)}) collective-permute-start(bf16[128,768]{1,0:T(8,128)(2,1)S(1)} %select_add_fusion.14), channel_id=1, source_target_pairs={{0,64},{64,128},{128,192},{192,256},{256,320},{320,384},{384,448},... | collective-permute-start | bytes 589832 | tf_op jit(solution)/shard_map/ppermute | solution.py:111
  233.4 11.4 %collective-permute-start.35 = (bf16[128,512]{1,0:T(8,128)(2,1)S(1)}, bf16[128,512]{1,0:T(8,128)(2,1)S(1)}, u32[]{:S(2)}, u32[]{:S(2)}) collective-permute-start(bf16[128,512]{1,0:T(8,128)(2,1)S(1)} %select_add_fusion.33), channel_id=1, source_target_pairs={{0,64},{64,128},{128,192},{192,256},{256,320},{320,384},{384,448},... | collective-permute-start | bytes 393224 | tf_op jit(solution)/shard_map/ppermute | solution.py:111
  247.0 12.6 %collective-permute-start.43 = (bf16[128,768]{1,0:T(8,128)(2,1)S(1)}, bf16[128,768]{1,0:T(8,128)(2,1)S(1)}, u32[]{:S(2)}, u32[]{:S(2)}) collective-permute-start(bf16[128,768]{1,0:T(8,128)(2,1)S(1)} %select_add_fusion.9), channel_id=1, source_target_pairs={{0,64},{64,128},{128,192},{192,256},{256,320},{320,384},{384,448},... | collective-permute-start | bytes 589832 | tf_op jit(solution)/shard_map/ppermute | solution.py:111
  260.7 13.4 %collective-permute-start.46 = (bf16[128,768]{1,0:T(8,128)(2,1)S(1)}, bf16[128,768]{1,0:T(8,128)(2,1)S(1)}, u32[]{:S(2)}, u32[]{:S(2)}) collective-permute-start(bf16[128,768]{1,0:T(8,128)(2,1)S(1)} %select_add_fusion.7), channel_id=1, source_target_pairs={{0,64},{64,128},{128,192},{192,256},{256,320},{320,384},{384,448},... | collective-permute-start | bytes 589832 | tf_op jit(solution)/shard_map/ppermute | solution.py:111
  264.9 11.2 %collective-permute-start.45 = (bf16[128,768]{1,0:T(8,128)(2,1)S(1)}, bf16[128,768]{1,0:T(8,128)(2,1)S(1)}, u32[]{:S(2)}, u32[]{:S(2)}) collective-permute-start(bf16[128,768]{1,0:T(8,128)(2,1)S(1)} %select_add_fusion.6), channel_id=1, source_target_pairs={{0,64},{64,128},{128,192},{192,256},{256,320},{320,384},{384,448},... | collective-permute-start | bytes 589832 | tf_op jit(solution)/shard_map/ppermute | solution.py:111
  289.8 15.8 %collective-permute-start.52 = (bf16[128,768]{1,0:T(8,128)(2,1)S(1)}, bf16[128,768]{1,0:T(8,128)(2,1)S(1)}, u32[]{:S(2)}, u32[]{:S(2)}) collective-permute-start(bf16[128,768]{1,0:T(8,128)(2,1)S(1)} %select_add_fusion.1), channel_id=1, source_target_pairs={{0,64},{64,128},{128,192},{192,256},{256,320},{320,384},{384,448},... | collective-permute-start | bytes 589832 | tf_op jit(solution)/shard_map/ppermute | solution.py:111
  294.4 11.2 %collective-permute-start.54 = (bf16[128,768]{1,0:T(8,128)(2,1)}, bf16[128,768]{1,0:T(8,128)(2,1)S(1)}, u32[]{:S(2)}, u32[]{:S(2)}) collective-permute-start(bf16[128,768]{1,0:T(8,128)(2,1)} %select_add_fusion), channel_id=1, source_target_pairs={{0,64},{64,128},{128,192},{192,256},{256,320},{320,384},{384,448},... | collective-permute-start | bytes 589832 | tf_op jit(solution)/shard_map/ppermute | solution.py:111
  (43 other events, 563.7 us)
Sparse Core Ops, SparseCore 0:
  164.2 54.8 reduce-scatter.1

commit v5 on v4

--- a/solution.py
+++ b/solution.py
@@ -68,7 +68,7 @@
 def gather_plane(rows):
     pieces = [rows, shift(rows, 3), shift(rows, 2), shift(rows, 1)]
     own = jnp.concatenate(pieces, axis=0)
-    return jnp.concatenate([own, swap(own, "core")], axis=0)
+    return own, swap(own, "core")
 
 
 def row_order(n_rows, kind):
@@ -79,11 +79,12 @@
     return (at == source).astype(jnp.bfloat16)
 
 
-def expert_part(x_rows, g_rows, w_in, w_out):
-    pre_act = dot_f32(x_rows, w_in, ((1,), (0,)))
-    value, slope = gelu_pair(pre_act)
-    back_hid = dot_f32(g_rows, w_out, ((1,), (1,)))
-    return value.astype(jnp.bfloat16), (back_hid * slope).astype(jnp.bfloat16)
+def home_order(n_rows):
+    to = lax.broadcasted_iota(jnp.int32, (n_rows, n_rows), 0)
+    at = lax.broadcasted_iota(jnp.int32, (n_rows, n_rows), 1)
+    zh = (to // CAP - lax.axis_index("zh")) & 1
+    source = zh * 16 + to // (2 * CAP) * CAP + (to & (CAP - 1))
+    return (at == source).astype(jnp.bfloat16)
 
 
 def block_of(rows, begin, height):
@@ -125,64 +126,58 @@
     far, order_x, order_g = lax.optimization_barrier(
         (swap(got, "zh"), row_order(64 * CAP, 0), row_order(64 * CAP, 1))
     )
-    rows = gather_plane(jnp.concatenate([got, far], axis=0))
-    x_all = dot_f32(order_x, rows, ((1,), (0,))).astype(jnp.bfloat16)
-    g_all = dot_f32(order_g, rows, ((1,), (0,))).astype(jnp.bfloat16)
-    hidden, hid_grad = expert_part(x_all, g_all, w_in, w_out)
-    other = swap(jnp.concatenate([hid_grad, hidden], axis=1), "core")
+    own, across = gather_plane(jnp.concatenate([got, far], axis=0))
+
+    def in_order(order):
+        half = order.shape[1] // 2
+        total = dot_f32(order[:, :half], own, ((1,), (0,)))
+        return (total + dot_f32(order[:, half:], across, ((1,), (0,)))).astype(jnp.bfloat16)
+
+    x_all, g_all = in_order(order_x), in_order(order_g)
+    pre_act = dot_f32(x_all, w_in, ((1,), (0,)))
+    value, slope = gelu_pair(pre_act)
+    hidden = value.astype(jnp.bfloat16)
+    hidden_both = jnp.concatenate([hidden, swap(hidden, "core")], axis=1)
+    back_hid = dot_f32(g_all, w_out, ((1,), (1,)))
+    hid_grad = (back_hid * slope).astype(jnp.bfloat16)
     partial = dot_f32(hid_grad, w_in, ((1,), (1,))).astype(jnp.bfloat16)
 
     def product(rows, units):
         return dot_f32(rows, units, ((0,), (0,))).astype(jnp.bfloat16)
 
-    cut = ff_dev // 2
-    own_in = product(x_all, hid_grad)
-    own_out = product(g_all, hidden)
-    other_in = product(x_all, other[:, :ff_dev])
-    other_out = product(g_all, other[:, ff_dev:])
-    streams = [
-        own_in,
-        jnp.concatenate([own_out, other_in[:, :cut]], axis=1),
-        jnp.concatenate([other_in[:, cut:], other_out], axis=1),
-    ]
+    hid_grad_both = jnp.concatenate([hid_grad, swap(hid_grad, "core")], axis=1)
+    grad_out = product(g_all, hidden_both)
+    grad_in = product(x_all, hid_grad_both)
 
     def along_y(rows):
         parts = rows.reshape(4, -1, d_model)
         total = parts[0].astype(jnp.float32)
         for by in (1, 3, 2):
             total = total + shift(parts[by], by).astype(jnp.float32)
-        total = total.astype(jnp.bfloat16)
-        turned = jnp.concatenate([total[4 * CAP :], total[: 4 * CAP]], axis=0)
-        return jnp.where(lax.axis_index("zh") == 0, total, turned)
-
-    def across_zh(rows):
-        return lax.psum_scatter(rows, "zh", scatter_dimension=0, tiled=True)
-
-    def along_x(rows):
-        parts = rows.reshape(4, CAP, d_model)
-        return lax.all_to_all(parts, "x", 0, 0, tiled=True).reshape(4 * CAP, d_model)
+        return total.astype(jnp.bfloat16)
+
+    def home(rows):
+        parts = dot_f32(home_order(rows.shape[0]), rows, ((1,), (0,))).astype(jnp.bfloat16)
+        parts = parts.reshape(8, CAP, d_model)
+        return lax.all_to_all(parts, ("x", "zh"), 0, 0, tiled=True).reshape(8 * CAP, d_model)
 
     core, half = lax.axis_index("core"), partial.shape[0] // 2
     given = swap(block_of(partial, (1 - core) * half, half), "core").astype(jnp.float32)
     given = (block_of(partial, core * half, half).astype(jnp.float32) + given).astype(jnp.bfloat16)
-    sel_slots = sel.reshape(4, 2, CAP, n_tok)[:, 0].reshape(4 * CAP, n_tok)
-
-    def to_tokens(rows):
-        return dot_f32(sel_slots, rows, ((0,), (0,))).astype(jnp.bfloat16)
-
-    sums, in_grad = line_sums(
-        streams, n_group, given, {0: along_y, 3: across_zh, 11: along_x, 14: to_tokens}
-    )
+    sums, slots = line_sums(
+        [grad_out, grad_in], n_group, given, {0: along_y, 3: lambda rows: rows, 11: home}
+    )
+    in_grad = dot_f32(sel, slots, ((0,), (0,))).astype(jnp.bfloat16)
     width = d_model // n_group
     here = lax.axis_index("group") * width
-    across = swap(jnp.concatenate([sums[1][:, ff_dev:], sums[2]], axis=1), "core")
+    across = [swap(carried[:, ff_dev:], "core") for carried in sums]
 
     def total(own, carried, given):
-        parts = (block_of(own, here, width), carried, given)
+        parts = (block_of(own, here, width)[:, :ff_dev], carried[:, :ff_dev], given)
         return sum(part.astype(jnp.float32) for part in parts).astype(jnp.bfloat16)
 
-    w_in_grad = total(own_in, sums[0], across[:, :ff_dev])
-    w_out_grad = total(own_out, sums[1][:, :ff_dev], across[:, ff_dev:])
+    w_out_grad = total(grad_out, sums[0], across[0])
+    w_in_grad = total(grad_in, sums[1], across[1])
     return in_grad, w_in_grad, w_out_grad.T
 
 

time: 322 us -> 304 us (0.944)
  the two profiles are of different devices: /device:TPU:34 before, /device:TPU:35 now
where the time goes in v5:
time: 304 us; the launch traced here: 302 us
  starting transfers between devices  160 us (53%)
  waiting for transfers between devices  86.4 us (28%)
  other arithmetic  33.6 us (11%)
  matrix products  16.6 us (5%)
    ppermute x30, starting transfers between devices, line_sums(): carried[k], last = (lax.ppermute(term, ('group', 'core'), pairs), term)  58.1 us
    ppermute x7, starting transfers between devices, swap(): return lax.ppermute(value, axis, [(0, 1), (1, 0)])  57.8 us
    ppermute x30, waiting for transfers between devices, line_sums(): carried[k], last = (lax.ppermute(term, ('group', 'core'), pairs), term)  48.2 us
    add x28, other arithmetic, line_sums(): term + jnp.where(rank <= step, carried[k], jnp.zeros_like(carried[k]))  28.2 us
    ppermute x7, waiting for transfers between devices, swap(): return lax.ppermute(value, axis, [(0, 1), (1, 0)])  23.1 us
    all_to_all x1, starting transfers between devices, home(): lax.all_to_all(parts, ('x', 'zh'), 0, 0, tiled=True)  22.9 us
    ppermute x6, starting transfers between devices, shift(): return lax.ppermute(value, 'y', [(i, (i + by) % 4) for i in range(4)])  17 us
    dot_general x15, matrix products, dot_f32(): lax.dot_general(a, b, (dims, ((), ())), preferred_element_type=jnp.float32)  16.6 us
  transfers between devices with their start and end apart: 45, of which 27 were waited for; matrix products, arithmetic and copies ran while one was open for 13% of the time, Pallas kernels for 0%

profile of v5, /device:TPU:35, one launch (start us, length us, event | category | flops | bytes accessed | tf_op | source)
XLA Modules:
  0.0 301.6 jit_solution(11358134745842537508)
XLA Ops:
  8.2 4.3 %all-to-all-start = ((bf16[4,8,2048]{2,1,0:T(8,128)(2,1)}), bf16[4,8,2048]{2,1,0:T(8,128)(2,1)S(1)}, u32[]{:S(2)}, u32[]{:S(2)}) async-start(bf16[4,8,2048]{2,1,0:T(8,128)(2,1)} %fusion.4), calls=%async_computation | async-start | bytes 262144 | tf_op jit(solution)/shard_map/all_to_all | solution.py:124
  12.5 3.6 %all-to-all-done = bf16[4,8,2048]{2,1,0:T(8,128)(2,1)S(1)} async-done(((bf16[4,8,2048]{2,1,0:T(8,128)(2,1)}), bf16[4,8,2048]{2,1,0:T(8,128)(2,1)S(1)}, u32[]{:S(2)}, u32[]{:S(2)}) %all-to-all-start) | async-done | bytes 131104 | tf_op jit(solution)/shard_map/all_to_all | solution.py:124
  16.1 27.8 %collective-permute-start = (bf16[32,2048]{1,0:T(8,128)(2,1)S(1)}, bf16[32,2048]{1,0:T(8,128)(2,1)S(1)}, u32[]{:S(2)}, u32[]{:S(2)}) collective-permute-start(bf16[32,2048]{1,0:T(8,128)(2,1)S(1)} %bitcast.46), channel_id=1, source_target_pairs={{0,8},{8,0},{1,9},{9,1},{2,10},{10,2},{3,11},{11,3},{4,12},{12,4},... | collective-permute-start | bytes 393224 | tf_op jit(solution)/shard_map/ppermute | solution.py:30
  45.0 20.7 %collective-permute-done = bf16[32,2048]{1,0:T(8,128)(2,1)S(1)} collective-permute-done((bf16[32,2048]{1,0:T(8,128)(2,1)S(1)}, bf16[32,2048]{1,0:T(8,128)(2,1)S(1)}, u32[]{:S(2)}, u32[]{:S(2)}) %collective-permute-start) | collective-permute-done | bytes 131104 | tf_op jit(solution)/shard_map/ppermute | solution.py:30
  65.7 4.6 %collective-permute-start.1 = (bf16[64,2048]{1,0:T(8,128)(2,1)S(1)}, bf16[64,2048]{1,0:T(8,128)(2,1)S(1)}, u32[]{:S(2)}, u32[]{:S(2)}) collective-permute-start(bf16[64,2048]{1,0:T(8,128)(2,1)S(1)} %pad_maximum_fusion), channel_id=1, source_target_pairs={{0,6},{2,0},{4,2},{6,4},{1,7},{3,1},{5,3},{7,5},{8,14},{10,8},{12,... | collective-permute-start | bytes 786440 | tf_op jit(solution)/shard_map/ppermute | solution.py:34
  70.4 2.3 collective-permute-start.2
  72.7 2.6 collective-permute-start.3
  75.3 4.2 %collective-permute-done.2 = bf16[64,2048]{1,0:T(8,128)(2,1)S(1)} collective-permute-done((bf16[64,2048]{1,0:T(8,128)(2,1)S(1)}, bf16[64,2048]{1,0:T(8,128)(2,1)S(1)}, u32[]{:S(2)}, u32[]{:S(2)}) %collective-permute-start.2) | collective-permute-done | bytes 262176 | tf_op jit(solution)/shard_map/ppermute | solution.py:34
  79.6 7.2 %collective-permute-done.3 = bf16[64,2048]{1,0:T(8,128)(2,1)S(1)} collective-permute-done((bf16[64,2048]{1,0:T(8,128)(2,1)S(1)}, bf16[64,2048]{1,0:T(8,128)(2,1)S(1)}, u32[]{:S(2)}, u32[]{:S(2)}) %collective-permute-start.3) | collective-permute-done | bytes 262176 | tf_op jit(solution)/shard_map/ppermute | solution.py:34
  86.8 3.2 %collective-permute-start.4 = (bf16[256,2048]{1,0:T(8,128)(2,1)S(1)}, bf16[256,2048]{1,0:T(8,128)(2,1)}, u32[]{:S(2)}, u32[]{:S(2)}) collective-permute-start(bf16[256,2048]{1,0:T(8,128)(2,1)S(1)} %constant_dynamic-update-slice_fusion), channel_id=1, source_target_pairs={{0,1},{1,0},{2,3},{3,2},{4,5},{5,4},{6,7},{7,6},{8,9},{9,8},{10,11... | collective-permute-start | bytes 3145736 | tf_op jit(solution)/shard_map/ppermute | solution.py:30
  90.1 2.4 collective-permute-done.4
  98.6 2.3 collective-permute-start.6
  104.7 2.3 collective-permute-start.5
  121.2 2.1 collective-permute-done.12
  129.8 2.3 collective-permute-start.10
  132.1 2.8 collective-permute-start.9
  134.9 2.5 collective-permute-start.8
  146.7 2.2 collective-permute-start.18
  152.0 2.1 collective-permute-done.18
  160.4 2.8 collective-permute-done.20
  169.5 3.1 %collective-permute-done.22 = bf16[128,1024]{1,0:T(8,128)(2,1)S(1)} collective-permute-done((bf16[128,1024]{1,0:T(8,128)(2,1)S(1)}, bf16[128,1024]{1,0:T(8,128)(2,1)S(1)}, u32[]{:S(2)}, u32[]{:S(2)}) %collective-permute-start.22) | collective-permute-done | bytes 262176 | tf_op jit(solution)/shard_map/ppermute | solution.py:112
  173.7 2.1 collective-permute-start.24
  179.2 3.1 %collective-permute-done.24 = bf16[128,1024]{1,0:T(8,128)(2,1)S(1)} collective-permute-done((bf16[128,1024]{1,0:T(8,128)(2,1)S(1)}, bf16[128,1024]{1,0:T(8,128)(2,1)S(1)}, u32[]{:S(2)}, u32[]{:S(2)}) %collective-permute-start.24) | collective-permute-done | bytes 262176 | tf_op jit(solution)/shard_map/ppermute | solution.py:112
  188.4 3.1 %collective-permute-done.26 = bf16[128,1024]{1,0:T(8,128)(2,1)S(1)} collective-permute-done((bf16[128,1024]{1,0:T(8,128)(2,1)S(1)}, bf16[128,1024]{1,0:T(8,128)(2,1)S(1)}, u32[]{:S(2)}, u32[]{:S(2)}) %collective-permute-start.26) | collective-permute-done | bytes 262176 | tf_op jit(solution)/shard_map/ppermute | solution.py:112
  197.8 3.1 %collective-permute-done.28 = bf16[128,1024]{1,0:T(8,128)(2,1)S(1)} collective-permute-done((bf16[128,1024]{1,0:T(8,128)(2,1)S(1)}, bf16[128,1024]{1,0:T(8,128)(2,1)S(1)}, u32[]{:S(2)}, u32[]{:S(2)}) %collective-permute-start.28) | collective-permute-done | bytes 262176 | tf_op jit(solution)/shard_map/ppermute | solution.py:112
  207.2 3.0 collective-permute-done.30
  216.6 3.4 %collective-permute-done.32 = bf16[128,1024]{1,0:T(8,128)(2,1)S(1)} collective-permute-done((bf16[128,1024]{1,0:T(8,128)(2,1)S(1)}, bf16[128,1024]{1,0:T(8,128)(2,1)S(1)}, u32[]{:S(2)}, u32[]{:S(2)}) %collective-permute-start.32) | collective-permute-done | bytes 262176 | tf_op jit(solution)/shard_map/ppermute | solution.py:112
  227.0 22.9 %all-to-all-start.1 = ((bf16[8,4,2048]{2,1,0:T(4,128)(2,1)}), bf16[8,4,2048]{2,1,0:T(4,128)(2,1)S(1)}, u32[]{:S(2)}, u32[]{:S(2)}) async-start(bf16[8,4,2048]{2,1,0:T(4,128)(2,1)} %reshape.277), calls=%async_computation.1 | async-start | bytes 262144 | tf_op jit(solution)/shard_map/all_to_all | solution.py:162
  256.0 7.5 %collective-permute-done.38 = bf16[128,1024]{1,0:T(8,128)(2,1)S(1)} collective-permute-done((bf16[128,1024]{1,0:T(8,128)(2,1)S(1)}, bf16[128,1024]{1,0:T(8,128)(2,1)S(1)}, u32[]{:S(2)}, u32[]{:S(2)}) %collective-permute-start.38) | collective-permute-done | bytes 262176 | tf_op jit(solution)/shard_map/ppermute | solution.py:112
  271.3 5.4 %collective-permute-done.39 = bf16[128,1024]{1,0:T(8,128)(2,1)S(1)} collective-permute-done((bf16[128,1024]{1,0:T(8,128)(2,1)S(1)}, bf16[128,1024]{1,0:T(8,128)(2,1)S(1)}, u32[]{:S(2)}, u32[]{:S(2)}) %collective-permute-start.39) | collective-permute-done | bytes 262176 | tf_op jit(solution)/shard_map/ppermute | solution.py:112
  276.7 17.4 %collective-permute-start.40 = (bf16[128,512]{1,0:T(8,128)(2,1)S(1)}, bf16[128,512]{1,0:T(8,128)(2,1)S(1)}, u32[]{:S(2)}, u32[]{:S(2)}) collective-permute-start(bf16[128,512]{1,0:T(8,128)(2,1)S(1)} %slice.69), channel_id=1, source_target_pairs={{0,1},{1,0},{2,3},{3,2},{4,5},{5,4},{6,7},{7,6},{8,9},{9,8},{10,11... | collective-permute-start | bytes 393224 | tf_op jit(solution)/shard_map/ppermute | solution.py:30
  294.2 2.8 collective-permute-start.42
  (170 shorter events, 118.6 us)
Async XLA Ops:
  16.1 49.6 %collective-permute-start = (bf16[32,2048]{1,0:T(8,128)(2,1)S(1)}, bf16[32,2048]{1,0:T(8,128)(2,1)S(1)}, u32[]{:S(2)}, u32[]{:S(2)}) collective-permute-start(bf16[32,2048]{1,0:T(8,128)(2,1)S(1)} %bitcast.46), channel_id=1, source_target_pairs={{0,8},{8,0},{1,9},{9,1},{2,10},{10,2},{3,11},{11,3},{4,12},{12,4},... | collective-permute-start | bytes 393224 | tf_op jit(solution)/shard_map/ppermute | solution.py:30
  65.7 9.6 %collective-permute-start.1 = (bf16[64,2048]{1,0:T(8,128)(2,1)S(1)}, bf16[64,2048]{1,0:T(8,128)(2,1)S(1)}, u32[]{:S(2)}, u32[]{:S(2)}) collective-permute-start(bf16[64,2048]{1,0:T(8,128)(2,1)S(1)} %pad_maximum_fusion), channel_id=1, source_target_pairs={{0,6},{2,0},{4,2},{6,4},{1,7},{3,1},{5,3},{7,5},{8,14},{10,8},{12,... | collective-permute-start | bytes 786440 | tf_op jit(solution)/shard_map/ppermute | solution.py:34
  70.4 9.2 %collective-permute-start.2 = (bf16[64,2048]{1,0:T(8,128)(2,1)S(1)}, bf16[64,2048]{1,0:T(8,128)(2,1)S(1)}, u32[]{:S(2)}, u32[]{:S(2)}) collective-permute-start(bf16[64,2048]{1,0:T(8,128)(2,1)S(1)} %pad_maximum_fusion), channel_id=1, source_target_pairs={{0,4},{2,6},{4,0},{6,2},{1,5},{3,7},{5,1},{7,3},{8,12},{10,14},{12... | collective-permute-start | bytes 786440 | tf_op jit(solution)/shard_map/ppermute | solution.py:34
  72.7 14.2 %collective-permute-start.3 = (bf16[64,2048]{1,0:T(8,128)(2,1)S(1)}, bf16[64,2048]{1,0:T(8,128)(2,1)S(1)}, u32[]{:S(2)}, u32[]{:S(2)}) collective-permute-start(bf16[64,2048]{1,0:T(8,128)(2,1)S(1)} %pad_maximum_fusion), channel_id=1, source_target_pairs={{0,2},{2,4},{4,6},{6,0},{1,3},{3,5},{5,7},{7,1},{8,10},{10,12},{12... | collective-permute-start | bytes 786440 | tf_op jit(solution)/shard_map/ppermute | solution.py:34
  98.6 8.4 %collective-permute-start.6 = (bf16[256,512]{1,0:T(8,128)(2,1)S(1)}, bf16[256,512]{1,0:T(8,128)(2,1)S(1)}, u32[]{:S(2)}, u32[]{:S(2)}) collective-permute-start(bf16[256,512]{1,0:T(8,128)(2,1)S(1)} %get-tuple-element.94), channel_id=1, source_target_pairs={{0,1},{1,0},{2,3},{3,2},{4,5},{5,4},{6,7},{7,6},{8,9},{9,8},{10,11... | collective-permute-start | bytes 786440 | tf_op jit(solution)/shard_map/ppermute | solution.py:30
  104.7 8.9 %collective-permute-start.5 = (bf16[128,2048]{1,0:T(8,128)(2,1)S(1)}, bf16[128,2048]{1,0:T(8,128)(2,1)S(1)}, u32[]{:S(2)}, u32[]{:S(2)}) collective-permute-start(bf16[128,2048]{1,0:T(8,128)(2,1)S(1)} %constant_dynamic-slice_fusion.2), channel_id=1, source_target_pairs={{0,1},{1,0},{2,3},{3,2},{4,5},{5,4},{6,7},{7,6},{8,9},{9,8},{10,11... | collective-permute-start | bytes 1572872 | tf_op jit(solution)/shard_map/ppermute | solution.py:30
  124.4 13.0 %collective-permute-start.14 = (bf16[128,1024]{1,0:T(8,128)(2,1)S(1)}, bf16[128,1024]{1,0:T(8,128)(2,1)S(1)}, u32[]{:S(2)}, u32[]{:S(2)}) collective-permute-start(bf16[128,1024]{1,0:T(8,128)(2,1)S(1)} %select_add_fusion.25), channel_id=1, source_target_pairs={{0,64},{64,128},{128,192},{192,256},{256,320},{320,384},{384,448},... | collective-permute-start | bytes 786440 | tf_op jit(solution)/shard_map/ppermute | solution.py:112
  127.9 12.6 %collective-permute-start.17 = (bf16[128,1024]{1,0:T(8,128)(2,1)S(1)}, bf16[128,1024]{1,0:T(8,128)(2,1)S(1)}, u32[]{:S(2)}, u32[]{:S(2)}) collective-permute-start(bf16[128,1024]{1,0:T(8,128)(2,1)S(1)} %select_add_fusion.24), channel_id=1, source_target_pairs={{0,64},{64,128},{128,192},{192,256},{256,320},{320,384},{384,448},... | collective-permute-start | bytes 786440 | tf_op jit(solution)/shard_map/ppermute | solution.py:112
  129.8 13.6 %collective-permute-start.10 = (bf16[32,2048]{1,0:T(8,128)(2,1)S(1)}, bf16[32,2048]{1,0:T(8,128)(2,1)S(1)}, u32[]{:S(2)}, u32[]{:S(2)}) collective-permute-start(bf16[32,2048]{1,0:T(8,128)(2,1)S(1)} %get-tuple-element.88), channel_id=1, source_target_pairs={{0,4},{2,6},{4,0},{6,2},{1,5},{3,7},{5,1},{7,3},{8,12},{10,14},{12... | collective-permute-start | bytes 393224 | tf_op jit(solution)/shard_map/ppermute | solution.py:34
  132.1 11.4 %collective-permute-start.9 = (bf16[32,2048]{1,0:T(8,128)(2,1)S(1)}, bf16[32,2048]{1,0:T(8,128)(2,1)S(1)}, u32[]{:S(2)}, u32[]{:S(2)}) collective-permute-start(bf16[32,2048]{1,0:T(8,128)(2,1)S(1)} %get-tuple-element.89), channel_id=1, source_target_pairs={{0,6},{2,0},{4,2},{6,4},{1,7},{3,1},{5,3},{7,5},{8,14},{10,8},{12,... | collective-permute-start | bytes 393224 | tf_op jit(solution)/shard_map/ppermute | solution.py:34
  134.9 8.6 %collective-permute-start.8 = (bf16[32,2048]{1,0:T(8,128)(2,1)S(1)}, bf16[32,2048]{1,0:T(8,128)(2,1)S(1)}, u32[]{:S(2)}, u32[]{:S(2)}) collective-permute-start(bf16[32,2048]{1,0:T(8,128)(2,1)S(1)} %get-tuple-element.87), channel_id=1, source_target_pairs={{0,2},{2,4},{4,6},{6,0},{1,3},{3,5},{5,7},{7,1},{8,10},{10,12},{12... | collective-permute-start | bytes 393224 | tf_op jit(solution)/shard_map/ppermute | solution.py:34
  158.5 8.0 %collective-permute-start.23 = (bf16[128,1024]{1,0:T(8,128)(2,1)S(1)}, bf16[128,1024]{1,0:T(8,128)(2,1)S(1)}, u32[]{:S(2)}, u32[]{:S(2)}) collective-permute-start(bf16[128,1024]{1,0:T(8,128)(2,1)S(1)} %select_add_fusion.18), channel_id=1, source_target_pairs={{0,64},{64,128},{128,192},{192,256},{256,320},{320,384},{384,448},... | collective-permute-start | bytes 786440 | tf_op jit(solution)/shard_map/ppermute | solution.py:112
  164.3 8.3 %collective-permute-start.22 = (bf16[128,1024]{1,0:T(8,128)(2,1)S(1)}, bf16[128,1024]{1,0:T(8,128)(2,1)S(1)}, u32[]{:S(2)}, u32[]{:S(2)}) collective-permute-start(bf16[128,1024]{1,0:T(8,128)(2,1)S(1)} %select_add_fusion.17), channel_id=1, source_target_pairs={{0,64},{64,128},{128,192},{192,256},{256,320},{320,384},{384,448},... | collective-permute-start | bytes 786440 | tf_op jit(solution)/shard_map/ppermute | solution.py:112
  167.6 8.6 %collective-permute-start.25 = (bf16[128,1024]{1,0:T(8,128)(2,1)S(1)}, bf16[128,1024]{1,0:T(8,128)(2,1)S(1)}, u32[]{:S(2)}, u32[]{:S(2)}) collective-permute-start(bf16[128,1024]{1,0:T(8,128)(2,1)S(1)} %select_add_fusion.16), channel_id=1, source_target_pairs={{0,64},{64,128},{128,192},{192,256},{256,320},{320,384},{384,448},... | collective-permute-start | bytes 786440 | tf_op jit(solution)/shard_map/ppermute | solution.py:112
  173.7 8.6 %collective-permute-start.24 = (bf16[128,1024]{1,0:T(8,128)(2,1)S(1)}, bf16[128,1024]{1,0:T(8,128)(2,1)S(1)}, u32[]{:S(2)}, u32[]{:S(2)}) collective-permute-start(bf16[128,1024]{1,0:T(8,128)(2,1)S(1)} %select_add_fusion.15), channel_id=1, source_target_pairs={{0,64},{64,128},{128,192},{192,256},{256,320},{320,384},{384,448},... | collective-permute-start | bytes 786440 | tf_op jit(solution)/shard_map/ppermute | solution.py:112
  177.3 8.0 %collective-permute-start.27 = (bf16[128,1024]{1,0:T(8,128)(2,1)S(1)}, bf16[128,1024]{1,0:T(8,128)(2,1)S(1)}, u32[]{:S(2)}, u32[]{:S(2)}) collective-permute-start(bf16[128,1024]{1,0:T(8,128)(2,1)S(1)} %select_add_fusion.14), channel_id=1, source_target_pairs={{0,64},{64,128},{128,192},{192,256},{256,320},{320,384},{384,448},... | collective-permute-start | bytes 786440 | tf_op jit(solution)/shard_map/ppermute | solution.py:112
  183.4 8.0 %collective-permute-start.26 = (bf16[128,1024]{1,0:T(8,128)(2,1)S(1)}, bf16[128,1024]{1,0:T(8,128)(2,1)S(1)}, u32[]{:S(2)}, u32[]{:S(2)}) collective-permute-start(bf16[128,1024]{1,0:T(8,128)(2,1)S(1)} %select_add_fusion.13), channel_id=1, source_target_pairs={{0,64},{64,128},{128,192},{192,256},{256,320},{320,384},{384,448},... | collective-permute-start | bytes 786440 | tf_op jit(solution)/shard_map/ppermute | solution.py:112
  186.4 8.3 %collective-permute-start.29 = (bf16[128,1024]{1,0:T(8,128)(2,1)S(1)}, bf16[128,1024]{1,0:T(8,128)(2,1)S(1)}, u32[]{:S(2)}, u32[]{:S(2)}) collective-permute-start(bf16[128,1024]{1,0:T(8,128)(2,1)S(1)} %select_add_fusion.12), channel_id=1, source_target_pairs={{0,64},{64,128},{128,192},{192,256},{256,320},{320,384},{384,448},... | collective-permute-start | bytes 786440 | tf_op jit(solution)/shard_map/ppermute | solution.py:112
  192.5 8.3 %collective-permute-start.28 = (bf16[128,1024]{1,0:T(8,128)(2,1)S(1)}, bf16[128,1024]{1,0:T(8,128)(2,1)S(1)}, u32[]{:S(2)}, u32[]{:S(2)}) collective-permute-start(bf16[128,1024]{1,0:T(8,128)(2,1)S(1)} %select_add_fusion.11), channel_id=1, source_target_pairs={{0,64},{64,128},{128,192},{192,256},{256,320},{320,384},{384,448},... | collective-permute-start | bytes 786440 | tf_op jit(solution)/shard_map/ppermute | solution.py:112
  195.8 8.3 %collective-permute-start.31 = (bf16[128,1024]{1,0:T(8,128)(2,1)S(1)}, bf16[128,1024]{1,0:T(8,128)(2,1)S(1)}, u32[]{:S(2)}, u32[]{:S(2)}) collective-permute-start(bf16[128,1024]{1,0:T(8,128)(2,1)S(1)} %select_add_fusion.10), channel_id=1, source_target_pairs={{0,64},{64,128},{128,192},{192,256},{256,320},{320,384},{384,448},... | collective-permute-start | bytes 786440 | tf_op jit(solution)/shard_map/ppermute | solution.py:112
  201.9 8.3 %collective-permute-start.30 = (bf16[128,1024]{1,0:T(8,128)(2,1)S(1)}, bf16[128,1024]{1,0:T(8,128)(2,1)S(1)}, u32[]{:S(2)}, u32[]{:S(2)}) collective-permute-start(bf16[128,1024]{1,0:T(8,128)(2,1)S(1)} %select_add_fusion.9), channel_id=1, source_target_pairs={{0,64},{64,128},{128,192},{192,256},{256,320},{320,384},{384,448},... | collective-permute-start | bytes 786440 | tf_op jit(solution)/shard_map/ppermute | solution.py:112
  205.3 8.3 %collective-permute-start.33 = (bf16[128,1024]{1,0:T(8,128)(2,1)S(1)}, bf16[128,1024]{1,0:T(8,128)(2,1)S(1)}, u32[]{:S(2)}, u32[]{:S(2)}) collective-permute-start(bf16[128,1024]{1,0:T(8,128)(2,1)S(1)} %select_add_fusion.8), channel_id=1, source_target_pairs={{0,64},{64,128},{128,192},{192,256},{256,320},{320,384},{384,448},... | collective-permute-start | bytes 786440 | tf_op jit(solution)/shard_map/ppermute | solution.py:112
  211.3 8.7 %collective-permute-start.32 = (bf16[128,1024]{1,0:T(8,128)(2,1)S(1)}, bf16[128,1024]{1,0:T(8,128)(2,1)S(1)}, u32[]{:S(2)}, u32[]{:S(2)}) collective-permute-start(bf16[128,1024]{1,0:T(8,128)(2,1)S(1)} %select_add_fusion.7), channel_id=1, source_target_pairs={{0,64},{64,128},{128,192},{192,256},{256,320},{320,384},{384,448},... | collective-permute-start | bytes 786440 | tf_op jit(solution)/shard_map/ppermute | solution.py:112
  214.6 8.3 %collective-permute-start.34 = (bf16[128,1024]{1,0:T(8,128)(2,1)S(1)}, bf16[128,1024]{1,0:T(8,128)(2,1)S(1)}, u32[]{:S(2)}, u32[]{:S(2)}) collective-permute-start(bf16[128,1024]{1,0:T(8,128)(2,1)S(1)} %select_add_fusion.6), channel_id=1, source_target_pairs={{0,64},{64,128},{128,192},{192,256},{256,320},{320,384},{384,448},... | collective-permute-start | bytes 786440 | tf_op jit(solution)/shard_map/ppermute | solution.py:112
  221.0 28.9 %collective-permute-start.36 = (bf16[128,1024]{1,0:T(8,128)(2,1)S(1)}, bf16[128,1024]{1,0:T(8,128)(2,1)S(1)}, u32[]{:S(2)}, u32[]{:S(2)}) collective-permute-start(bf16[128,1024]{1,0:T(8,128)(2,1)S(1)} %select_add_fusion.5), channel_id=1, source_target_pairs={{0,64},{64,128},{128,192},{192,256},{256,320},{320,384},{384,448},... | collective-permute-start | bytes 786440 | tf_op jit(solution)/shard_map/ppermute | solution.py:112
  224.1 28.9 %collective-permute-start.35 = (bf16[128,1024]{1,0:T(8,128)(2,1)S(1)}, bf16[128,1024]{1,0:T(8,128)(2,1)S(1)}, u32[]{:S(2)}, u32[]{:S(2)}) collective-permute-start(bf16[128,1024]{1,0:T(8,128)(2,1)S(1)} %select_add_fusion.4), channel_id=1, source_target_pairs={{0,64},{64,128},{128,192},{192,256},{256,320},{320,384},{384,448},... | collective-permute-start | bytes 786440 | tf_op jit(solution)/shard_map/ppermute | solution.py:112
  227.0 70.0 %all-to-all-start.1 = ((bf16[8,4,2048]{2,1,0:T(4,128)(2,1)}), bf16[8,4,2048]{2,1,0:T(4,128)(2,1)S(1)}, u32[]{:S(2)}, u32[]{:S(2)}) async-start(bf16[8,4,2048]{2,1,0:T(4,128)(2,1)} %reshape.277), calls=%async_computation.1 | async-start | bytes 262144 | tf_op jit(solution)/shard_map/all_to_all | solution.py:162
  251.0 12.5 %collective-permute-start.38 = (bf16[128,1024]{1,0:T(8,128)(2,1)S(1)}, bf16[128,1024]{1,0:T(8,128)(2,1)S(1)}, u32[]{:S(2)}, u32[]{:S(2)}) collective-permute-start(bf16[128,1024]{1,0:T(8,128)(2,1)S(1)} %select_add_fusion.3), channel_id=1, source_target_pairs={{0,64},{64,128},{128,192},{192,256},{256,320},{320,384},{384,448},... | collective-permute-start | bytes 786440 | tf_op jit(solution)/shard_map/ppermute | solution.py:112
  254.0 12.3 %collective-permute-start.37 = (bf16[128,1024]{1,0:T(8,128)(2,1)S(1)}, bf16[128,1024]{1,0:T(8,128)(2,1)S(1)}, u32[]{:S(2)}, u32[]{:S(2)}) collective-permute-start(bf16[128,1024]{1,0:T(8,128)(2,1)S(1)} %select_add_fusion.2), channel_id=1, source_target_pairs={{0,64},{64,128},{128,192},{192,256},{256,320},{320,384},{384,448},... | collective-permute-start | bytes 786440 | tf_op jit(solution)/shard_map/ppermute | solution.py:112
  267.4 9.3 %collective-permute-start.39 = (bf16[128,1024]{1,0:T(8,128)(2,1)S(1)}, bf16[128,1024]{1,0:T(8,128)(2,1)S(1)}, u32[]{:S(2)}, u32[]{:S(2)}) collective-permute-start(bf16[128,1024]{1,0:T(8,128)(2,1)S(1)} %select_add_fusion), channel_id=1, source_target_pairs={{0,64},{64,128},{128,192},{192,256},{256,320},{320,384},{384,448},... | collective-permute-start | bytes 786440 | tf_op jit(solution)/shard_map/ppermute | solution.py:112
  269.3 24.8 %collective-permute-start.41 = (bf16[128,1024]{1,0:T(8,128)(2,1)S(1)}, bf16[128,1024]{1,0:T(8,128)(2,1)S(1)}, u32[]{:S(2)}, u32[]{:S(2)}) collective-permute-start(bf16[128,1024]{1,0:T(8,128)(2,1)S(1)} %select_add_fusion.1), channel_id=1, source_target_pairs={{0,64},{64,128},{128,192},{192,256},{256,320},{320,384},{384,448},... | collective-permute-start | bytes 786440 | tf_op jit(solution)/shard_map/ppermute | solution.py:112
  276.7 23.2 %collective-permute-start.40 = (bf16[128,512]{1,0:T(8,128)(2,1)S(1)}, bf16[128,512]{1,0:T(8,128)(2,1)S(1)}, u32[]{:S(2)}, u32[]{:S(2)}) collective-permute-start(bf16[128,512]{1,0:T(8,128)(2,1)S(1)} %slice.69), channel_id=1, source_target_pairs={{0,1},{1,0},{2,3},{3,2},{4,5},{5,4},{6,7},{7,6},{8,9},{9,8},{10,11... | collective-permute-start | bytes 393224 | tf_op jit(solution)/shard_map/ppermute | solution.py:30
  (26 other events, 675.2 us)

commit v6 on v5

--- a/solution.py
+++ b/solution.py
@@ -75,14 +75,17 @@
     to = lax.broadcasted_iota(jnp.int32, (n_rows, 2 * n_rows), 0)
     at = lax.broadcasted_iota(jnp.int32, (n_rows, 2 * n_rows), 1)
     core = (to // 128 - lax.axis_index("core")) & 1
-    source = core * 256 + ((to & 127) // CAP) * (2 * CAP) + kind * CAP + (to & (CAP - 1))
+    y = (to // 32 - lax.axis_index("y")) & 3
+    zh = (to // 16 - lax.axis_index("zh")) & 1
+    x = (to // CAP) & 3
+    source = core * 256 + y * 64 + zh * 32 + x * 8 + kind * CAP + (to & (CAP - 1))
     return (at == source).astype(jnp.bfloat16)
 
 
 def home_order(n_rows):
     to = lax.broadcasted_iota(jnp.int32, (n_rows, n_rows), 0)
     at = lax.broadcasted_iota(jnp.int32, (n_rows, n_rows), 1)
-    zh = (to // CAP - lax.axis_index("zh")) & 1
+    zh = (to // CAP) & 1
     source = zh * 16 + to // (2 * CAP) * CAP + (to & (CAP - 1))
     return (at == source).astype(jnp.bfloat16)
 
@@ -99,11 +102,12 @@
     here, core = lax.axis_index("group"), lax.axis_index("core")
     rank = jnp.where(core == 0, here, n_group - 1 - here)
     towards = height * (1 - 2 * core)
-    pairs = [(2 * i, 2 * i + 2) for i in range(n_group - 1)]
-    pairs += [(2 * i + 3, 2 * i + 1) for i in range(n_group - 1)]
     carried, last = [None] * len(streams), streams[0]
     for step in range(n_group - 1):
         begin = lax.clamp(0, here * height + (n_group - 1 - step) * towards, top)
+        reach = min((step // 4 + 1) * 4, n_group - 1)
+        pairs = [(2 * i, 2 * i + 2) for i in range(reach)]
+        pairs += [(2 * (n_group - 1 - i) + 1, 2 * (n_group - 2 - i) + 1) for i in range(reach)]
         for k, rows in enumerate(streams):
             term = block_of(rows, begin, height)
             if step:
@@ -113,6 +117,7 @@
         if step in ties:
             beside, carried[0] = lax.optimization_barrier((beside, carried[0]))
             beside = ties[step](beside)
+    beside, _ = lax.optimization_barrier((beside, last))
     return carried, beside
 
 
@@ -150,11 +155,10 @@
     grad_in = product(x_all, hid_grad_both)
 
     def along_y(rows):
-        parts = rows.reshape(4, -1, d_model)
-        total = parts[0].astype(jnp.float32)
-        for by in (1, 3, 2):
-            total = total + shift(parts[by], by).astype(jnp.float32)
-        return total.astype(jnp.bfloat16)
+        return lax.all_to_all(rows.reshape(4, -1, d_model), "y", 0, 0, tiled=True)
+
+    def summed(parts):
+        return jnp.sum(parts.astype(jnp.float32), axis=0).astype(jnp.bfloat16)
 
     def home(rows):
         parts = dot_f32(home_order(rows.shape[0]), rows, ((1,), (0,))).astype(jnp.bfloat16)
@@ -165,8 +169,9 @@
     given = swap(block_of(partial, (1 - core) * half, half), "core").astype(jnp.float32)
     given = (block_of(partial, core * half, half).astype(jnp.float32) + given).astype(jnp.bfloat16)
     sums, slots = line_sums(
-        [grad_out, grad_in], n_group, given, {0: along_y, 3: lambda rows: rows, 11: home}
-    )
+        [grad_out, grad_in], n_group, given, {0: along_y, 2: summed, 4: lambda rows: rows}
+    )
+    slots = home(slots)
     in_grad = dot_f32(sel, slots, ((0,), (0,))).astype(jnp.bfloat16)
     width = d_model // n_group
     here = lax.axis_index("group") * width

time: 304 us -> 310 us (1.020)
  the two profiles are of different devices: /device:TPU:35 before, /device:TPU:96 now
where the time goes in v6:
time: 310 us; the launch traced here: 308 us
  starting transfers between devices  191 us (62%)
  waiting for transfers between devices  58.5 us (19%)
  other arithmetic  36.1 us (12%)
  matrix products  17.9 us (6%)
    ppermute x30, starting transfers between devices, line_sums(): carried[k], last = (lax.ppermute(term, ('group', 'core'), pairs), term)  106 us
    ppermute x7, starting transfers between devices, swap(): return lax.ppermute(value, axis, [(0, 1), (1, 0)])  38.4 us
    add x28, other arithmetic, line_sums(): term + jnp.where(rank <= step, carried[k], jnp.zeros_like(carried[k]))  28.5 us
    all_to_all x1, starting transfers between devices, home(): lax.all_to_all(parts, ('x', 'zh'), 0, 0, tiled=True)  28.1 us
    ppermute x30, waiting for transfers between devices, line_sums(): carried[k], last = (lax.ppermute(term, ('group', 'core'), pairs), term)  22.5 us
    dot_general x15, matrix products, dot_f32(): lax.dot_general(a, b, (dims, ((), ())), preferred_element_type=jnp.float32)  17.9 us
    ppermute x7, waiting for transfers between devices, swap(): return lax.ppermute(value, axis, [(0, 1), (1, 0)])  16.5 us
    ppermute x3, starting transfers between devices, shift(): return lax.ppermute(value, 'y', [(i, (i + by) % 4) for i in range(4)])  10.3 us
  transfers between devices with their start and end apart: 43, of which 16 were waited for; matrix products, arithmetic and copies ran while one was open for 13% of the time, Pallas kernels for 0%

profile of v6, /device:TPU:96, one launch (start us, length us, event | category | flops | bytes accessed | tf_op | source)
XLA Modules:
  0.0 307.9 jit_solution(2001997674767686430)
XLA Ops:
  8.2 4.3 %all-to-all-start = ((bf16[4,8,2048]{2,1,0:T(8,128)(2,1)}), bf16[4,8,2048]{2,1,0:T(8,128)(2,1)S(1)}, u32[]{:S(2)}, u32[]{:S(2)}) async-start(bf16[4,8,2048]{2,1,0:T(8,128)(2,1)} %fusion.4), calls=%async_computation | async-start | bytes 262144 | tf_op jit(solution)/shard_map/all_to_all | solution.py:129
  12.6 5.9 %all-to-all-done = bf16[4,8,2048]{2,1,0:T(8,128)(2,1)S(1)} async-done(((bf16[4,8,2048]{2,1,0:T(8,128)(2,1)}), bf16[4,8,2048]{2,1,0:T(8,128)(2,1)S(1)}, u32[]{:S(2)}, u32[]{:S(2)}) %all-to-all-start) | async-done | bytes 131104 | tf_op jit(solution)/shard_map/all_to_all | solution.py:129
  18.5 26.3 %collective-permute-start = (bf16[32,2048]{1,0:T(8,128)(2,1)S(1)}, bf16[32,2048]{1,0:T(8,128)(2,1)S(1)}, u32[]{:S(2)}, u32[]{:S(2)}) collective-permute-start(bf16[32,2048]{1,0:T(8,128)(2,1)S(1)} %bitcast.47), channel_id=1, source_target_pairs={{0,8},{8,0},{1,9},{9,1},{2,10},{10,2},{3,11},{11,3},{4,12},{12,4},... | collective-permute-start | bytes 393224 | tf_op jit(solution)/shard_map/ppermute | solution.py:30
  46.1 13.8 %collective-permute-done = bf16[32,2048]{1,0:T(8,128)(2,1)S(1)} collective-permute-done((bf16[32,2048]{1,0:T(8,128)(2,1)S(1)}, bf16[32,2048]{1,0:T(8,128)(2,1)S(1)}, u32[]{:S(2)}, u32[]{:S(2)}) %collective-permute-start) | collective-permute-done | bytes 131104 | tf_op jit(solution)/shard_map/ppermute | solution.py:30
  59.9 4.9 %collective-permute-start.1 = (bf16[64,2048]{1,0:T(8,128)(2,1)S(1)}, bf16[64,2048]{1,0:T(8,128)(2,1)S(1)}, u32[]{:S(2)}, u32[]{:S(2)}) collective-permute-start(bf16[64,2048]{1,0:T(8,128)(2,1)S(1)} %pad_maximum_fusion), channel_id=1, source_target_pairs={{0,6},{2,0},{4,2},{6,4},{1,7},{3,1},{5,3},{7,5},{8,14},{10,8},{12,... | collective-permute-start | bytes 786440 | tf_op jit(solution)/shard_map/ppermute | solution.py:34
  67.4 2.9 collective-permute-start.3
  70.3 4.3 %collective-permute-done.2 = bf16[64,2048]{1,0:T(8,128)(2,1)S(1)} collective-permute-done((bf16[64,2048]{1,0:T(8,128)(2,1)S(1)}, bf16[64,2048]{1,0:T(8,128)(2,1)S(1)}, u32[]{:S(2)}, u32[]{:S(2)}) %collective-permute-start.2) | collective-permute-done | bytes 262176 | tf_op jit(solution)/shard_map/ppermute | solution.py:34
  106.2 3.1 %collective-permute-start.9 = (bf16[128,1024]{1,0:T(8,128)(2,1)S(1)}, bf16[128,1024]{1,0:T(8,128)(2,1)S(1)}, u32[]{:S(2)}, u32[]{:S(2)}) collective-permute-start(bf16[128,1024]{1,0:T(8,128)(2,1)S(1)} %select_add_fusion.27), channel_id=1, source_target_pairs={{0,64},{64,128},{128,192},{192,256},{961,897},{897,833},{833,769},... | collective-permute-start | bytes 786440 | tf_op jit(solution)/shard_map/ppermute | solution.py:116
  109.6 3.1 %collective-permute-start.12 = (bf16[128,1024]{1,0:T(8,128)(2,1)S(1)}, bf16[128,1024]{1,0:T(8,128)(2,1)}, u32[]{:S(2)}, u32[]{:S(2)}) collective-permute-start(bf16[128,1024]{1,0:T(8,128)(2,1)S(1)} %select_add_fusion.26), channel_id=1, source_target_pairs={{0,64},{64,128},{128,192},{192,256},{961,897},{897,833},{833,769},... | collective-permute-start | bytes 786440 | tf_op jit(solution)/shard_map/ppermute | solution.py:116
  112.7 3.5 %all-to-all-start.1 = ((bf16[4,32,2048]{2,1,0:T(8,128)(2,1)}), bf16[4,32,2048]{2,1,0:T(8,128)(2,1)S(1)}, u32[]{:S(2)}, u32[]{:S(2)}) async-start(bf16[4,32,2048]{2,1,0:T(8,128)(2,1)} %bitcast.7), calls=%async_computation.1 | async-start | bytes 1048576 | tf_op jit(solution)/shard_map/all_to_all | solution.py:158
  116.2 5.4 %collective-permute-done.9 = bf16[128,1024]{1,0:T(8,128)(2,1)S(1)} collective-permute-done((bf16[128,1024]{1,0:T(8,128)(2,1)S(1)}, bf16[128,1024]{1,0:T(8,128)(2,1)S(1)}, u32[]{:S(2)}, u32[]{:S(2)}) %collective-permute-start.9) | collective-permute-done | bytes 262176 | tf_op jit(solution)/shard_map/ppermute | solution.py:116
  128.1 3.4 %collective-permute-done.11 = bf16[128,1024]{1,0:T(8,128)(2,1)S(1)} collective-permute-done((bf16[128,1024]{1,0:T(8,128)(2,1)S(1)}, bf16[128,1024]{1,0:T(8,128)(2,1)S(1)}, u32[]{:S(2)}, u32[]{:S(2)}) %collective-permute-start.11) | collective-permute-done | bytes 262176 | tf_op jit(solution)/shard_map/ppermute | solution.py:116
  141.9 3.8 %collective-permute-start.15 = (bf16[128,1024]{1,0:T(8,128)(2,1)S(1)}, bf16[128,1024]{1,0:T(8,128)(2,1)S(1)}, u32[]{:S(2)}, u32[]{:S(2)}) collective-permute-start(bf16[128,1024]{1,0:T(8,128)(2,1)S(1)} %select_add_fusion.21), channel_id=1, source_target_pairs={{0,64},{64,128},{128,192},{192,256},{256,320},{320,384},{384,448},... | collective-permute-start | bytes 786440 | tf_op jit(solution)/shard_map/ppermute | solution.py:116
  151.3 5.0 %collective-permute-start.19 = (bf16[128,1024]{1,0:T(8,128)(2,1)S(1)}, bf16[128,1024]{1,0:T(8,128)(2,1)S(1)}, u32[]{:S(2)}, u32[]{:S(2)}) collective-permute-start(bf16[128,1024]{1,0:T(8,128)(2,1)S(1)} %select_add_fusion.19), channel_id=1, source_target_pairs={{0,64},{64,128},{128,192},{192,256},{256,320},{320,384},{384,448},... | collective-permute-start | bytes 786440 | tf_op jit(solution)/shard_map/ppermute | solution.py:116
  161.3 5.5 %collective-permute-start.21 = (bf16[128,1024]{1,0:T(8,128)(2,1)S(1)}, bf16[128,1024]{1,0:T(8,128)(2,1)S(1)}, u32[]{:S(2)}, u32[]{:S(2)}) collective-permute-start(bf16[128,1024]{1,0:T(8,128)(2,1)S(1)} %select_add_fusion.17), channel_id=1, source_target_pairs={{0,64},{64,128},{128,192},{192,256},{256,320},{320,384},{384,448},... | collective-permute-start | bytes 786440 | tf_op jit(solution)/shard_map/ppermute | solution.py:116
  171.9 5.7 %collective-permute-start.23 = (bf16[128,1024]{1,0:T(8,128)(2,1)S(1)}, bf16[128,1024]{1,0:T(8,128)(2,1)S(1)}, u32[]{:S(2)}, u32[]{:S(2)}) collective-permute-start(bf16[128,1024]{1,0:T(8,128)(2,1)S(1)} %select_add_fusion.15), channel_id=1, source_target_pairs={{0,64},{64,128},{128,192},{192,256},{256,320},{320,384},{384,448},... | collective-permute-start | bytes 786440 | tf_op jit(solution)/shard_map/ppermute | solution.py:116
  182.4 5.5 %collective-permute-start.25 = (bf16[128,1024]{1,0:T(8,128)(2,1)S(1)}, bf16[128,1024]{1,0:T(8,128)(2,1)S(1)}, u32[]{:S(2)}, u32[]{:S(2)}) collective-permute-start(bf16[128,1024]{1,0:T(8,128)(2,1)S(1)} %select_add_fusion.13), channel_id=1, source_target_pairs={{0,64},{64,128},{128,192},{192,256},{256,320},{320,384},{384,448},... | collective-permute-start | bytes 786440 | tf_op jit(solution)/shard_map/ppermute | solution.py:116
  189.0 2.8 collective-permute-start.24
  193.0 5.5 %collective-permute-start.27 = (bf16[128,1024]{1,0:T(8,128)(2,1)S(1)}, bf16[128,1024]{1,0:T(8,128)(2,1)S(1)}, u32[]{:S(2)}, u32[]{:S(2)}) collective-permute-start(bf16[128,1024]{1,0:T(8,128)(2,1)S(1)} %select_add_fusion.11), channel_id=1, source_target_pairs={{0,64},{64,128},{128,192},{192,256},{256,320},{320,384},{384,448},... | collective-permute-start | bytes 786440 | tf_op jit(solution)/shard_map/ppermute | solution.py:116
  199.6 2.8 collective-permute-start.26
  203.5 5.5 %collective-permute-start.29 = (bf16[128,1024]{1,0:T(8,128)(2,1)S(1)}, bf16[128,1024]{1,0:T(8,128)(2,1)S(1)}, u32[]{:S(2)}, u32[]{:S(2)}) collective-permute-start(bf16[128,1024]{1,0:T(8,128)(2,1)S(1)} %select_add_fusion.9), channel_id=1, source_target_pairs={{0,64},{64,128},{128,192},{192,256},{256,320},{320,384},{384,448},... | collective-permute-start | bytes 786440 | tf_op jit(solution)/shard_map/ppermute | solution.py:116
  210.1 3.5 %collective-permute-start.28 = (bf16[128,1024]{1,0:T(8,128)(2,1)S(1)}, bf16[128,1024]{1,0:T(8,128)(2,1)S(1)}, u32[]{:S(2)}, u32[]{:S(2)}) collective-permute-start(bf16[128,1024]{1,0:T(8,128)(2,1)S(1)} %select_add_fusion.8), channel_id=1, source_target_pairs={{0,64},{64,128},{128,192},{192,256},{256,320},{320,384},{384,448},... | collective-permute-start | bytes 786440 | tf_op jit(solution)/shard_map/ppermute | solution.py:116
  214.8 4.8 %collective-permute-start.31 = (bf16[128,1024]{1,0:T(8,128)(2,1)S(1)}, bf16[128,1024]{1,0:T(8,128)(2,1)S(1)}, u32[]{:S(2)}, u32[]{:S(2)}) collective-permute-start(bf16[128,1024]{1,0:T(8,128)(2,1)S(1)} %select_add_fusion.7), channel_id=1, source_target_pairs={{0,64},{64,128},{128,192},{192,256},{256,320},{320,384},{384,448},... | collective-permute-start | bytes 786440 | tf_op jit(solution)/shard_map/ppermute | solution.py:116
  220.7 3.5 %collective-permute-start.30 = (bf16[128,1024]{1,0:T(8,128)(2,1)S(1)}, bf16[128,1024]{1,0:T(8,128)(2,1)S(1)}, u32[]{:S(2)}, u32[]{:S(2)}) collective-permute-start(bf16[128,1024]{1,0:T(8,128)(2,1)S(1)} %select_add_fusion.6), channel_id=1, source_target_pairs={{0,64},{64,128},{128,192},{192,256},{256,320},{320,384},{384,448},... | collective-permute-start | bytes 786440 | tf_op jit(solution)/shard_map/ppermute | solution.py:116
  225.3 4.8 %collective-permute-start.33 = (bf16[128,1024]{1,0:T(8,128)(2,1)S(1)}, bf16[128,1024]{1,0:T(8,128)(2,1)S(1)}, u32[]{:S(2)}, u32[]{:S(2)}) collective-permute-start(bf16[128,1024]{1,0:T(8,128)(2,1)S(1)} %select_add_fusion.5), channel_id=1, source_target_pairs={{0,64},{64,128},{128,192},{192,256},{256,320},{320,384},{384,448},... | collective-permute-start | bytes 786440 | tf_op jit(solution)/shard_map/ppermute | solution.py:116
  231.2 3.5 %collective-permute-start.32 = (bf16[128,1024]{1,0:T(8,128)(2,1)S(1)}, bf16[128,1024]{1,0:T(8,128)(2,1)S(1)}, u32[]{:S(2)}, u32[]{:S(2)}) collective-permute-start(bf16[128,1024]{1,0:T(8,128)(2,1)S(1)} %select_add_fusion.4), channel_id=1, source_target_pairs={{0,64},{64,128},{128,192},{192,256},{256,320},{320,384},{384,448},... | collective-permute-start | bytes 786440 | tf_op jit(solution)/shard_map/ppermute | solution.py:116
  236.4 4.3 %collective-permute-start.35 = (bf16[128,1024]{1,0:T(8,128)(2,1)S(1)}, bf16[128,1024]{1,0:T(8,128)(2,1)S(1)}, u32[]{:S(2)}, u32[]{:S(2)}) collective-permute-start(bf16[128,1024]{1,0:T(8,128)(2,1)S(1)} %select_add_fusion.3), channel_id=1, source_target_pairs={{0,64},{64,128},{128,192},{192,256},{256,320},{320,384},{384,448},... | collective-permute-start | bytes 786440 | tf_op jit(solution)/shard_map/ppermute | solution.py:116
  241.8 3.5 %collective-permute-start.34 = (bf16[128,1024]{1,0:T(8,128)(2,1)S(1)}, bf16[128,1024]{1,0:T(8,128)(2,1)S(1)}, u32[]{:S(2)}, u32[]{:S(2)}) collective-permute-start(bf16[128,1024]{1,0:T(8,128)(2,1)S(1)} %select_add_fusion.2), channel_id=1, source_target_pairs={{0,64},{64,128},{128,192},{192,256},{256,320},{320,384},{384,448},... | collective-permute-start | bytes 786440 | tf_op jit(solution)/shard_map/ppermute | solution.py:116
  246.9 3.2 %collective-permute-done.34 = bf16[128,1024]{1,0:T(8,128)(2,1)S(1)} collective-permute-done((bf16[128,1024]{1,0:T(8,128)(2,1)S(1)}, bf16[128,1024]{1,0:T(8,128)(2,1)S(1)}, u32[]{:S(2)}, u32[]{:S(2)}) %collective-permute-start.34) | collective-permute-done | bytes 262176 | tf_op jit(solution)/shard_map/ppermute | solution.py:116
  252.9 28.1 %all-to-all-start.2 = ((bf16[8,4,2048]{2,1,0:T(4,128)(2,1)}), bf16[8,4,2048]{2,1,0:T(4,128)(2,1)S(1)}, u32[]{:S(2)}, u32[]{:S(2)}) async-start(bf16[8,4,2048]{2,1,0:T(4,128)(2,1)} %reshape.272), calls=%async_computation.2 | async-start | bytes 262144 | tf_op jit(solution)/shard_map/all_to_all | solution.py:166
  281.0 4.3 %collective-permute-start.38 = (bf16[128,1024]{1,0:T(8,128)(2,1)S(1)}, bf16[128,1024]{1,0:T(8,128)(2,1)S(1)}, u32[]{:S(2)}, u32[]{:S(2)}) collective-permute-start(bf16[128,1024]{1,0:T(8,128)(2,1)S(1)} %select_add_fusion.1), channel_id=1, source_target_pairs={{0,64},{64,128},{128,192},{192,256},{256,320},{320,384},{384,448},... | collective-permute-start | bytes 786440 | tf_op jit(solution)/shard_map/ppermute | solution.py:116
  299.6 6.4 %all-to-all-done.2 = bf16[8,4,2048]{2,1,0:T(4,128)(2,1)S(1)} async-done(((bf16[8,4,2048]{2,1,0:T(4,128)(2,1)}), bf16[8,4,2048]{2,1,0:T(4,128)(2,1)S(1)}, u32[]{:S(2)}, u32[]{:S(2)}) %all-to-all-start.2) | async-done | bytes 131104 | tf_op jit(solution)/shard_map/all_to_all | solution.py:166
  (158 shorter events, 112.9 us)
Async XLA Ops:
  8.2 10.3 %all-to-all-start = ((bf16[4,8,2048]{2,1,0:T(8,128)(2,1)}), bf16[4,8,2048]{2,1,0:T(8,128)(2,1)S(1)}, u32[]{:S(2)}, u32[]{:S(2)}) async-start(bf16[4,8,2048]{2,1,0:T(8,128)(2,1)} %fusion.4), calls=%async_computation | async-start | bytes 262144 | tf_op jit(solution)/shard_map/all_to_all | solution.py:129
  18.5 41.4 %collective-permute-start = (bf16[32,2048]{1,0:T(8,128)(2,1)S(1)}, bf16[32,2048]{1,0:T(8,128)(2,1)S(1)}, u32[]{:S(2)}, u32[]{:S(2)}) collective-permute-start(bf16[32,2048]{1,0:T(8,128)(2,1)S(1)} %bitcast.47), channel_id=1, source_target_pairs={{0,8},{8,0},{1,9},{9,1},{2,10},{10,2},{3,11},{11,3},{4,12},{12,4},... | collective-permute-start | bytes 393224 | tf_op jit(solution)/shard_map/ppermute | solution.py:30
  59.9 10.4 %collective-permute-start.1 = (bf16[64,2048]{1,0:T(8,128)(2,1)S(1)}, bf16[64,2048]{1,0:T(8,128)(2,1)S(1)}, u32[]{:S(2)}, u32[]{:S(2)}) collective-permute-start(bf16[64,2048]{1,0:T(8,128)(2,1)S(1)} %pad_maximum_fusion), channel_id=1, source_target_pairs={{0,6},{2,0},{4,2},{6,4},{1,7},{3,1},{5,3},{7,5},{8,14},{10,8},{12,... | collective-permute-start | bytes 786440 | tf_op jit(solution)/shard_map/ppermute | solution.py:34
  64.9 9.8 %collective-permute-start.2 = (bf16[64,2048]{1,0:T(8,128)(2,1)S(1)}, bf16[64,2048]{1,0:T(8,128)(2,1)S(1)}, u32[]{:S(2)}, u32[]{:S(2)}) collective-permute-start(bf16[64,2048]{1,0:T(8,128)(2,1)S(1)} %pad_maximum_fusion), channel_id=1, source_target_pairs={{0,4},{2,6},{4,0},{6,2},{1,5},{3,7},{5,1},{7,3},{8,12},{10,14},{12... | collective-permute-start | bytes 786440 | tf_op jit(solution)/shard_map/ppermute | solution.py:34
  67.4 10.0 %collective-permute-start.3 = (bf16[64,2048]{1,0:T(8,128)(2,1)S(1)}, bf16[64,2048]{1,0:T(8,128)(2,1)S(1)}, u32[]{:S(2)}, u32[]{:S(2)}) collective-permute-start(bf16[64,2048]{1,0:T(8,128)(2,1)S(1)} %pad_maximum_fusion), channel_id=1, source_target_pairs={{0,2},{2,4},{4,6},{6,0},{1,3},{3,5},{5,7},{7,1},{8,10},{10,12},{12... | collective-permute-start | bytes 786440 | tf_op jit(solution)/shard_map/ppermute | solution.py:34
  106.2 15.4 %collective-permute-start.9 = (bf16[128,1024]{1,0:T(8,128)(2,1)S(1)}, bf16[128,1024]{1,0:T(8,128)(2,1)S(1)}, u32[]{:S(2)}, u32[]{:S(2)}) collective-permute-start(bf16[128,1024]{1,0:T(8,128)(2,1)S(1)} %select_add_fusion.27), channel_id=1, source_target_pairs={{0,64},{64,128},{128,192},{192,256},{961,897},{897,833},{833,769},... | collective-permute-start | bytes 786440 | tf_op jit(solution)/shard_map/ppermute | solution.py:116
  109.6 15.5 %collective-permute-start.12 = (bf16[128,1024]{1,0:T(8,128)(2,1)S(1)}, bf16[128,1024]{1,0:T(8,128)(2,1)}, u32[]{:S(2)}, u32[]{:S(2)}) collective-permute-start(bf16[128,1024]{1,0:T(8,128)(2,1)S(1)} %select_add_fusion.26), channel_id=1, source_target_pairs={{0,64},{64,128},{128,192},{192,256},{961,897},{897,833},{833,769},... | collective-permute-start | bytes 786440 | tf_op jit(solution)/shard_map/ppermute | solution.py:116
  112.7 15.4 %all-to-all-start.1 = ((bf16[4,32,2048]{2,1,0:T(8,128)(2,1)}), bf16[4,32,2048]{2,1,0:T(8,128)(2,1)S(1)}, u32[]{:S(2)}, u32[]{:S(2)}) async-start(bf16[4,32,2048]{2,1,0:T(8,128)(2,1)} %bitcast.7), calls=%async_computation.1 | async-start | bytes 1048576 | tf_op jit(solution)/shard_map/all_to_all | solution.py:158
  122.7 8.8 %collective-permute-start.11 = (bf16[128,1024]{1,0:T(8,128)(2,1)S(1)}, bf16[128,1024]{1,0:T(8,128)(2,1)S(1)}, u32[]{:S(2)}, u32[]{:S(2)}) collective-permute-start(bf16[128,1024]{1,0:T(8,128)(2,1)S(1)} %select_add_fusion.25), channel_id=1, source_target_pairs={{0,64},{64,128},{128,192},{192,256},{961,897},{897,833},{833,769},... | collective-permute-start | bytes 786440 | tf_op jit(solution)/shard_map/ppermute | solution.py:116
  126.1 9.0 %collective-permute-start.14 = (bf16[128,1024]{1,0:T(8,128)(2,1)S(1)}, bf16[128,1024]{1,0:T(8,128)(2,1)}, u32[]{:S(2)}, u32[]{:S(2)}) collective-permute-start(bf16[128,1024]{1,0:T(8,128)(2,1)S(1)} %select_add_fusion.24), channel_id=1, source_target_pairs={{0,64},{64,128},{128,192},{192,256},{961,897},{897,833},{833,769},... | collective-permute-start | bytes 786440 | tf_op jit(solution)/shard_map/ppermute | solution.py:116
  136.4 9.4 %collective-permute-start.16 = (bf16[128,1024]{1,0:T(8,128)(2,1)S(1)}, bf16[128,1024]{1,0:T(8,128)(2,1)}, u32[]{:S(2)}, u32[]{:S(2)}) collective-permute-start(bf16[128,1024]{1,0:T(8,128)(2,1)S(1)} %select_add_fusion.22), channel_id=1, source_target_pairs={{0,64},{64,128},{128,192},{192,256},{961,897},{897,833},{833,769},... | collective-permute-start | bytes 786440 | tf_op jit(solution)/shard_map/ppermute | solution.py:116
  146.9 9.4 %collective-permute-start.17 = (bf16[128,1024]{1,0:T(8,128)(2,1)S(1)}, bf16[128,1024]{1,0:T(8,128)(2,1)}, u32[]{:S(2)}, u32[]{:S(2)}) collective-permute-start(bf16[128,1024]{1,0:T(8,128)(2,1)S(1)} %select_add_fusion.20), channel_id=1, source_target_pairs={{0,64},{64,128},{128,192},{192,256},{256,320},{320,384},{384,448},... | collective-permute-start | bytes 786440 | tf_op jit(solution)/shard_map/ppermute | solution.py:116
  151.3 8.9 %collective-permute-start.19 = (bf16[128,1024]{1,0:T(8,128)(2,1)S(1)}, bf16[128,1024]{1,0:T(8,128)(2,1)S(1)}, u32[]{:S(2)}, u32[]{:S(2)}) collective-permute-start(bf16[128,1024]{1,0:T(8,128)(2,1)S(1)} %select_add_fusion.19), channel_id=1, source_target_pairs={{0,64},{64,128},{128,192},{192,256},{256,320},{320,384},{384,448},... | collective-permute-start | bytes 786440 | tf_op jit(solution)/shard_map/ppermute | solution.py:116
  157.5 9.4 %collective-permute-start.18 = (bf16[128,1024]{1,0:T(8,128)(2,1)S(1)}, bf16[128,1024]{1,0:T(8,128)(2,1)S(1)}, u32[]{:S(2)}, u32[]{:S(2)}) collective-permute-start(bf16[128,1024]{1,0:T(8,128)(2,1)S(1)} %select_add_fusion.18), channel_id=1, source_target_pairs={{0,64},{64,128},{128,192},{192,256},{256,320},{320,384},{384,448},... | collective-permute-start | bytes 786440 | tf_op jit(solution)/shard_map/ppermute | solution.py:116
  161.3 9.5 %collective-permute-start.21 = (bf16[128,1024]{1,0:T(8,128)(2,1)S(1)}, bf16[128,1024]{1,0:T(8,128)(2,1)S(1)}, u32[]{:S(2)}, u32[]{:S(2)}) collective-permute-start(bf16[128,1024]{1,0:T(8,128)(2,1)S(1)} %select_add_fusion.17), channel_id=1, source_target_pairs={{0,64},{64,128},{128,192},{192,256},{256,320},{320,384},{384,448},... | collective-permute-start | bytes 786440 | tf_op jit(solution)/shard_map/ppermute | solution.py:116
  167.9 9.6 %collective-permute-start.20 = (bf16[128,1024]{1,0:T(8,128)(2,1)S(1)}, bf16[128,1024]{1,0:T(8,128)(2,1)S(1)}, u32[]{:S(2)}, u32[]{:S(2)}) collective-permute-start(bf16[128,1024]{1,0:T(8,128)(2,1)S(1)} %select_add_fusion.16), channel_id=1, source_target_pairs={{0,64},{64,128},{128,192},{192,256},{256,320},{320,384},{384,448},... | collective-permute-start | bytes 786440 | tf_op jit(solution)/shard_map/ppermute | solution.py:116
  171.9 9.5 %collective-permute-start.23 = (bf16[128,1024]{1,0:T(8,128)(2,1)S(1)}, bf16[128,1024]{1,0:T(8,128)(2,1)S(1)}, u32[]{:S(2)}, u32[]{:S(2)}) collective-permute-start(bf16[128,1024]{1,0:T(8,128)(2,1)S(1)} %select_add_fusion.15), channel_id=1, source_target_pairs={{0,64},{64,128},{128,192},{192,256},{256,320},{320,384},{384,448},... | collective-permute-start | bytes 786440 | tf_op jit(solution)/shard_map/ppermute | solution.py:116
  178.7 9.3 %collective-permute-start.22 = (bf16[128,1024]{1,0:T(8,128)(2,1)S(1)}, bf16[128,1024]{1,0:T(8,128)(2,1)S(1)}, u32[]{:S(2)}, u32[]{:S(2)}) collective-permute-start(bf16[128,1024]{1,0:T(8,128)(2,1)S(1)} %select_add_fusion.14), channel_id=1, source_target_pairs={{0,64},{64,128},{128,192},{192,256},{256,320},{320,384},{384,448},... | collective-permute-start | bytes 786440 | tf_op jit(solution)/shard_map/ppermute | solution.py:116
  182.4 9.5 %collective-permute-start.25 = (bf16[128,1024]{1,0:T(8,128)(2,1)S(1)}, bf16[128,1024]{1,0:T(8,128)(2,1)S(1)}, u32[]{:S(2)}, u32[]{:S(2)}) collective-permute-start(bf16[128,1024]{1,0:T(8,128)(2,1)S(1)} %select_add_fusion.13), channel_id=1, source_target_pairs={{0,64},{64,128},{128,192},{192,256},{256,320},{320,384},{384,448},... | collective-permute-start | bytes 786440 | tf_op jit(solution)/shard_map/ppermute | solution.py:116
  189.0 9.5 %collective-permute-start.24 = (bf16[128,1024]{1,0:T(8,128)(2,1)S(1)}, bf16[128,1024]{1,0:T(8,128)(2,1)S(1)}, u32[]{:S(2)}, u32[]{:S(2)}) collective-permute-start(bf16[128,1024]{1,0:T(8,128)(2,1)S(1)} %select_add_fusion.12), channel_id=1, source_target_pairs={{0,64},{64,128},{128,192},{192,256},{256,320},{320,384},{384,448},... | collective-permute-start | bytes 786440 | tf_op jit(solution)/shard_map/ppermute | solution.py:116
  193.0 9.5 %collective-permute-start.27 = (bf16[128,1024]{1,0:T(8,128)(2,1)S(1)}, bf16[128,1024]{1,0:T(8,128)(2,1)S(1)}, u32[]{:S(2)}, u32[]{:S(2)}) collective-permute-start(bf16[128,1024]{1,0:T(8,128)(2,1)S(1)} %select_add_fusion.11), channel_id=1, source_target_pairs={{0,64},{64,128},{128,192},{192,256},{256,320},{320,384},{384,448},... | collective-permute-start | bytes 786440 | tf_op jit(solution)/shard_map/ppermute | solution.py:116
  199.6 9.5 %collective-permute-start.26 = (bf16[128,1024]{1,0:T(8,128)(2,1)S(1)}, bf16[128,1024]{1,0:T(8,128)(2,1)S(1)}, u32[]{:S(2)}, u32[]{:S(2)}) collective-permute-start(bf16[128,1024]{1,0:T(8,128)(2,1)S(1)} %select_add_fusion.10), channel_id=1, source_target_pairs={{0,64},{64,128},{128,192},{192,256},{256,320},{320,384},{384,448},... | collective-permute-start | bytes 786440 | tf_op jit(solution)/shard_map/ppermute | solution.py:116
  203.5 10.2 %collective-permute-start.29 = (bf16[128,1024]{1,0:T(8,128)(2,1)S(1)}, bf16[128,1024]{1,0:T(8,128)(2,1)S(1)}, u32[]{:S(2)}, u32[]{:S(2)}) collective-permute-start(bf16[128,1024]{1,0:T(8,128)(2,1)S(1)} %select_add_fusion.9), channel_id=1, source_target_pairs={{0,64},{64,128},{128,192},{192,256},{256,320},{320,384},{384,448},... | collective-permute-start | bytes 786440 | tf_op jit(solution)/shard_map/ppermute | solution.py:116
  210.1 9.5 %collective-permute-start.28 = (bf16[128,1024]{1,0:T(8,128)(2,1)S(1)}, bf16[128,1024]{1,0:T(8,128)(2,1)S(1)}, u32[]{:S(2)}, u32[]{:S(2)}) collective-permute-start(bf16[128,1024]{1,0:T(8,128)(2,1)S(1)} %select_add_fusion.8), channel_id=1, source_target_pairs={{0,64},{64,128},{128,192},{192,256},{256,320},{320,384},{384,448},... | collective-permute-start | bytes 786440 | tf_op jit(solution)/shard_map/ppermute | solution.py:116
  214.8 9.5 %collective-permute-start.31 = (bf16[128,1024]{1,0:T(8,128)(2,1)S(1)}, bf16[128,1024]{1,0:T(8,128)(2,1)S(1)}, u32[]{:S(2)}, u32[]{:S(2)}) collective-permute-start(bf16[128,1024]{1,0:T(8,128)(2,1)S(1)} %select_add_fusion.7), channel_id=1, source_target_pairs={{0,64},{64,128},{128,192},{192,256},{256,320},{320,384},{384,448},... | collective-permute-start | bytes 786440 | tf_op jit(solution)/shard_map/ppermute | solution.py:116
  220.7 9.5 %collective-permute-start.30 = (bf16[128,1024]{1,0:T(8,128)(2,1)S(1)}, bf16[128,1024]{1,0:T(8,128)(2,1)S(1)}, u32[]{:S(2)}, u32[]{:S(2)}) collective-permute-start(bf16[128,1024]{1,0:T(8,128)(2,1)S(1)} %select_add_fusion.6), channel_id=1, source_target_pairs={{0,64},{64,128},{128,192},{192,256},{256,320},{320,384},{384,448},... | collective-permute-start | bytes 786440 | tf_op jit(solution)/shard_map/ppermute | solution.py:116
  225.3 10.0 %collective-permute-start.33 = (bf16[128,1024]{1,0:T(8,128)(2,1)S(1)}, bf16[128,1024]{1,0:T(8,128)(2,1)S(1)}, u32[]{:S(2)}, u32[]{:S(2)}) collective-permute-start(bf16[128,1024]{1,0:T(8,128)(2,1)S(1)} %select_add_fusion.5), channel_id=1, source_target_pairs={{0,64},{64,128},{128,192},{192,256},{256,320},{320,384},{384,448},... | collective-permute-start | bytes 786440 | tf_op jit(solution)/shard_map/ppermute | solution.py:116
  231.2 9.5 %collective-permute-start.32 = (bf16[128,1024]{1,0:T(8,128)(2,1)S(1)}, bf16[128,1024]{1,0:T(8,128)(2,1)S(1)}, u32[]{:S(2)}, u32[]{:S(2)}) collective-permute-start(bf16[128,1024]{1,0:T(8,128)(2,1)S(1)} %select_add_fusion.4), channel_id=1, source_target_pairs={{0,64},{64,128},{128,192},{192,256},{256,320},{320,384},{384,448},... | collective-permute-start | bytes 786440 | tf_op jit(solution)/shard_map/ppermute | solution.py:116
  236.4 9.5 %collective-permute-start.35 = (bf16[128,1024]{1,0:T(8,128)(2,1)S(1)}, bf16[128,1024]{1,0:T(8,128)(2,1)S(1)}, u32[]{:S(2)}, u32[]{:S(2)}) collective-permute-start(bf16[128,1024]{1,0:T(8,128)(2,1)S(1)} %select_add_fusion.3), channel_id=1, source_target_pairs={{0,64},{64,128},{128,192},{192,256},{256,320},{320,384},{384,448},... | collective-permute-start | bytes 786440 | tf_op jit(solution)/shard_map/ppermute | solution.py:116
  252.9 53.1 %all-to-all-start.2 = ((bf16[8,4,2048]{2,1,0:T(4,128)(2,1)}), bf16[8,4,2048]{2,1,0:T(4,128)(2,1)S(1)}, u32[]{:S(2)}, u32[]{:S(2)}) async-start(bf16[8,4,2048]{2,1,0:T(4,128)(2,1)} %reshape.272), calls=%async_computation.2 | async-start | bytes 262144 | tf_op jit(solution)/shard_map/all_to_all | solution.py:166
  281.0 9.0 %collective-permute-start.38 = (bf16[128,1024]{1,0:T(8,128)(2,1)S(1)}, bf16[128,1024]{1,0:T(8,128)(2,1)S(1)}, u32[]{:S(2)}, u32[]{:S(2)}) collective-permute-start(bf16[128,1024]{1,0:T(8,128)(2,1)S(1)} %select_add_fusion.1), channel_id=1, source_target_pairs={{0,64},{64,128},{128,192},{192,256},{256,320},{320,384},{384,448},... | collective-permute-start | bytes 786440 | tf_op jit(solution)/shard_map/ppermute | solution.py:116
  285.3 9.0 %collective-permute-start.36 = (bf16[128,1024]{1,0:T(8,128)(2,1)S(1)}, bf16[128,1024]{1,0:T(8,128)(2,1)S(1)}, u32[]{:S(2)}, u32[]{:S(2)}) collective-permute-start(bf16[128,1024]{1,0:T(8,128)(2,1)S(1)} %select_add_fusion), channel_id=1, source_target_pairs={{0,64},{64,128},{128,192},{192,256},{256,320},{320,384},{384,448},... | collective-permute-start | bytes 786440 | tf_op jit(solution)/shard_map/ppermute | solution.py:116
  (19 other events, 356.9 us)

commit v7 on v6

--- a/solution.py
+++ b/solution.py
@@ -105,7 +105,7 @@
     carried, last = [None] * len(streams), streams[0]
     for step in range(n_group - 1):
         begin = lax.clamp(0, here * height + (n_group - 1 - step) * towards, top)
-        reach = min((step // 4 + 1) * 4, n_group - 1)
+        reach = min((step // 2 + 1) * 2, n_group - 1)
         pairs = [(2 * i, 2 * i + 2) for i in range(reach)]
         pairs += [(2 * (n_group - 1 - i) + 1, 2 * (n_group - 2 - i) + 1) for i in range(reach)]
         for k, rows in enumerate(streams):
@@ -117,7 +117,6 @@
         if step in ties:
             beside, carried[0] = lax.optimization_barrier((beside, carried[0]))
             beside = ties[step](beside)
-    beside, _ = lax.optimization_barrier((beside, last))
     return carried, beside
 
 
@@ -169,9 +168,8 @@
     given = swap(block_of(partial, (1 - core) * half, half), "core").astype(jnp.float32)
     given = (block_of(partial, core * half, half).astype(jnp.float32) + given).astype(jnp.bfloat16)
     sums, slots = line_sums(
-        [grad_out, grad_in], n_group, given, {0: along_y, 2: summed, 4: lambda rows: rows}
-    )
-    slots = home(slots)
+        [grad_out, grad_in], n_group, given, {0: along_y, 1: lambda parts: home(summed(parts)), 4: lambda rows: rows}
+    )
     in_grad = dot_f32(sel, slots, ((0,), (0,))).astype(jnp.bfloat16)
     width = d_model // n_group
     here = lax.axis_index("group") * width

time: 310 us -> 301 us (0.971)
  the two profiles are of different devices: /device:TPU:96 before, /device:TPU:107 now
where the time goes in v7:
time: 301 us; the launch traced here: 298 us
  starting transfers between devices  158 us (52%)
  waiting for transfers between devices  78.2 us (26%)
  other arithmetic  37.9 us (13%)
  matrix products  17.3 us (6%)
  local copies, waits for them, and re-layouts  4.85 us (2%)
    ppermute x7, starting transfers between devices, swap(): return lax.ppermute(value, axis, [(0, 1), (1, 0)])  82 us
    ppermute x30, waiting for transfers between devices, line_sums(): carried[k], last = (lax.ppermute(term, ('group', 'core'), pairs), term)  41.6 us
    ppermute x30, starting transfers between devices, line_sums(): carried[k], last = (lax.ppermute(term, ('group', 'core'), pairs), term)  33.2 us
    add x28, other arithmetic, line_sums(): term + jnp.where(rank <= step, carried[k], jnp.zeros_like(carried[k]))  30.2 us
    all_to_all x1, starting transfers between devices, home(): lax.all_to_all(parts, ('x', 'zh'), 0, 0, tiled=True)  22.8 us
    dot_general x15, matrix products, dot_f32(): lax.dot_general(a, b, (dims, ((), ())), preferred_element_type=jnp.float32)  17.3 us
    all_to_all x1, waiting for transfers between devices, home(): lax.all_to_all(parts, ('x', 'zh'), 0, 0, tiled=True)  14.8 us
    ppermute x7, waiting for transfers between devices, swap(): return lax.ppermute(value, axis, [(0, 1), (1, 0)])  10.7 us
  transfers between devices with their start and end apart: 43, of which 15 were waited for; matrix products, arithmetic and copies ran while one was open for 14% of the time, Pallas kernels for 0%

profile of v7, /device:TPU:107, one launch (start us, length us, event | category | flops | bytes accessed | tf_op | source)
XLA Modules:
  0.0 298.0 jit_solution(18274784120368580986)
XLA Ops:
  6.2 2.0 fusion.4
  8.2 4.3 %all-to-all-start = ((bf16[4,8,2048]{2,1,0:T(8,128)(2,1)}), bf16[4,8,2048]{2,1,0:T(8,128)(2,1)S(1)}, u32[]{:S(2)}, u32[]{:S(2)}) async-start(bf16[4,8,2048]{2,1,0:T(8,128)(2,1)} %fusion.4), calls=%async_computation | async-start | bytes 262144 | tf_op jit(solution)/shard_map/all_to_all | solution.py:128
  12.5 3.6 %all-to-all-done = bf16[4,8,2048]{2,1,0:T(8,128)(2,1)S(1)} async-done(((bf16[4,8,2048]{2,1,0:T(8,128)(2,1)}), bf16[4,8,2048]{2,1,0:T(8,128)(2,1)S(1)}, u32[]{:S(2)}, u32[]{:S(2)}) %all-to-all-start) | async-done | bytes 131104 | tf_op jit(solution)/shard_map/all_to_all | solution.py:128
  16.1 26.0 %collective-permute-start = (bf16[32,2048]{1,0:T(8,128)(2,1)S(1)}, bf16[32,2048]{1,0:T(8,128)(2,1)S(1)}, u32[]{:S(2)}, u32[]{:S(2)}) collective-permute-start(bf16[32,2048]{1,0:T(8,128)(2,1)S(1)} %bitcast.46), channel_id=1, source_target_pairs={{0,8},{8,0},{1,9},{9,1},{2,10},{10,2},{3,11},{11,3},{4,12},{12,4},... | collective-permute-start | bytes 393224 | tf_op jit(solution)/shard_map/ppermute | solution.py:30
  43.4 8.9 %collective-permute-done = bf16[32,2048]{1,0:T(8,128)(2,1)S(1)} collective-permute-done((bf16[32,2048]{1,0:T(8,128)(2,1)S(1)}, bf16[32,2048]{1,0:T(8,128)(2,1)S(1)}, u32[]{:S(2)}, u32[]{:S(2)}) %collective-permute-start) | collective-permute-done | bytes 131104 | tf_op jit(solution)/shard_map/ppermute | solution.py:30
  52.4 2.1 collective-permute-start.1
  54.5 4.2 %collective-permute-start.2 = (bf16[64,2048]{1,0:T(8,128)(2,1)S(1)}, bf16[64,2048]{1,0:T(8,128)(2,1)S(1)}, u32[]{:S(2)}, u32[]{:S(2)}) collective-permute-start(bf16[64,2048]{1,0:T(8,128)(2,1)S(1)} %pad_maximum_fusion), channel_id=1, source_target_pairs={{0,4},{2,6},{4,0},{6,2},{1,5},{3,7},{5,1},{7,3},{8,12},{10,14},{12... | collective-permute-start | bytes 786440 | tf_op jit(solution)/shard_map/ppermute | solution.py:34
  58.7 3.5 %collective-permute-start.3 = (bf16[64,2048]{1,0:T(8,128)(2,1)S(1)}, bf16[64,2048]{1,0:T(8,128)(2,1)S(1)}, u32[]{:S(2)}, u32[]{:S(2)}) collective-permute-start(bf16[64,2048]{1,0:T(8,128)(2,1)S(1)} %pad_maximum_fusion), channel_id=1, source_target_pairs={{0,2},{2,4},{4,6},{6,0},{1,3},{3,5},{5,7},{7,1},{8,10},{10,12},{12... | collective-permute-start | bytes 786440 | tf_op jit(solution)/shard_map/ppermute | solution.py:34
  63.3 3.0 %collective-permute-done.3 = bf16[64,2048]{1,0:T(8,128)(2,1)S(1)} collective-permute-done((bf16[64,2048]{1,0:T(8,128)(2,1)S(1)}, bf16[64,2048]{1,0:T(8,128)(2,1)S(1)}, u32[]{:S(2)}, u32[]{:S(2)}) %collective-permute-start.3) | collective-permute-done | bytes 262176 | tf_op jit(solution)/shard_map/ppermute | solution.py:34
  66.3 10.4 %collective-permute-start.4 = (bf16[256,2048]{1,0:T(8,128)(2,1)S(1)}, bf16[256,2048]{1,0:T(8,128)(2,1)}, u32[]{:S(2)}, u32[]{:S(2)}) collective-permute-start(bf16[256,2048]{1,0:T(8,128)(2,1)S(1)} %constant_dynamic-update-slice_fusion), channel_id=1, source_target_pairs={{0,1},{1,0},{2,3},{3,2},{4,5},{5,4},{6,7},{7,6},{8,9},{9,8},{10,11... | collective-permute-start | bytes 3145736 | tf_op jit(solution)/shard_map/ppermute | solution.py:30
  85.3 2.3 collective-permute-start.6
  89.3 2.0 collective-permute-start.8
  91.4 2.3 collective-permute-start.5
  97.2 1.9 copy-done.2
  101.4 6.0 %all-to-all-start.1 = ((bf16[4,32,2048]{2,1,0:T(8,128)(2,1)}), bf16[4,32,2048]{2,1,0:T(8,128)(2,1)S(1)}, u32[]{:S(2)}, u32[]{:S(2)}) async-start(bf16[4,32,2048]{2,1,0:T(8,128)(2,1)} %bitcast.6), calls=%async_computation.1 | async-start | bytes 1048576 | tf_op jit(solution)/shard_map/all_to_all | solution.py:157
  112.2 3.5 %all-to-all-done.1 = bf16[4,32,2048]{2,1,0:T(8,128)(2,1)S(1)} async-done(((bf16[4,32,2048]{2,1,0:T(8,128)(2,1)}), bf16[4,32,2048]{2,1,0:T(8,128)(2,1)S(1)}, u32[]{:S(2)}, u32[]{:S(2)}) %all-to-all-start.1) | async-done | bytes 524320 | tf_op jit(solution)/shard_map/all_to_all | solution.py:157
  121.7 22.8 %all-to-all-start.2 = ((bf16[8,4,2048]{2,1,0:T(4,128)(2,1)}), bf16[8,4,2048]{2,1,0:T(4,128)(2,1)S(1)}, u32[]{:S(2)}, u32[]{:S(2)}) async-start(bf16[8,4,2048]{2,1,0:T(4,128)(2,1)} %reshape.188), calls=%async_computation.2 | async-start | bytes 262144 | tf_op jit(solution)/shard_map/all_to_all | solution.py:165
  152.3 14.8 %all-to-all-done.2 = bf16[8,4,2048]{2,1,0:T(4,128)(2,1)S(1)} async-done(((bf16[8,4,2048]{2,1,0:T(4,128)(2,1)}), bf16[8,4,2048]{2,1,0:T(4,128)(2,1)S(1)}, u32[]{:S(2)}, u32[]{:S(2)}) %all-to-all-start.2) | async-done | bytes 131104 | tf_op jit(solution)/shard_map/all_to_all | solution.py:165
  190.0 8.6 %collective-permute-done.29 = bf16[128,1024]{1,0:T(8,128)(2,1)S(1)} collective-permute-done((bf16[128,1024]{1,0:T(8,128)(2,1)S(1)}, bf16[128,1024]{1,0:T(8,128)(2,1)S(1)}, u32[]{:S(2)}, u32[]{:S(2)}) %collective-permute-start.29) | collective-permute-done | bytes 262176 | tf_op jit(solution)/shard_map/ppermute | solution.py:116
  204.0 21.2 %collective-permute-done.31 = bf16[128,1024]{1,0:T(8,128)(2,1)S(1)} collective-permute-done((bf16[128,1024]{1,0:T(8,128)(2,1)S(1)}, bf16[128,1024]{1,0:T(8,128)(2,1)S(1)}, u32[]{:S(2)}, u32[]{:S(2)}) %collective-permute-start.31) | collective-permute-done | bytes 262176 | tf_op jit(solution)/shard_map/ppermute | solution.py:116
  226.3 1.9 collective-permute-start.33
  229.4 1.9 collective-permute-start.32
  231.3 3.3 %collective-permute-done.33 = bf16[128,1024]{1,0:T(8,128)(2,1)S(1)} collective-permute-done((bf16[128,1024]{1,0:T(8,128)(2,1)S(1)}, bf16[128,1024]{1,0:T(8,128)(2,1)S(1)}, u32[]{:S(2)}, u32[]{:S(2)}) %collective-permute-start.33) | collective-permute-done | bytes 262176 | tf_op jit(solution)/shard_map/ppermute | solution.py:116
  235.7 1.9 collective-permute-start.35
  237.7 2.1 collective-permute-done.32
  240.8 1.9 collective-permute-start.34
  245.1 1.9 collective-permute-start.38
  247.1 2.1 collective-permute-done.34
  250.2 1.9 collective-permute-start.36
  252.2 2.2 collective-permute-done.38
  254.4 34.7 %collective-permute-start.39 = (bf16[128,512]{1,0:T(8,128)(2,1)S(1)}, bf16[128,512]{1,0:T(8,128)(2,1)S(1)}, u32[]{:S(2)}, u32[]{:S(2)}) collective-permute-start(bf16[128,512]{1,0:T(8,128)(2,1)S(1)} %slice.51), channel_id=1, source_target_pairs={{0,1},{1,0},{2,3},{3,2},{4,5},{5,4},{6,7},{7,6},{8,9},{9,8},{10,11... | collective-permute-start | bytes 393224 | tf_op jit(solution)/shard_map/ppermute | solution.py:30
  290.4 4.2 %collective-permute-start.37 = (bf16[128,512]{1,0:T(8,128)(2,1)S(1)}, bf16[128,512]{1,0:T(8,128)(2,1)S(1)}, u32[]{:S(2)}, u32[]{:S(2)}) collective-permute-start(bf16[128,512]{1,0:T(8,128)(2,1)S(1)} %slice.49), channel_id=1, source_target_pairs={{0,1},{1,0},{2,3},{3,2},{4,5},{5,4},{6,7},{7,6},{8,9},{9,8},{10,11... | collective-permute-start | bytes 393224 | tf_op jit(solution)/shard_map/ppermute | solution.py:30
  (160 shorter events, 82.7 us)
Async XLA Ops:
  8.2 7.9 %all-to-all-start = ((bf16[4,8,2048]{2,1,0:T(8,128)(2,1)}), bf16[4,8,2048]{2,1,0:T(8,128)(2,1)S(1)}, u32[]{:S(2)}, u32[]{:S(2)}) async-start(bf16[4,8,2048]{2,1,0:T(8,128)(2,1)} %fusion.4), calls=%async_computation | async-start | bytes 262144 | tf_op jit(solution)/shard_map/all_to_all | solution.py:128
  16.1 36.2 %collective-permute-start = (bf16[32,2048]{1,0:T(8,128)(2,1)S(1)}, bf16[32,2048]{1,0:T(8,128)(2,1)S(1)}, u32[]{:S(2)}, u32[]{:S(2)}) collective-permute-start(bf16[32,2048]{1,0:T(8,128)(2,1)S(1)} %bitcast.46), channel_id=1, source_target_pairs={{0,8},{8,0},{1,9},{9,1},{2,10},{10,2},{3,11},{11,3},{4,12},{12,4},... | collective-permute-start | bytes 393224 | tf_op jit(solution)/shard_map/ppermute | solution.py:30
  52.4 9.9 %collective-permute-start.1 = (bf16[64,2048]{1,0:T(8,128)(2,1)S(1)}, bf16[64,2048]{1,0:T(8,128)(2,1)S(1)}, u32[]{:S(2)}, u32[]{:S(2)}) collective-permute-start(bf16[64,2048]{1,0:T(8,128)(2,1)S(1)} %pad_maximum_fusion), channel_id=1, source_target_pairs={{0,6},{2,0},{4,2},{6,4},{1,7},{3,1},{5,3},{7,5},{8,14},{10,8},{12,... | collective-permute-start | bytes 786440 | tf_op jit(solution)/shard_map/ppermute | solution.py:34
  54.5 8.8 %collective-permute-start.2 = (bf16[64,2048]{1,0:T(8,128)(2,1)S(1)}, bf16[64,2048]{1,0:T(8,128)(2,1)S(1)}, u32[]{:S(2)}, u32[]{:S(2)}) collective-permute-start(bf16[64,2048]{1,0:T(8,128)(2,1)S(1)} %pad_maximum_fusion), channel_id=1, source_target_pairs={{0,4},{2,6},{4,0},{6,2},{1,5},{3,7},{5,1},{7,3},{8,12},{10,14},{12... | collective-permute-start | bytes 786440 | tf_op jit(solution)/shard_map/ppermute | solution.py:34
  58.7 7.6 %collective-permute-start.3 = (bf16[64,2048]{1,0:T(8,128)(2,1)S(1)}, bf16[64,2048]{1,0:T(8,128)(2,1)S(1)}, u32[]{:S(2)}, u32[]{:S(2)}) collective-permute-start(bf16[64,2048]{1,0:T(8,128)(2,1)S(1)} %pad_maximum_fusion), channel_id=1, source_target_pairs={{0,2},{2,4},{4,6},{6,0},{1,3},{3,5},{5,7},{7,1},{8,10},{10,12},{12... | collective-permute-start | bytes 786440 | tf_op jit(solution)/shard_map/ppermute | solution.py:34
  66.3 12.8 %collective-permute-start.4 = (bf16[256,2048]{1,0:T(8,128)(2,1)S(1)}, bf16[256,2048]{1,0:T(8,128)(2,1)}, u32[]{:S(2)}, u32[]{:S(2)}) collective-permute-start(bf16[256,2048]{1,0:T(8,128)(2,1)S(1)} %constant_dynamic-update-slice_fusion), channel_id=1, source_target_pairs={{0,1},{1,0},{2,3},{3,2},{4,5},{5,4},{6,7},{7,6},{8,9},{9,8},{10,11... | collective-permute-start | bytes 3145736 | tf_op jit(solution)/shard_map/ppermute | solution.py:30
  85.3 8.4 %collective-permute-start.6 = (bf16[256,512]{1,0:T(8,128)(2,1)S(1)}, bf16[256,512]{1,0:T(8,128)(2,1)S(1)}, u32[]{:S(2)}, u32[]{:S(2)}) collective-permute-start(bf16[256,512]{1,0:T(8,128)(2,1)S(1)} %get-tuple-element.91), channel_id=1, source_target_pairs={{0,1},{1,0},{2,3},{3,2},{4,5},{5,4},{6,7},{7,6},{8,9},{9,8},{10,11... | collective-permute-start | bytes 786440 | tf_op jit(solution)/shard_map/ppermute | solution.py:30
  89.3 6.5 %collective-permute-start.8 = (bf16[256,512]{1,0:T(8,128)(2,1)S(1)}, bf16[256,512]{1,0:T(8,128)(2,1)S(1)}, u32[]{:S(2)}, u32[]{:S(2)}) collective-permute-start(bf16[256,512]{1,0:T(8,128)(2,1)S(1)} %fusion.5), channel_id=1, source_target_pairs={{0,1},{1,0},{2,3},{3,2},{4,5},{5,4},{6,7},{7,6},{8,9},{9,8},{10,11... | collective-permute-start | bytes 786440 | tf_op jit(solution)/shard_map/ppermute | solution.py:30
  91.4 9.0 %collective-permute-start.5 = (bf16[128,2048]{1,0:T(8,128)(2,1)S(1)}, bf16[128,2048]{1,0:T(8,128)(2,1)S(1)}, u32[]{:S(2)}, u32[]{:S(2)}) collective-permute-start(bf16[128,2048]{1,0:T(8,128)(2,1)S(1)} %constant_dynamic-slice_fusion.2), channel_id=1, source_target_pairs={{0,1},{1,0},{2,3},{3,2},{4,5},{5,4},{6,7},{7,6},{8,9},{9,8},{10,11... | collective-permute-start | bytes 1572872 | tf_op jit(solution)/shard_map/ppermute | solution.py:30
  95.1 6.3 %collective-permute-start.7 = (bf16[128,1024]{1,0:T(8,128)(2,1)S(1)}, bf16[128,1024]{1,0:T(8,128)(2,1)S(1)}, u32[]{:S(2)}, u32[]{:S(2)}) collective-permute-start(bf16[128,1024]{1,0:T(8,128)(2,1)S(1)} %constant_dynamic-slice_fusion.1), channel_id=1, source_target_pairs={{0,64},{64,128},{961,897},{897,833},{2,66},{66,130},{963,899},{899... | collective-permute-start | bytes 786440 | tf_op jit(solution)/shard_map/ppermute | solution.py:116
  99.1 10.0 %collective-permute-start.10 = (bf16[128,1024]{1,0:T(8,128)(2,1)S(1)}, bf16[128,1024]{1,0:T(8,128)(2,1)}, u32[]{:S(2)}, u32[]{:S(2)}) collective-permute-start(bf16[128,1024]{1,0:T(8,128)(2,1)S(1)} %constant_dynamic-slice_fusion), channel_id=1, source_target_pairs={{0,64},{64,128},{961,897},{897,833},{2,66},{66,130},{963,899},{899... | collective-permute-start | bytes 786440 | tf_op jit(solution)/shard_map/ppermute | solution.py:116
  101.4 14.3 %all-to-all-start.1 = ((bf16[4,32,2048]{2,1,0:T(8,128)(2,1)}), bf16[4,32,2048]{2,1,0:T(8,128)(2,1)S(1)}, u32[]{:S(2)}, u32[]{:S(2)}) async-start(bf16[4,32,2048]{2,1,0:T(8,128)(2,1)} %bitcast.6), calls=%async_computation.1 | async-start | bytes 1048576 | tf_op jit(solution)/shard_map/all_to_all | solution.py:157
  108.4 3.8 %collective-permute-start.9 = (bf16[128,1024]{1,0:T(8,128)(2,1)S(1)}, bf16[128,1024]{1,0:T(8,128)(2,1)S(1)}, u32[]{:S(2)}, u32[]{:S(2)}) collective-permute-start(bf16[128,1024]{1,0:T(8,128)(2,1)S(1)} %select_add_fusion.27), channel_id=1, source_target_pairs={{0,64},{64,128},{961,897},{897,833},{2,66},{66,130},{963,899},{899... | collective-permute-start | bytes 786440 | tf_op jit(solution)/shard_map/ppermute | solution.py:116
  110.2 7.2 %collective-permute-start.12 = (bf16[128,1024]{1,0:T(8,128)(2,1)S(1)}, bf16[128,1024]{1,0:T(8,128)(2,1)}, u32[]{:S(2)}, u32[]{:S(2)}) collective-permute-start(bf16[128,1024]{1,0:T(8,128)(2,1)S(1)} %select_add_fusion.26), channel_id=1, source_target_pairs={{0,64},{64,128},{961,897},{897,833},{2,66},{66,130},{963,899},{899... | collective-permute-start | bytes 786440 | tf_op jit(solution)/shard_map/ppermute | solution.py:116
  116.7 27.7 %collective-permute-start.11 = (bf16[128,1024]{1,0:T(8,128)(2,1)S(1)}, bf16[128,1024]{1,0:T(8,128)(2,1)S(1)}, u32[]{:S(2)}, u32[]{:S(2)}) collective-permute-start(bf16[128,1024]{1,0:T(8,128)(2,1)S(1)} %select_add_fusion.25), channel_id=1, source_target_pairs={{0,64},{64,128},{128,192},{192,256},{961,897},{897,833},{833,769},... | collective-permute-start | bytes 786440 | tf_op jit(solution)/shard_map/ppermute | solution.py:116
  118.5 27.7 %collective-permute-start.14 = (bf16[128,1024]{1,0:T(8,128)(2,1)S(1)}, bf16[128,1024]{1,0:T(8,128)(2,1)}, u32[]{:S(2)}, u32[]{:S(2)}) collective-permute-start(bf16[128,1024]{1,0:T(8,128)(2,1)S(1)} %select_add_fusion.24), channel_id=1, source_target_pairs={{0,64},{64,128},{128,192},{192,256},{961,897},{897,833},{833,769},... | collective-permute-start | bytes 786440 | tf_op jit(solution)/shard_map/ppermute | solution.py:116
  121.7 45.4 %all-to-all-start.2 = ((bf16[8,4,2048]{2,1,0:T(4,128)(2,1)}), bf16[8,4,2048]{2,1,0:T(4,128)(2,1)S(1)}, u32[]{:S(2)}, u32[]{:S(2)}) async-start(bf16[8,4,2048]{2,1,0:T(4,128)(2,1)} %reshape.188), calls=%async_computation.2 | async-start | bytes 262144 | tf_op jit(solution)/shard_map/all_to_all | solution.py:165
  145.5 3.2 %collective-permute-start.13 = (bf16[128,1024]{1,0:T(8,128)(2,1)S(1)}, bf16[128,1024]{1,0:T(8,128)(2,1)S(1)}, u32[]{:S(2)}, u32[]{:S(2)}) collective-permute-start(bf16[128,1024]{1,0:T(8,128)(2,1)S(1)} %select_add_fusion.23), channel_id=1, source_target_pairs={{0,64},{64,128},{128,192},{192,256},{961,897},{897,833},{833,769},... | collective-permute-start | bytes 786440 | tf_op jit(solution)/shard_map/ppermute | solution.py:116
  149.8 17.4 %collective-permute-start.15 = (bf16[128,1024]{1,0:T(8,128)(2,1)S(1)}, bf16[128,1024]{1,0:T(8,128)(2,1)S(1)}, u32[]{:S(2)}, u32[]{:S(2)}) collective-permute-start(bf16[128,1024]{1,0:T(8,128)(2,1)S(1)} %select_add_fusion.21), channel_id=1, source_target_pairs={{0,64},{64,128},{128,192},{192,256},{256,320},{320,384},{961,897},... | collective-permute-start | bytes 786440 | tf_op jit(solution)/shard_map/ppermute | solution.py:116
  151.6 17.4 %collective-permute-start.17 = (bf16[128,1024]{1,0:T(8,128)(2,1)S(1)}, bf16[128,1024]{1,0:T(8,128)(2,1)S(1)}, u32[]{:S(2)}, u32[]{:S(2)}) collective-permute-start(bf16[128,1024]{1,0:T(8,128)(2,1)S(1)} %select_add_fusion.20), channel_id=1, source_target_pairs={{0,64},{64,128},{128,192},{192,256},{256,320},{320,384},{961,897},... | collective-permute-start | bytes 786440 | tf_op jit(solution)/shard_map/ppermute | solution.py:116
  186.3 12.3 %collective-permute-start.29 = (bf16[128,1024]{1,0:T(8,128)(2,1)S(1)}, bf16[128,1024]{1,0:T(8,128)(2,1)S(1)}, u32[]{:S(2)}, u32[]{:S(2)}) collective-permute-start(bf16[128,1024]{1,0:T(8,128)(2,1)S(1)} %select_add_fusion.9), channel_id=1, source_target_pairs={{0,64},{64,128},{128,192},{192,256},{256,320},{320,384},{384,448},... | collective-permute-start | bytes 786440 | tf_op jit(solution)/shard_map/ppermute | solution.py:116
  188.7 12.9 %collective-permute-start.28 = (bf16[128,1024]{1,0:T(8,128)(2,1)S(1)}, bf16[128,1024]{1,0:T(8,128)(2,1)S(1)}, u32[]{:S(2)}, u32[]{:S(2)}) collective-permute-start(bf16[128,1024]{1,0:T(8,128)(2,1)S(1)} %select_add_fusion.8), channel_id=1, source_target_pairs={{0,64},{64,128},{128,192},{192,256},{256,320},{320,384},{384,448},... | collective-permute-start | bytes 786440 | tf_op jit(solution)/shard_map/ppermute | solution.py:116
  199.7 25.6 %collective-permute-start.31 = (bf16[128,1024]{1,0:T(8,128)(2,1)S(1)}, bf16[128,1024]{1,0:T(8,128)(2,1)S(1)}, u32[]{:S(2)}, u32[]{:S(2)}) collective-permute-start(bf16[128,1024]{1,0:T(8,128)(2,1)S(1)} %select_add_fusion.7), channel_id=1, source_target_pairs={{0,64},{64,128},{128,192},{192,256},{256,320},{320,384},{384,448},... | collective-permute-start | bytes 786440 | tf_op jit(solution)/shard_map/ppermute | solution.py:116
  202.7 25.6 %collective-permute-start.30 = (bf16[128,1024]{1,0:T(8,128)(2,1)S(1)}, bf16[128,1024]{1,0:T(8,128)(2,1)S(1)}, u32[]{:S(2)}, u32[]{:S(2)}) collective-permute-start(bf16[128,1024]{1,0:T(8,128)(2,1)S(1)} %select_add_fusion.6), channel_id=1, source_target_pairs={{0,64},{64,128},{128,192},{192,256},{256,320},{320,384},{384,448},... | collective-permute-start | bytes 786440 | tf_op jit(solution)/shard_map/ppermute | solution.py:116
  226.3 8.3 %collective-permute-start.33 = (bf16[128,1024]{1,0:T(8,128)(2,1)S(1)}, bf16[128,1024]{1,0:T(8,128)(2,1)S(1)}, u32[]{:S(2)}, u32[]{:S(2)}) collective-permute-start(bf16[128,1024]{1,0:T(8,128)(2,1)S(1)} %select_add_fusion.5), channel_id=1, source_target_pairs={{0,64},{64,128},{128,192},{192,256},{256,320},{320,384},{384,448},... | collective-permute-start | bytes 786440 | tf_op jit(solution)/shard_map/ppermute | solution.py:116
  229.4 10.4 %collective-permute-start.32 = (bf16[128,1024]{1,0:T(8,128)(2,1)S(1)}, bf16[128,1024]{1,0:T(8,128)(2,1)S(1)}, u32[]{:S(2)}, u32[]{:S(2)}) collective-permute-start(bf16[128,1024]{1,0:T(8,128)(2,1)S(1)} %select_add_fusion.4), channel_id=1, source_target_pairs={{0,64},{64,128},{128,192},{192,256},{256,320},{320,384},{384,448},... | collective-permute-start | bytes 786440 | tf_op jit(solution)/shard_map/ppermute | solution.py:116
  235.7 8.3 %collective-permute-start.35 = (bf16[128,1024]{1,0:T(8,128)(2,1)S(1)}, bf16[128,1024]{1,0:T(8,128)(2,1)S(1)}, u32[]{:S(2)}, u32[]{:S(2)}) collective-permute-start(bf16[128,1024]{1,0:T(8,128)(2,1)S(1)} %select_add_fusion.3), channel_id=1, source_target_pairs={{0,64},{64,128},{128,192},{192,256},{256,320},{320,384},{384,448},... | collective-permute-start | bytes 786440 | tf_op jit(solution)/shard_map/ppermute | solution.py:116
  240.8 8.3 %collective-permute-start.34 = (bf16[128,1024]{1,0:T(8,128)(2,1)S(1)}, bf16[128,1024]{1,0:T(8,128)(2,1)S(1)}, u32[]{:S(2)}, u32[]{:S(2)}) collective-permute-start(bf16[128,1024]{1,0:T(8,128)(2,1)S(1)} %select_add_fusion.2), channel_id=1, source_target_pairs={{0,64},{64,128},{128,192},{192,256},{256,320},{320,384},{384,448},... | collective-permute-start | bytes 786440 | tf_op jit(solution)/shard_map/ppermute | solution.py:116
  245.1 9.2 %collective-permute-start.38 = (bf16[128,1024]{1,0:T(8,128)(2,1)S(1)}, bf16[128,1024]{1,0:T(8,128)(2,1)S(1)}, u32[]{:S(2)}, u32[]{:S(2)}) collective-permute-start(bf16[128,1024]{1,0:T(8,128)(2,1)S(1)} %select_add_fusion.1), channel_id=1, source_target_pairs={{0,64},{64,128},{128,192},{192,256},{256,320},{320,384},{384,448},... | collective-permute-start | bytes 786440 | tf_op jit(solution)/shard_map/ppermute | solution.py:116
  250.2 40.1 %collective-permute-start.36 = (bf16[128,1024]{1,0:T(8,128)(2,1)S(1)}, bf16[128,1024]{1,0:T(8,128)(2,1)S(1)}, u32[]{:S(2)}, u32[]{:S(2)}) collective-permute-start(bf16[128,1024]{1,0:T(8,128)(2,1)S(1)} %select_add_fusion), channel_id=1, source_target_pairs={{0,64},{64,128},{128,192},{192,256},{256,320},{320,384},{384,448},... | collective-permute-start | bytes 786440 | tf_op jit(solution)/shard_map/ppermute | solution.py:116
  254.4 40.2 %collective-permute-start.39 = (bf16[128,512]{1,0:T(8,128)(2,1)S(1)}, bf16[128,512]{1,0:T(8,128)(2,1)S(1)}, u32[]{:S(2)}, u32[]{:S(2)}) collective-permute-start(bf16[128,512]{1,0:T(8,128)(2,1)S(1)} %slice.51), channel_id=1, source_target_pairs={{0,1},{1,0},{2,3},{3,2},{4,5},{5,4},{6,7},{7,6},{8,9},{9,8},{10,11... | collective-permute-start | bytes 393224 | tf_op jit(solution)/shard_map/ppermute | solution.py:30
  290.4 6.0 %collective-permute-start.37 = (bf16[128,512]{1,0:T(8,128)(2,1)S(1)}, bf16[128,512]{1,0:T(8,128)(2,1)S(1)}, u32[]{:S(2)}, u32[]{:S(2)}) collective-permute-start(bf16[128,512]{1,0:T(8,128)(2,1)S(1)} %slice.49), channel_id=1, source_target_pairs={{0,1},{1,0},{2,3},{3,2},{4,5},{5,4},{6,7},{7,6},{8,9},{9,8},{10,11... | collective-permute-start | bytes 393224 | tf_op jit(solution)/shard_map/ppermute | solution.py:30
  (20 other events, 382.9 us)

commit v8 on v7

--- a/solution.py
+++ b/solution.py
@@ -132,12 +132,9 @@
     )
     own, across = gather_plane(jnp.concatenate([got, far], axis=0))
 
-    def in_order(order):
-        half = order.shape[1] // 2
-        total = dot_f32(order[:, :half], own, ((1,), (0,)))
-        return (total + dot_f32(order[:, half:], across, ((1,), (0,)))).astype(jnp.bfloat16)
-
-    x_all, g_all = in_order(order_x), in_order(order_g)
+    rows = jnp.concatenate(lax.optimization_barrier((own, across)), axis=0)
+    x_all = dot_f32(order_x, rows, ((1,), (0,))).astype(jnp.bfloat16)
+    g_all = dot_f32(order_g, rows, ((1,), (0,))).astype(jnp.bfloat16)
     pre_act = dot_f32(x_all, w_in, ((1,), (0,)))
     value, slope = gelu_pair(pre_act)
     hidden = value.astype(jnp.bfloat16)

time: 301 us -> 298 us (0.990)
  matrix products: 17.3 us -> 13.5 us
    dot_general x15 -> x13, matrix products: 17.3 us -> 13.5 us  [dot_f32(): lax.dot_general(a, b, (dims, ((), ())), preferred_element_type=jnp.float32)]
  transfers between devices with their start and end apart: 43 -> 43, of which waited for: 15 -> 15; matrix products, arithmetic and copies ran while one was open for 14% -> 15% of each run, Pallas kernels for 0% -> 0%
where the time goes in v8:
time: 298 us; the launch traced here: 296 us
  starting transfers between devices  158 us (53%)
  waiting for transfers between devices  78.2 us (26%)
  other arithmetic  37.9 us (13%)
  matrix products  13.5 us (5%)
  local copies, waits for them, and re-layouts  6.24 us (2%)
    ppermute x7, starting transfers between devices, swap(): return lax.ppermute(value, axis, [(0, 1), (1, 0)])  82 us
    ppermute x30, waiting for transfers between devices, line_sums(): carried[k], last = (lax.ppermute(term, ('group', 'core'), pairs), term)  41.6 us
    ppermute x30, starting transfers between devices, line_sums(): carried[k], last = (lax.ppermute(term, ('group', 'core'), pairs), term)  33.2 us
    add x28, other arithmetic, line_sums(): term + jnp.where(rank <= step, carried[k], jnp.zeros_like(carried[k]))  30.2 us
    all_to_all x1, starting transfers between devices, home(): lax.all_to_all(parts, ('x', 'zh'), 0, 0, tiled=True)  22.8 us
    all_to_all x1, waiting for transfers between devices, home(): lax.all_to_all(parts, ('x', 'zh'), 0, 0, tiled=True)  14.8 us
    dot_general x13, matrix products, dot_f32(): lax.dot_general(a, b, (dims, ((), ())), preferred_element_type=jnp.float32)  13.5 us
    ppermute x7, waiting for transfers between devices, swap(): return lax.ppermute(value, axis, [(0, 1), (1, 0)])  10.7 us
  transfers between devices with their start and end apart: 43, of which 15 were waited for; matrix products, arithmetic and copies ran while one was open for 15% of the time, Pallas kernels for 0%

profile of v8, /device:TPU:107, one launch (start us, length us, event | category | flops | bytes accessed | tf_op | source)
XLA Modules:
  0.0 295.6 jit_solution(5663646975401521600)
XLA Ops:
  6.2 2.0 fusion.2
  8.2 4.3 %all-to-all-start = ((bf16[4,8,2048]{2,1,0:T(8,128)(2,1)}), bf16[4,8,2048]{2,1,0:T(8,128)(2,1)S(1)}, u32[]{:S(2)}, u32[]{:S(2)}) async-start(bf16[4,8,2048]{2,1,0:T(8,128)(2,1)} %fusion.2), calls=%async_computation | async-start | bytes 262144 | tf_op jit(solution)/shard_map/all_to_all | solution.py:128
  12.6 3.5 %all-to-all-done = bf16[4,8,2048]{2,1,0:T(8,128)(2,1)S(1)} async-done(((bf16[4,8,2048]{2,1,0:T(8,128)(2,1)}), bf16[4,8,2048]{2,1,0:T(8,128)(2,1)S(1)}, u32[]{:S(2)}, u32[]{:S(2)}) %all-to-all-start) | async-done | bytes 131104 | tf_op jit(solution)/shard_map/all_to_all | solution.py:128
  16.1 26.0 %collective-permute-start = (bf16[32,2048]{1,0:T(8,128)(2,1)S(1)}, bf16[32,2048]{1,0:T(8,128)(2,1)S(1)}, u32[]{:S(2)}, u32[]{:S(2)}) collective-permute-start(bf16[32,2048]{1,0:T(8,128)(2,1)S(1)} %bitcast.46), channel_id=1, source_target_pairs={{0,8},{8,0},{1,9},{9,1},{2,10},{10,2},{3,11},{11,3},{4,12},{12,4},... | collective-permute-start | bytes 393224 | tf_op jit(solution)/shard_map/ppermute | solution.py:30
  43.4 8.9 %collective-permute-done = bf16[32,2048]{1,0:T(8,128)(2,1)S(1)} collective-permute-done((bf16[32,2048]{1,0:T(8,128)(2,1)S(1)}, bf16[32,2048]{1,0:T(8,128)(2,1)S(1)}, u32[]{:S(2)}, u32[]{:S(2)}) %collective-permute-start) | collective-permute-done | bytes 131104 | tf_op jit(solution)/shard_map/ppermute | solution.py:30
  52.4 2.1 collective-permute-start.1
  54.5 4.2 %collective-permute-start.2 = (bf16[64,2048]{1,0:T(8,128)(2,1)S(1)}, bf16[64,2048]{1,0:T(8,128)(2,1)S(1)}, u32[]{:S(2)}, u32[]{:S(2)}) collective-permute-start(bf16[64,2048]{1,0:T(8,128)(2,1)S(1)} %pad_maximum_fusion), channel_id=1, source_target_pairs={{0,4},{2,6},{4,0},{6,2},{1,5},{3,7},{5,1},{7,3},{8,12},{10,14},{12... | collective-permute-start | bytes 786440 | tf_op jit(solution)/shard_map/ppermute | solution.py:34
  58.7 3.5 %collective-permute-start.3 = (bf16[64,2048]{1,0:T(8,128)(2,1)S(1)}, bf16[64,2048]{1,0:T(8,128)(2,1)S(1)}, u32[]{:S(2)}, u32[]{:S(2)}) collective-permute-start(bf16[64,2048]{1,0:T(8,128)(2,1)S(1)} %pad_maximum_fusion), channel_id=1, source_target_pairs={{0,2},{2,4},{4,6},{6,0},{1,3},{3,5},{5,7},{7,1},{8,10},{10,12},{12... | collective-permute-start | bytes 786440 | tf_op jit(solution)/shard_map/ppermute | solution.py:34
  63.3 3.0 %collective-permute-done.3 = bf16[64,2048]{1,0:T(8,128)(2,1)S(1)} collective-permute-done((bf16[64,2048]{1,0:T(8,128)(2,1)S(1)}, bf16[64,2048]{1,0:T(8,128)(2,1)S(1)}, u32[]{:S(2)}, u32[]{:S(2)}) %collective-permute-start.3) | collective-permute-done | bytes 262176 | tf_op jit(solution)/shard_map/ppermute | solution.py:34
  66.3 10.4 %collective-permute-start.4 = (bf16[256,2048]{1,0:T(8,128)(2,1)S(1)}, bf16[256,2048]{1,0:T(8,128)(2,1)}, u32[]{:S(2)}, u32[]{:S(2)}) collective-permute-start(bf16[256,2048]{1,0:T(8,128)(2,1)S(1)} %constant_dynamic-update-slice_fusion), channel_id=1, source_target_pairs={{0,1},{1,0},{2,3},{3,2},{4,5},{5,4},{6,7},{7,6},{8,9},{9,8},{10,11... | collective-permute-start | bytes 3145736 | tf_op jit(solution)/shard_map/ppermute | solution.py:30
  82.9 2.3 collective-permute-start.6
  86.9 2.0 collective-permute-start.8
  89.0 2.3 collective-permute-start.5
  94.8 1.9 copy-done.2
  99.0 6.0 %all-to-all-start.1 = ((bf16[4,32,2048]{2,1,0:T(8,128)(2,1)}), bf16[4,32,2048]{2,1,0:T(8,128)(2,1)S(1)}, u32[]{:S(2)}, u32[]{:S(2)}) async-start(bf16[4,32,2048]{2,1,0:T(8,128)(2,1)} %bitcast.6), calls=%async_computation.1 | async-start | bytes 1048576 | tf_op jit(solution)/shard_map/all_to_all | solution.py:154
  109.8 3.5 %all-to-all-done.1 = bf16[4,32,2048]{2,1,0:T(8,128)(2,1)S(1)} async-done(((bf16[4,32,2048]{2,1,0:T(8,128)(2,1)}), bf16[4,32,2048]{2,1,0:T(8,128)(2,1)S(1)}, u32[]{:S(2)}, u32[]{:S(2)}) %all-to-all-start.1) | async-done | bytes 524320 | tf_op jit(solution)/shard_map/all_to_all | solution.py:154
  119.3 22.8 %all-to-all-start.2 = ((bf16[8,4,2048]{2,1,0:T(4,128)(2,1)}), bf16[8,4,2048]{2,1,0:T(4,128)(2,1)S(1)}, u32[]{:S(2)}, u32[]{:S(2)}) async-start(bf16[8,4,2048]{2,1,0:T(4,128)(2,1)} %reshape.188), calls=%async_computation.2 | async-start | bytes 262144 | tf_op jit(solution)/shard_map/all_to_all | solution.py:162
  149.9 14.8 %all-to-all-done.2 = bf16[8,4,2048]{2,1,0:T(4,128)(2,1)S(1)} async-done(((bf16[8,4,2048]{2,1,0:T(4,128)(2,1)}), bf16[8,4,2048]{2,1,0:T(4,128)(2,1)S(1)}, u32[]{:S(2)}, u32[]{:S(2)}) %all-to-all-start.2) | async-done | bytes 131104 | tf_op jit(solution)/shard_map/all_to_all | solution.py:162
  187.6 8.6 %collective-permute-done.29 = bf16[128,1024]{1,0:T(8,128)(2,1)S(1)} collective-permute-done((bf16[128,1024]{1,0:T(8,128)(2,1)S(1)}, bf16[128,1024]{1,0:T(8,128)(2,1)S(1)}, u32[]{:S(2)}, u32[]{:S(2)}) %collective-permute-start.29) | collective-permute-done | bytes 262176 | tf_op jit(solution)/shard_map/ppermute | solution.py:116
  201.6 21.2 %collective-permute-done.31 = bf16[128,1024]{1,0:T(8,128)(2,1)S(1)} collective-permute-done((bf16[128,1024]{1,0:T(8,128)(2,1)S(1)}, bf16[128,1024]{1,0:T(8,128)(2,1)S(1)}, u32[]{:S(2)}, u32[]{:S(2)}) %collective-permute-start.31) | collective-permute-done | bytes 262176 | tf_op jit(solution)/shard_map/ppermute | solution.py:116
  223.9 1.9 collective-permute-start.33
  226.9 1.9 collective-permute-start.32
  228.9 3.3 %collective-permute-done.33 = bf16[128,1024]{1,0:T(8,128)(2,1)S(1)} collective-permute-done((bf16[128,1024]{1,0:T(8,128)(2,1)S(1)}, bf16[128,1024]{1,0:T(8,128)(2,1)S(1)}, u32[]{:S(2)}, u32[]{:S(2)}) %collective-permute-start.33) | collective-permute-done | bytes 262176 | tf_op jit(solution)/shard_map/ppermute | solution.py:116
  233.3 1.9 collective-permute-start.35
  235.2 1.9 collective-permute-done.32
  238.3 1.9 collective-permute-start.34
  242.7 1.9 collective-permute-start.38
  244.6 1.9 collective-permute-done.34
  247.7 1.9 collective-permute-start.36
  249.6 2.4 collective-permute-done.38
  252.0 34.8 %collective-permute-start.39 = (bf16[128,512]{1,0:T(8,128)(2,1)S(1)}, bf16[128,512]{1,0:T(8,128)(2,1)S(1)}, u32[]{:S(2)}, u32[]{:S(2)}) collective-permute-start(bf16[128,512]{1,0:T(8,128)(2,1)S(1)} %slice.35), channel_id=1, source_target_pairs={{0,1},{1,0},{2,3},{3,2},{4,5},{5,4},{6,7},{7,6},{8,9},{9,8},{10,11... | collective-permute-start | bytes 393224 | tf_op jit(solution)/shard_map/ppermute | solution.py:30
  288.0 4.2 %collective-permute-start.37 = (bf16[128,512]{1,0:T(8,128)(2,1)S(1)}, bf16[128,512]{1,0:T(8,128)(2,1)S(1)}, u32[]{:S(2)}, u32[]{:S(2)}) collective-permute-start(bf16[128,512]{1,0:T(8,128)(2,1)S(1)} %slice.33), channel_id=1, source_target_pairs={{0,1},{1,0},{2,3},{3,2},{4,5},{5,4},{6,7},{7,6},{8,9},{9,8},{10,11... | collective-permute-start | bytes 393224 | tf_op jit(solution)/shard_map/ppermute | solution.py:30
  (162 shorter events, 80.4 us)
Async XLA Ops:
  8.2 7.9 %all-to-all-start = ((bf16[4,8,2048]{2,1,0:T(8,128)(2,1)}), bf16[4,8,2048]{2,1,0:T(8,128)(2,1)S(1)}, u32[]{:S(2)}, u32[]{:S(2)}) async-start(bf16[4,8,2048]{2,1,0:T(8,128)(2,1)} %fusion.2), calls=%async_computation | async-start | bytes 262144 | tf_op jit(solution)/shard_map/all_to_all | solution.py:128
  16.1 36.2 %collective-permute-start = (bf16[32,2048]{1,0:T(8,128)(2,1)S(1)}, bf16[32,2048]{1,0:T(8,128)(2,1)S(1)}, u32[]{:S(2)}, u32[]{:S(2)}) collective-permute-start(bf16[32,2048]{1,0:T(8,128)(2,1)S(1)} %bitcast.46), channel_id=1, source_target_pairs={{0,8},{8,0},{1,9},{9,1},{2,10},{10,2},{3,11},{11,3},{4,12},{12,4},... | collective-permute-start | bytes 393224 | tf_op jit(solution)/shard_map/ppermute | solution.py:30
  52.4 9.9 %collective-permute-start.1 = (bf16[64,2048]{1,0:T(8,128)(2,1)S(1)}, bf16[64,2048]{1,0:T(8,128)(2,1)S(1)}, u32[]{:S(2)}, u32[]{:S(2)}) collective-permute-start(bf16[64,2048]{1,0:T(8,128)(2,1)S(1)} %pad_maximum_fusion), channel_id=1, source_target_pairs={{0,6},{2,0},{4,2},{6,4},{1,7},{3,1},{5,3},{7,5},{8,14},{10,8},{12,... | collective-permute-start | bytes 786440 | tf_op jit(solution)/shard_map/ppermute | solution.py:34
  54.5 8.8 %collective-permute-start.2 = (bf16[64,2048]{1,0:T(8,128)(2,1)S(1)}, bf16[64,2048]{1,0:T(8,128)(2,1)S(1)}, u32[]{:S(2)}, u32[]{:S(2)}) collective-permute-start(bf16[64,2048]{1,0:T(8,128)(2,1)S(1)} %pad_maximum_fusion), channel_id=1, source_target_pairs={{0,4},{2,6},{4,0},{6,2},{1,5},{3,7},{5,1},{7,3},{8,12},{10,14},{12... | collective-permute-start | bytes 786440 | tf_op jit(solution)/shard_map/ppermute | solution.py:34
  58.7 7.6 %collective-permute-start.3 = (bf16[64,2048]{1,0:T(8,128)(2,1)S(1)}, bf16[64,2048]{1,0:T(8,128)(2,1)S(1)}, u32[]{:S(2)}, u32[]{:S(2)}) collective-permute-start(bf16[64,2048]{1,0:T(8,128)(2,1)S(1)} %pad_maximum_fusion), channel_id=1, source_target_pairs={{0,2},{2,4},{4,6},{6,0},{1,3},{3,5},{5,7},{7,1},{8,10},{10,12},{12... | collective-permute-start | bytes 786440 | tf_op jit(solution)/shard_map/ppermute | solution.py:34
  66.3 12.8 %collective-permute-start.4 = (bf16[256,2048]{1,0:T(8,128)(2,1)S(1)}, bf16[256,2048]{1,0:T(8,128)(2,1)}, u32[]{:S(2)}, u32[]{:S(2)}) collective-permute-start(bf16[256,2048]{1,0:T(8,128)(2,1)S(1)} %constant_dynamic-update-slice_fusion), channel_id=1, source_target_pairs={{0,1},{1,0},{2,3},{3,2},{4,5},{5,4},{6,7},{7,6},{8,9},{9,8},{10,11... | collective-permute-start | bytes 3145736 | tf_op jit(solution)/shard_map/ppermute | solution.py:30
  82.9 8.4 %collective-permute-start.6 = (bf16[256,512]{1,0:T(8,128)(2,1)S(1)}, bf16[256,512]{1,0:T(8,128)(2,1)S(1)}, u32[]{:S(2)}, u32[]{:S(2)}) collective-permute-start(bf16[256,512]{1,0:T(8,128)(2,1)S(1)} %get-tuple-element.95), channel_id=1, source_target_pairs={{0,1},{1,0},{2,3},{3,2},{4,5},{5,4},{6,7},{7,6},{8,9},{9,8},{10,11... | collective-permute-start | bytes 786440 | tf_op jit(solution)/shard_map/ppermute | solution.py:30
  86.9 6.5 %collective-permute-start.8 = (bf16[256,512]{1,0:T(8,128)(2,1)S(1)}, bf16[256,512]{1,0:T(8,128)(2,1)S(1)}, u32[]{:S(2)}, u32[]{:S(2)}) collective-permute-start(bf16[256,512]{1,0:T(8,128)(2,1)S(1)} %fusion.3), channel_id=1, source_target_pairs={{0,1},{1,0},{2,3},{3,2},{4,5},{5,4},{6,7},{7,6},{8,9},{9,8},{10,11... | collective-permute-start | bytes 786440 | tf_op jit(solution)/shard_map/ppermute | solution.py:30
  89.0 9.0 %collective-permute-start.5 = (bf16[128,2048]{1,0:T(8,128)(2,1)S(1)}, bf16[128,2048]{1,0:T(8,128)(2,1)S(1)}, u32[]{:S(2)}, u32[]{:S(2)}) collective-permute-start(bf16[128,2048]{1,0:T(8,128)(2,1)S(1)} %constant_dynamic-slice_fusion.2), channel_id=1, source_target_pairs={{0,1},{1,0},{2,3},{3,2},{4,5},{5,4},{6,7},{7,6},{8,9},{9,8},{10,11... | collective-permute-start | bytes 1572872 | tf_op jit(solution)/shard_map/ppermute | solution.py:30
  92.7 6.3 %collective-permute-start.7 = (bf16[128,1024]{1,0:T(8,128)(2,1)S(1)}, bf16[128,1024]{1,0:T(8,128)(2,1)S(1)}, u32[]{:S(2)}, u32[]{:S(2)}) collective-permute-start(bf16[128,1024]{1,0:T(8,128)(2,1)S(1)} %constant_dynamic-slice_fusion.1), channel_id=1, source_target_pairs={{0,64},{64,128},{961,897},{897,833},{2,66},{66,130},{963,899},{899... | collective-permute-start | bytes 786440 | tf_op jit(solution)/shard_map/ppermute | solution.py:116
  96.7 10.0 %collective-permute-start.10 = (bf16[128,1024]{1,0:T(8,128)(2,1)S(1)}, bf16[128,1024]{1,0:T(8,128)(2,1)}, u32[]{:S(2)}, u32[]{:S(2)}) collective-permute-start(bf16[128,1024]{1,0:T(8,128)(2,1)S(1)} %constant_dynamic-slice_fusion), channel_id=1, source_target_pairs={{0,64},{64,128},{961,897},{897,833},{2,66},{66,130},{963,899},{899... | collective-permute-start | bytes 786440 | tf_op jit(solution)/shard_map/ppermute | solution.py:116
  99.0 14.3 %all-to-all-start.1 = ((bf16[4,32,2048]{2,1,0:T(8,128)(2,1)}), bf16[4,32,2048]{2,1,0:T(8,128)(2,1)S(1)}, u32[]{:S(2)}, u32[]{:S(2)}) async-start(bf16[4,32,2048]{2,1,0:T(8,128)(2,1)} %bitcast.6), calls=%async_computation.1 | async-start | bytes 1048576 | tf_op jit(solution)/shard_map/all_to_all | solution.py:154
  106.0 3.7 %collective-permute-start.9 = (bf16[128,1024]{1,0:T(8,128)(2,1)S(1)}, bf16[128,1024]{1,0:T(8,128)(2,1)S(1)}, u32[]{:S(2)}, u32[]{:S(2)}) collective-permute-start(bf16[128,1024]{1,0:T(8,128)(2,1)S(1)} %select_add_fusion.27), channel_id=1, source_target_pairs={{0,64},{64,128},{961,897},{897,833},{2,66},{66,130},{963,899},{899... | collective-permute-start | bytes 786440 | tf_op jit(solution)/shard_map/ppermute | solution.py:116
  107.8 7.2 %collective-permute-start.12 = (bf16[128,1024]{1,0:T(8,128)(2,1)S(1)}, bf16[128,1024]{1,0:T(8,128)(2,1)}, u32[]{:S(2)}, u32[]{:S(2)}) collective-permute-start(bf16[128,1024]{1,0:T(8,128)(2,1)S(1)} %select_add_fusion.26), channel_id=1, source_target_pairs={{0,64},{64,128},{961,897},{897,833},{2,66},{66,130},{963,899},{899... | collective-permute-start | bytes 786440 | tf_op jit(solution)/shard_map/ppermute | solution.py:116
  114.3 27.7 %collective-permute-start.11 = (bf16[128,1024]{1,0:T(8,128)(2,1)S(1)}, bf16[128,1024]{1,0:T(8,128)(2,1)S(1)}, u32[]{:S(2)}, u32[]{:S(2)}) collective-permute-start(bf16[128,1024]{1,0:T(8,128)(2,1)S(1)} %select_add_fusion.25), channel_id=1, source_target_pairs={{0,64},{64,128},{128,192},{192,256},{961,897},{897,833},{833,769},... | collective-permute-start | bytes 786440 | tf_op jit(solution)/shard_map/ppermute | solution.py:116
  116.1 27.7 %collective-permute-start.14 = (bf16[128,1024]{1,0:T(8,128)(2,1)S(1)}, bf16[128,1024]{1,0:T(8,128)(2,1)}, u32[]{:S(2)}, u32[]{:S(2)}) collective-permute-start(bf16[128,1024]{1,0:T(8,128)(2,1)S(1)} %select_add_fusion.24), channel_id=1, source_target_pairs={{0,64},{64,128},{128,192},{192,256},{961,897},{897,833},{833,769},... | collective-permute-start | bytes 786440 | tf_op jit(solution)/shard_map/ppermute | solution.py:116
  119.3 45.4 %all-to-all-start.2 = ((bf16[8,4,2048]{2,1,0:T(4,128)(2,1)}), bf16[8,4,2048]{2,1,0:T(4,128)(2,1)S(1)}, u32[]{:S(2)}, u32[]{:S(2)}) async-start(bf16[8,4,2048]{2,1,0:T(4,128)(2,1)} %reshape.188), calls=%async_computation.2 | async-start | bytes 262144 | tf_op jit(solution)/shard_map/all_to_all | solution.py:162
  143.1 3.2 %collective-permute-start.13 = (bf16[128,1024]{1,0:T(8,128)(2,1)S(1)}, bf16[128,1024]{1,0:T(8,128)(2,1)S(1)}, u32[]{:S(2)}, u32[]{:S(2)}) collective-permute-start(bf16[128,1024]{1,0:T(8,128)(2,1)S(1)} %select_add_fusion.23), channel_id=1, source_target_pairs={{0,64},{64,128},{128,192},{192,256},{961,897},{897,833},{833,769},... | collective-permute-start | bytes 786440 | tf_op jit(solution)/shard_map/ppermute | solution.py:116
  147.4 17.4 %collective-permute-start.15 = (bf16[128,1024]{1,0:T(8,128)(2,1)S(1)}, bf16[128,1024]{1,0:T(8,128)(2,1)S(1)}, u32[]{:S(2)}, u32[]{:S(2)}) collective-permute-start(bf16[128,1024]{1,0:T(8,128)(2,1)S(1)} %select_add_fusion.21), channel_id=1, source_target_pairs={{0,64},{64,128},{128,192},{192,256},{256,320},{320,384},{961,897},... | collective-permute-start | bytes 786440 | tf_op jit(solution)/shard_map/ppermute | solution.py:116
  149.2 17.4 %collective-permute-start.17 = (bf16[128,1024]{1,0:T(8,128)(2,1)S(1)}, bf16[128,1024]{1,0:T(8,128)(2,1)S(1)}, u32[]{:S(2)}, u32[]{:S(2)}) collective-permute-start(bf16[128,1024]{1,0:T(8,128)(2,1)S(1)} %select_add_fusion.20), channel_id=1, source_target_pairs={{0,64},{64,128},{128,192},{192,256},{256,320},{320,384},{961,897},... | collective-permute-start | bytes 786440 | tf_op jit(solution)/shard_map/ppermute | solution.py:116
  183.9 12.3 %collective-permute-start.29 = (bf16[128,1024]{1,0:T(8,128)(2,1)S(1)}, bf16[128,1024]{1,0:T(8,128)(2,1)S(1)}, u32[]{:S(2)}, u32[]{:S(2)}) collective-permute-start(bf16[128,1024]{1,0:T(8,128)(2,1)S(1)} %select_add_fusion.9), channel_id=1, source_target_pairs={{0,64},{64,128},{128,192},{192,256},{256,320},{320,384},{384,448},... | collective-permute-start | bytes 786440 | tf_op jit(solution)/shard_map/ppermute | solution.py:116
  186.3 12.9 %collective-permute-start.28 = (bf16[128,1024]{1,0:T(8,128)(2,1)S(1)}, bf16[128,1024]{1,0:T(8,128)(2,1)S(1)}, u32[]{:S(2)}, u32[]{:S(2)}) collective-permute-start(bf16[128,1024]{1,0:T(8,128)(2,1)S(1)} %select_add_fusion.8), channel_id=1, source_target_pairs={{0,64},{64,128},{128,192},{192,256},{256,320},{320,384},{384,448},... | collective-permute-start | bytes 786440 | tf_op jit(solution)/shard_map/ppermute | solution.py:116
  197.3 25.6 %collective-permute-start.31 = (bf16[128,1024]{1,0:T(8,128)(2,1)S(1)}, bf16[128,1024]{1,0:T(8,128)(2,1)S(1)}, u32[]{:S(2)}, u32[]{:S(2)}) collective-permute-start(bf16[128,1024]{1,0:T(8,128)(2,1)S(1)} %select_add_fusion.7), channel_id=1, source_target_pairs={{0,64},{64,128},{128,192},{192,256},{256,320},{320,384},{384,448},... | collective-permute-start | bytes 786440 | tf_op jit(solution)/shard_map/ppermute | solution.py:116
  200.3 25.6 %collective-permute-start.30 = (bf16[128,1024]{1,0:T(8,128)(2,1)S(1)}, bf16[128,1024]{1,0:T(8,128)(2,1)S(1)}, u32[]{:S(2)}, u32[]{:S(2)}) collective-permute-start(bf16[128,1024]{1,0:T(8,128)(2,1)S(1)} %select_add_fusion.6), channel_id=1, source_target_pairs={{0,64},{64,128},{128,192},{192,256},{256,320},{320,384},{384,448},... | collective-permute-start | bytes 786440 | tf_op jit(solution)/shard_map/ppermute | solution.py:116
  223.9 8.3 %collective-permute-start.33 = (bf16[128,1024]{1,0:T(8,128)(2,1)S(1)}, bf16[128,1024]{1,0:T(8,128)(2,1)S(1)}, u32[]{:S(2)}, u32[]{:S(2)}) collective-permute-start(bf16[128,1024]{1,0:T(8,128)(2,1)S(1)} %select_add_fusion.5), channel_id=1, source_target_pairs={{0,64},{64,128},{128,192},{192,256},{256,320},{320,384},{384,448},... | collective-permute-start | bytes 786440 | tf_op jit(solution)/shard_map/ppermute | solution.py:116
  226.9 10.2 %collective-permute-start.32 = (bf16[128,1024]{1,0:T(8,128)(2,1)S(1)}, bf16[128,1024]{1,0:T(8,128)(2,1)S(1)}, u32[]{:S(2)}, u32[]{:S(2)}) collective-permute-start(bf16[128,1024]{1,0:T(8,128)(2,1)S(1)} %select_add_fusion.4), channel_id=1, source_target_pairs={{0,64},{64,128},{128,192},{192,256},{256,320},{320,384},{384,448},... | collective-permute-start | bytes 786440 | tf_op jit(solution)/shard_map/ppermute | solution.py:116
  233.3 8.3 %collective-permute-start.35 = (bf16[128,1024]{1,0:T(8,128)(2,1)S(1)}, bf16[128,1024]{1,0:T(8,128)(2,1)S(1)}, u32[]{:S(2)}, u32[]{:S(2)}) collective-permute-start(bf16[128,1024]{1,0:T(8,128)(2,1)S(1)} %select_add_fusion.3), channel_id=1, source_target_pairs={{0,64},{64,128},{128,192},{192,256},{256,320},{320,384},{384,448},... | collective-permute-start | bytes 786440 | tf_op jit(solution)/shard_map/ppermute | solution.py:116
  238.3 8.3 %collective-permute-start.34 = (bf16[128,1024]{1,0:T(8,128)(2,1)S(1)}, bf16[128,1024]{1,0:T(8,128)(2,1)S(1)}, u32[]{:S(2)}, u32[]{:S(2)}) collective-permute-start(bf16[128,1024]{1,0:T(8,128)(2,1)S(1)} %select_add_fusion.2), channel_id=1, source_target_pairs={{0,64},{64,128},{128,192},{192,256},{256,320},{320,384},{384,448},... | collective-permute-start | bytes 786440 | tf_op jit(solution)/shard_map/ppermute | solution.py:116
  242.7 9.2 %collective-permute-start.38 = (bf16[128,1024]{1,0:T(8,128)(2,1)S(1)}, bf16[128,1024]{1,0:T(8,128)(2,1)S(1)}, u32[]{:S(2)}, u32[]{:S(2)}) collective-permute-start(bf16[128,1024]{1,0:T(8,128)(2,1)S(1)} %select_add_fusion.1), channel_id=1, source_target_pairs={{0,64},{64,128},{128,192},{192,256},{256,320},{320,384},{384,448},... | collective-permute-start | bytes 786440 | tf_op jit(solution)/shard_map/ppermute | solution.py:116
  247.7 40.3 %collective-permute-start.36 = (bf16[128,1024]{1,0:T(8,128)(2,1)S(1)}, bf16[128,1024]{1,0:T(8,128)(2,1)S(1)}, u32[]{:S(2)}, u32[]{:S(2)}) collective-permute-start(bf16[128,1024]{1,0:T(8,128)(2,1)S(1)} %select_add_fusion), channel_id=1, source_target_pairs={{0,64},{64,128},{128,192},{192,256},{256,320},{320,384},{384,448},... | collective-permute-start | bytes 786440 | tf_op jit(solution)/shard_map/ppermute | solution.py:116
  252.0 40.3 %collective-permute-start.39 = (bf16[128,512]{1,0:T(8,128)(2,1)S(1)}, bf16[128,512]{1,0:T(8,128)(2,1)S(1)}, u32[]{:S(2)}, u32[]{:S(2)}) collective-permute-start(bf16[128,512]{1,0:T(8,128)(2,1)S(1)} %slice.35), channel_id=1, source_target_pairs={{0,1},{1,0},{2,3},{3,2},{4,5},{5,4},{6,7},{7,6},{8,9},{9,8},{10,11... | collective-permute-start | bytes 393224 | tf_op jit(solution)/shard_map/ppermute | solution.py:30
  288.0 6.0 %collective-permute-start.37 = (bf16[128,512]{1,0:T(8,128)(2,1)S(1)}, bf16[128,512]{1,0:T(8,128)(2,1)S(1)}, u32[]{:S(2)}, u32[]{:S(2)}) collective-permute-start(bf16[128,512]{1,0:T(8,128)(2,1)S(1)} %slice.33), channel_id=1, source_target_pairs={{0,1},{1,0},{2,3},{3,2},{4,5},{5,4},{6,7},{7,6},{8,9},{9,8},{10,11... | collective-permute-start | bytes 393224 | tf_op jit(solution)/shard_map/ppermute | solution.py:30
  (21 other events, 306.0 us)
